TPU v7x, 32 devices: a whole 2x2x4 slice. The times are simulated.
32 devices in a mesh: wave: 8 (over z, y), lev: 4 (over x, core).
Axes of the slice: x: 2, y: 2, z: 4, core: 2. Of those that a mesh axis runs over, the one named last changes fastest.
Arguments:
- spectral: bfloat16 [2, 16, 640, 1281], P(None, 'lev', 'wave'), may hold values from -6 to 6
- legendre: bfloat16 [640, 1281, 64], P(('wave', 'lev')), may hold values from -0.0048828125 to 0.0048828125
- wave_table: int32 [640], replicated, may hold values from 0 to 639, each once
- courant_lon: float32 [16, 64, 5120], P('lev', 'wave'), may hold values from -0.35 to 0.35
- courant_lat: float32 [16, 64, 5120], P('lev', 'wave'), may hold values from -0.35 to 0.35
Outputs:
- tracer: float32 [16, 64, 5120], P('lev', 'wave')
Inputs may be any that keep to these rules, and one draw needn't show every extreme that they name: A permutation of the pairs: slot s carries wavenumbers wave_table[s] and 1279 - wave_table[s].
All inputs are finite; a program needn't handle non-finite values.
Results may differ from a plain program's by a relative error of at most 0.003.
Values may be sent and summed in bfloat16 or wider, within the bound.
No kernel may reach another device: no remote copies, remote signals or barrier semaphores. Data moves between devices by JAX's collectives and lax.ppermute only.
A program may use at most 64 MiB of HBM per device.

v0:
```python
import functools
import math

import jax
import jax.numpy as jnp
import ml_dtypes
import numpy as np
from jax import lax
from jax.experimental import pallas as pl
from jax.experimental.pallas import tpu as pltpu
from jax.sharding import PartitionSpec as P

PASSES = 4
HALO = 2 * PASSES
SUB = 8
LANES = 128
NEAR = 2 * LANES
F32 = jnp.float32
BF16 = jnp.bfloat16


def params(mib):
    return pltpu.CompilerParams(vmem_limit_bytes=mib << 20)


def lane_index():
    return lax.broadcasted_iota(jnp.int32, (SUB, LANES), 1)


def pack_kernel(count, x_ref, *refs):
    outs, turned = refs[:count], refs[count]
    slots, degrees = x_ref.shape[1:]
    own = slots // count
    me = lax.axis_index("lev")

    def gather(first, rows):
        for lo in range(0, degrees, LANES):
            hi = min(lo + LANES, degrees)
            tile = jnp.stack(
                [x_ref[i, first : first + rows, lo:hi].astype(F32) for i in range(SUB)], 0
            )
            turned[first : first + rows, :, lo:hi] = jnp.swapaxes(tile, 0, 1)

    for first in range(0, slots, SUB):
        gather(first, SUB)
    for step, out in enumerate(outs):
        start = (me ^ step) * own

        def pair(i, carry, out=out, start=start):
            second = jnp.minimum(start + 2 * i + 1, slots - 1)
            both = [turned[start + 2 * i], turned[second]]
            out[i] = jnp.concatenate(both, 0).astype(BF16)
            return carry

        lax.fori_loop(0, out.shape[0], pair, 0)


def pack(spectral, count):
    parts, levels, slots, degrees = spectral.shape
    out = jax.ShapeDtypeStruct((-(-slots // count // 2), 2 * SUB, degrees), BF16)
    return pl.pallas_call(
        functools.partial(pack_kernel, count),
        out_shape=[out] * count,
        scratch_shapes=[pltpu.VMEM((slots, SUB, degrees), F32)],
        compiler_params=params(40),
        name="pack",
    )(spectral.reshape(parts * levels, slots, degrees))


def legendre_kernel(steps, bands, waves, pad, pairs_ref, *refs):
    count = len(steps)
    blocks, table = refs[:count], refs[count]
    outs = refs[count + 1 : 2 * count + 1]
    sums = refs[2 * count + 1]
    own, degrees, lats = table.shape
    wide = sums.shape[-1]
    band = lats // bands
    pieces = band // SUB + 2
    if wide > lats:
        sums[...] = jnp.zeros_like(sums)
    elif 2 * own < pad:
        sums[:, 2 * own :] = jnp.zeros((count, pad - 2 * own, SUB, wide), F32)

    def pair(i, carry):
        rows = jnp.concatenate([block[i] for block in blocks], 0).astype(F32)
        row = lax.broadcasted_iota(jnp.int32, rows.shape, 0) % (2 * SUB)
        degree = lax.broadcasted_iota(jnp.int32, rows.shape, 1)
        second = jnp.minimum(2 * i + 1, own - 1)
        bound = waves - jnp.where(row < SUB, pairs_ref[2 * i], pairs_ref[second])
        low = jnp.where(degree < bound, rows, 0.0)
        both = jnp.concatenate([low, rows - low], 0).astype(BF16)
        for j in range(2):
            got = jnp.dot(both, table[second if j else 2 * i], preferred_element_type=F32)
            for half in range(2):
                for d in range(count):
                    first = (half * count + d) * 2 * SUB + j * SUB
                    sums[d, 4 * i + 2 * j + half, :, :lats] = got[first : first + SUB]
        return carry

    lax.fori_loop(0, blocks[0].shape[0], pair, 0)
    lane = lax.broadcasted_iota(jnp.int32, (SUB, wide), 1)
    for d in range(count):
        tiles = [
            [jnp.swapaxes(sums[d, 8 * g : 8 * g + 8, :, k : k + LANES], 0, 1) for k in range(0, wide, LANES)]
            for g in range(pad // SUB)
        ]
        wides = []
        for i in range(SUB):
            tall = []
            for piece in range(pieces):
                shift = SUB - SUB * piece
                for g in range(pad // SUB):
                    value = jnp.concatenate([tile[i] for tile in tiles[g]], 1)
                    if shift:
                        value = pltpu.roll(value, shift % wide, 1)
                        value = jnp.where((lane >= shift) & (lane < lats + shift), value, 0.0)
                    tall.append(value)
            spare = LANES - pieces * pad
            if spare:
                tall.append(jnp.zeros((spare, wide), F32))
            wides.append(jnp.transpose(jnp.concatenate(tall, 0)))
        for w in range(bands):
            for i in range(0, SUB, 2):
                two = [wides[i + k][w * band : w * band + SUB] for k in range(2)]
                outs[d][w, i * SUB : (i + 2) * SUB, :] = jnp.concatenate(two, 0).astype(BF16)


def legendre_sums(steps, blocks, table, own_pairs, bands, waves, pad):
    own, degrees, lats = table.shape
    wide = -(-lats // LANES) * LANES
    out = jax.ShapeDtypeStruct((bands, SUB * SUB, LANES), BF16)
    vmem = pl.BlockSpec(memory_space=pltpu.VMEM)
    return pl.pallas_call(
        functools.partial(legendre_kernel, steps, bands, waves, pad),
        out_shape=[out] * len(steps),
        in_specs=[pl.BlockSpec(memory_space=pltpu.SMEM)] + [vmem] * (len(steps) + 1),
        scratch_shapes=[pltpu.VMEM((len(steps), pad, SUB, wide), F32)],
        compiler_params=params(40),
        name="legendre",
    )(own_pairs, *blocks, table)


def wraps(levels):
    def to_east(x):
        return pltpu.roll(x, levels, 0)

    def to_west(x):
        return pltpu.roll(x, SUB - levels, 0)

    return to_east, to_west


def from_west(values, levels):
    to_east, _ = wraps(levels)
    first = lane_index() == 0
    rolled = [pltpu.roll(x, 1, 1) for x in values]
    before = [to_east(rolled[-1])] + rolled[:-1]
    return [jnp.where(first, b, r) for b, r in zip(before, rolled)]


def from_east(values, levels):
    _, to_west = wraps(levels)
    last = lane_index() == LANES - 1
    rolled = [pltpu.roll(x, LANES - 1, 1) for x in values]
    after = rolled[1:] + [to_west(rolled[0])]
    return [jnp.where(last, a, r) for a, r in zip(after, rolled)]


def courant_kernel(lon, lat, below, above, cx, cy, ax, bx, ay, by):
    levels, band, nlon = lon.shape
    parts = SUB // levels
    rows, chunks = cx.shape[:2]
    for field, (own, out) in enumerate(((lon, cx), (lat, cy))):
        for block in range(rows // SUB):

            def chunk(v, carry, field=field, own=own, out=out, block=block):
                tiles = []
                for part in range(parts):
                    lanes = pl.ds(pl.multiple_of(part * (nlon // parts) + v * LANES, LANES), LANES)
                    if 0 < block < rows // SUB - 1:
                        for level in range(levels):
                            tiles.append(own[level, (block - 1) * SUB : block * SUB, lanes])
                    else:
                        far = below if block == 0 else above
                        for level in range(0, levels, 2):
                            first = (field * levels + level) * SUB
                            both = far[first : first + 2 * SUB, lanes].astype(F32)
                            tiles += [both[:SUB], both[SUB:]]
                turned = jnp.swapaxes(jnp.stack(tiles, 0), 0, 1)
                for t in range(SUB):
                    out[block * SUB + t, v] = turned[t]
                return carry

            lax.fori_loop(0, chunks, chunk, 0)

    def factors(t, carry):
        u = [cx[t, v] for v in range(chunks)]
        w = [cy[t, v] for v in range(chunks)]
        near = [w[v] + cy[t + 1, v] for v in range(chunks)]
        mean = [a + b for a, b in zip(near, from_west(near, levels))]
        for v in range(chunks):
            ax[t, v] = 0.5 * (jnp.abs(u[v]) - u[v] * u[v])
            bx[t, v] = 0.0625 * u[v] * mean[v]
        near = [u[v] + cx[t - 1, v] for v in range(chunks)]
        mean = [a + b for a, b in zip(near, from_east(near, levels))]
        for v in range(chunks):
            ay[t, v] = 0.5 * (jnp.abs(w[v]) - w[v] * w[v])
            by[t, v] = 0.0625 * w[v] * mean[v]
        return carry

    lax.fori_loop(1, rows - 1, factors, 0)


def courant_fields(lon, lat, below, above):
    levels, band, nlon = lon.shape
    chunks = nlon * levels // (SUB * LANES)
    out = jax.ShapeDtypeStruct((band + 2 * HALO, chunks, SUB, LANES), F32)
    return pl.pallas_call(
        courant_kernel, out_shape=[out] * 6, compiler_params=params(40), name="courant"
    )(lon, lat, below, above)


def real_transform(real, imag):
    n = len(real)
    half, quarter = n // 2, n // 4

    def weighted(terms):
        total = None
        for factor, value in terms:
            if abs(factor) < 1e-9:
                continue
            if abs(abs(factor) - 1.0) < 1e-9:
                total = (value if factor > 0 else -value) if total is None else (
                    total + value if factor > 0 else total - value
                )
            else:
                total = factor * value if total is None else total + factor * value
        return total

    def sums(odd):
        cosines, sines = [], []
        numbers = range(odd, half, 2)
        for a in range(quarter + 1):
            sign = -1.0 if a % 2 else 1.0
            angle = [2.0 * math.pi * m * a / n for m in numbers]
            cosines.append(
                weighted([(math.cos(x), combined[sign][0][m]) for x, m in zip(angle, numbers)])
            )
            sines.append(
                weighted([(math.sin(x), combined[sign][1][m]) for x, m in zip(angle, numbers)])
            )
        return cosines, sines

    def add(x, y):
        return y if x is None else x if y is None else x + y

    def negative(x):
        return None if x is None else -x

    def subtract(x, y):
        return negative(y) if x is None else x if y is None else x - y

    combined = {
        sign: [
            [part[m] + part[m + half] if sign > 0 else part[m] - part[m + half] for m in range(half)]
            for part in (real, imag)
        ]
        for sign in (1.0, -1.0)
    }
    even_cos, even_sin = sums(0)
    odd_cos, odd_sin = sums(1)
    even, odd = [None] * half, [None] * half
    for a in range(quarter + 1):
        even[a] = subtract(even_cos[a], even_sin[a])
        odd[a] = subtract(odd_cos[a], odd_sin[a])
        if 0 < a < half - a:
            even[half - a] = add(even_cos[a], even_sin[a])
            odd[half - a] = negative(add(odd_cos[a], odd_sin[a]))
    return [add(e, o) for e, o in zip(even, odd)] + [subtract(e, o) for e, o in zip(even, odd)]


def transform(arrived, order, table, lhs, mixed, inner, tiles, field, pad, levels):
    sources = arrived.shape[0]
    rows, chunks = field.shape[:2]
    pieces = rows // SUB
    group = LANES // pad
    lane = lax.broadcasted_iota(jnp.int32, (SUB * SUB, LANES), 1)
    height = levels * SUB
    for g in range(-(-sources // group)):
        members = [arrived[q].astype(F32) for q in range(g * group, min(sources, (g + 1) * group))]
        for piece in range(pieces):
            value = None
            for i, member in enumerate(members):
                shift = pad * (i - piece) % LANES
                turned = pltpu.roll(member, shift, 1) if shift else member
                value = turned if value is None else jnp.where(lane >= i * pad, turned, value)
            value = value.astype(BF16)
            for c in range(2):
                first = (c * pieces + piece) * height
                lhs[first : first + height, g * LANES : (g + 1) * LANES] = value[
                    c * height : (c + 1) * height
                ]
    half = pieces * height
    waves = order.shape[1]
    far, depth = table.shape[0], waves // table.shape[0]
    left = lax.broadcasted_iota(jnp.int32, (half, LANES), 1) < depth
    for lo in range(0, waves, NEAR):
        width = min(NEAR, waves - lo)
        got = jnp.dot(lhs[...], order[:, lo : lo + width], preferred_element_type=F32)
        for k in range(0, width, LANES):
            real, imag = got[:half, k : k + LANES], got[half:, k : k + LANES]
            m = (lo + k) // depth
            mixed[m] = jnp.where(left, real, pltpu.roll(imag, depth, 1)).astype(BF16)
            mixed[m + 1] = jnp.where(left, pltpu.roll(real, depth, 1), imag).astype(BF16)

    def mix(m, carry):
        value = mixed[m]
        inner[m] = jnp.dot(
            jnp.concatenate([value, value], 1), table[m], preferred_element_type=F32
        )
        return carry

    lax.fori_loop(0, far, mix, 0)
    parts = SUB // levels
    per_part = far // parts

    def finish(piece, carry):
        for near in range(0, NEAR, LANES):
            for level in range(levels):
                span = pl.ds(pl.multiple_of((piece * levels + level) * SUB, SUB), SUB)
                real = [inner[m, span, near : near + LANES] for m in range(far)]
                imag = [inner[m, span, NEAR + near : NEAR + near + LANES] for m in range(far)]
                for a, value in enumerate(real_transform(real, imag)):
                    tiles[a % per_part, a // per_part * levels + level] = value
            for a in range(per_part):
                turned = jnp.swapaxes(tiles[a], 0, 1)
                for t in range(SUB):
                    field[piece * SUB + t, a * (NEAR // LANES) + near // LANES] = turned[t]
        return carry

    lax.fori_loop(0, pieces, finish, 0)


def upwind_rows(t, count, old, new, cx, cy, levels):
    chunks = old.shape[1]
    to_east, to_west = wraps(levels)
    lane = lane_index()
    first, last = lane == 0, lane == LANES - 1
    rolled = [to_east(pltpu.roll(old[t + r, chunks - 1], 1, 1)) for r in range(count)]
    flux_first, flux_left, base_left = None, None, None
    for v in range(chunks + 1):
        if v < chunks:
            q = [old[t - 1 + r, v] for r in range(count + 2)]
            flux_lat = []
            for r in range(count + 1):
                speed = cy[t + r, v]
                flux_lat.append(jnp.maximum(speed, 0.0) * q[r] + jnp.minimum(speed, 0.0) * q[r + 1])
            fluxes, base = [], []
            for r in range(count):
                turned = pltpu.roll(q[r + 1], 1, 1)
                west = jnp.where(first, rolled[r], turned)
                rolled[r] = turned
                speed = cx[t + r, v]
                flux = jnp.maximum(speed, 0.0) * west + jnp.minimum(speed, 0.0) * q[r + 1]
                base.append((q[r + 1] + flux) - (flux_lat[r + 1] - flux_lat[r]))
                fluxes.append(pltpu.roll(flux, LANES - 1, 1))
            if v == 0:
                flux_first = fluxes
        else:
            fluxes = [to_west(x) for x in flux_first]
        if v > 0:
            for r in range(count):
                new[t + r, v - 1] = base_left[r] - jnp.where(last, fluxes[r], flux_left[r])
        flux_left, base_left = fluxes, base


def corrective_rows(t, count, old, new, ax, bx, ay, by, levels):
    chunks = old.shape[1]
    to_east, to_west = wraps(levels)
    lane = lane_index()
    first, last = lane == 0, lane == LANES - 1
    span = range(count + 2)

    def inverse(x):
        return pl.reciprocal(jnp.maximum(x, 1.0), approx=True)

    def flux(a, b, gradient, cross, total, step):
        speed = a * gradient - b * cross
        return speed * total - jnp.abs(speed) * step

    right = [to_east(pltpu.roll(old[t - 1 + r, chunks - 1], 1, 1)) for r in span]
    here = [old[t - 1 + r, 0] for r in span]
    left = [pltpu.roll(x, LANES - 1, 1) for x in here]
    left_first = left
    flux_first, flux_left, base_left = None, None, None
    for v in range(chunks + 1):
        if v < chunks:
            if v + 1 < chunks:
                following = [old[t - 1 + r, v + 1] for r in span]
                left_next = [pltpu.roll(x, LANES - 1, 1) for x in following]
            else:
                following, left_next = None, [to_west(x) for x in left_first]
            right_here = [pltpu.roll(x, 1, 1) for x in here]
            west = [jnp.where(first, right[r], right_here[r]) for r in span]
            east = [jnp.where(last, left_next[r], left[r]) for r in span]
            size = [jnp.abs(x) for x in here]
            size_west = [jnp.abs(x) for x in west]
            size_east = [jnp.abs(x) for x in east]
            total = [here[r] + west[r] for r in span]
            sizes = [size[r] + size_west[r] for r in span]
            apart = [east[r] - west[r] for r in span]
            sizes_apart = [size_east[r] + size_west[r] for r in span]
            flux_lat = []
            for r in range(count + 1):
                step = here[r + 1] - here[r]
                gradient = step * inverse(size[r + 1] + size[r])
                cross = (apart[r + 1] + apart[r]) * inverse(sizes_apart[r + 1] + sizes_apart[r])
                flux_lat.append(
                    flux(ay[t + r, v], by[t + r, v], gradient, cross, here[r + 1] + here[r], step)
                )
            fluxes, base = [], []
            for r in range(1, count + 1):
                step = here[r] - west[r]
                gradient = step * inverse(sizes[r])
                cross = (total[r + 1] - total[r - 1]) * inverse(sizes[r + 1] + sizes[r - 1])
                value = flux(ax[t + r - 1, v], bx[t + r - 1, v], gradient, cross, total[r], step)
                base.append((here[r] + value) - (flux_lat[r] - flux_lat[r - 1]))
                fluxes.append(pltpu.roll(value, LANES - 1, 1))
            if v == 0:
                flux_first = fluxes
            right, here, left = right_here, following, left_next
        else:
            fluxes = [to_west(x) for x in flux_first]
        if v > 0:
            for r in range(count):
                new[t + r, v - 1] = base_left[r] - jnp.where(last, fluxes[r], flux_left[r])
        flux_left, base_left = fluxes, base


def advect_kernel(
    pad, arrived, order, table, cx, cy, ax, bx, ay, by, out, lhs, mixed, inner, tiles, field, upwind
):
    levels, band, nlon = out.shape
    rows, chunks = field.shape[:2]
    transform(arrived, order, table, lhs, mixed, inner, tiles, field, pad, levels)
    outermost = lax.axis_index("wave") == 0

    def clear(where):
        @pl.when(outermost)
        def _():
            where[HALO - 1] = jnp.zeros((chunks, SUB, LANES), F32)

    def one_pass(number, carry):
        start = 2 * number + 1

        def first(i, carry):
            upwind_rows(start + 2 * i, 2, field, upwind, cx, cy, levels)
            return carry

        lax.fori_loop(0, rows // 2 - 1 - 2 * number, first, 0)
        clear(upwind)

        def second(i, carry):
            corrective_rows(start + 1 + 4 * i, 4, upwind, field, ax, bx, ay, by, levels)
            return carry

        lax.fori_loop(0, rows // 4 - 1 - number, second, 0)
        clear(field)
        return carry

    lax.fori_loop(0, PASSES, one_pass, 0)
    parts = SUB // levels
    for block in range(band // SUB):
        first = HALO + block * SUB
        for v in range(chunks):
            turned = jnp.swapaxes(field[first : first + SUB, v], 0, 1)
            for part in range(parts):
                lanes = part * (nlon // parts) + v * LANES
                for level in range(levels):
                    out[level, block * SUB : (block + 1) * SUB, lanes : lanes + LANES] = turned[
                        part * levels + level
                    ]


def advect(arrived, order, table, fields, shape, pad):
    levels, band, nlon = shape
    rows, chunks = fields[0].shape[:2]
    half = rows * levels
    far = table.shape[0]
    return pl.pallas_call(
        functools.partial(advect_kernel, pad),
        out_shape=jax.ShapeDtypeStruct(shape, F32),
        scratch_shapes=[
            pltpu.VMEM((2 * half, order.shape[0]), BF16),
            pltpu.VMEM((far, half, LANES), BF16),
            pltpu.VMEM((far, half, 2 * NEAR), F32),
            pltpu.VMEM((far * levels // SUB, SUB, SUB, LANES), F32),
            pltpu.VMEM((rows, chunks, SUB, LANES), F32),
            pltpu.VMEM((rows, chunks, SUB, LANES), F32),
        ],
        compiler_params=params(56),
        name="advect",
    )(arrived, order, table, *fields)


def mixing_table(waves, nlon):
    far = nlon // NEAR
    depth = waves // far
    number = far * np.arange(depth)[None, :, None] + np.arange(far)[:, None, None]
    angle = 2.0 * np.pi / nlon * (number * np.arange(NEAR)[None, None, :] % nlon)
    cos, sin = np.cos(angle), np.sin(angle)
    whole = np.concatenate(
        [np.concatenate([cos, sin], 2), np.concatenate([-sin, cos], 2)], 1
    ).astype(np.float32)
    high = whole.astype(ml_dtypes.bfloat16)
    low = (whole - high.astype(np.float32)).astype(ml_dtypes.bfloat16)
    return np.concatenate([high, low], 1)


def order_matrix(wave_table, sources, pad, far):
    waves = 2 * wave_table.shape[0]
    group = LANES // pad
    numbers = jnp.stack([wave_table, waves - 1 - wave_table], 1).reshape(sources, -1)
    column = numbers % far * (waves // far) + numbers // far
    extra = -sources % group
    column = jnp.pad(column, ((0, extra), (0, pad - column.shape[1])), constant_values=-1)
    column = column.reshape(-1, group * pad)
    column = jnp.pad(column, ((0, 0), (0, LANES - group * pad)), constant_values=-1).reshape(-1, 1)
    weight = jnp.where(column == 0, 1.0, 2.0).astype(BF16)
    return jnp.where(jnp.arange(waves)[None, :] == column, weight, jnp.zeros((), BF16))


def body(spectral, legendre, wave_table, courant_lon, courant_lat):
    wave_count, level_count = lax.axis_size("wave"), lax.axis_size("lev")
    wave_rank, level_rank = lax.axis_index("wave"), lax.axis_index("lev")
    levels, band, nlon = courant_lon.shape
    own = legendre.shape[0]
    waves = 2 * wave_table.shape[0]
    pad = -(-2 * own // SUB) * SUB

    up = [(i, i + 1) for i in range(wave_count - 1)]
    down = [(i + 1, i) for i in range(wave_count - 1)]
    winds = jnp.stack([courant_lon, courant_lat], 0).astype(BF16)
    upper = winds[:, :, band - HALO :].reshape(-1, nlon)
    lower = winds[:, :, :HALO].reshape(-1, nlon)

    blocks = list(pack(spectral, level_count))
    for step in range(1, level_count):
        pairs = [(i, i ^ step) for i in range(level_count)]
        blocks[step] = lax.ppermute(blocks[step], "lev", pairs)
    below = lax.ppermute(upper, "wave", up)
    above = lax.ppermute(lower, "wave", down)

    own_pairs = lax.dynamic_slice_in_dim(
        wave_table, (wave_rank * level_count + level_rank) * own, own
    )
    half = level_count // 2
    sums = []
    for steps in (tuple(range(half)), tuple(range(half, level_count))):
        sums += legendre_sums(
            steps, [blocks[s] for s in steps], legendre, own_pairs, wave_count, waves, pad
        )
    stacked = jnp.stack(sums, 1)
    stacked = jnp.take(stacked, level_rank ^ jnp.arange(level_count), axis=1)
    arrived = lax.all_to_all(
        stacked.reshape(-1, SUB * SUB, LANES), ("wave", "lev"), 0, 0, tiled=True
    )

    fields = courant_fields(courant_lon, courant_lat, below, above)
    table = jnp.asarray(mixing_table(waves, nlon))
    order = order_matrix(wave_table, wave_count * level_count, pad, nlon // NEAR)
    return advect(arrived, order, table, fields, courant_lon.shape, pad)


def solution(mesh):
    placed = (
        P(None, "lev", "wave", None),
        P(("wave", "lev"), None, None),
        P(),
        P("lev", "wave", None),
        P("lev", "wave", None),
    )
    return jax.shard_map(
        body, mesh=mesh, in_specs=placed, out_specs=P("lev", "wave", None), check_vma=False
    )
```

profile of v0, /device:TPU:0, one launch (start us, length us, event | category | flops | bytes accessed | tf_op | source)
XLA Modules:
  0.0 110.6 jit_solution(6687806843422873035)
XLA Ops:
  0.0 1.5 %convert_bitcast_fusion = (bf16[1,4,8,5120]{3,2,1,0:T(8,128)(2,1)S(1)}, bf16[1,4,8,5120]{3,2,1,0:T(8,128)(2,1)S(1)}) fusion(f32[4,8,5120]{2,1,0:T(8,128)} %lat.1, f32[4,8,5120]{2,1,0:T(8,128)} %lon.1), kind=kLoop, calls=%fused_computation.6 | loop fusion | flops 327680 | bytes 1966080 | tf_op jit(solution)/shard_map/stack | solution.py:543
  1.5 0.9 pad_maximum_fusion
  2.4 1.3 %collective-permute-start.4 = (bf16[64,5120]{1,0:T(8,128)(2,1)}, bf16[64,5120]{1,0:T(8,128)(2,1)S(1)}, u32[]{:S(2)}, u32[]{:S(2)}) collective-permute-start(bf16[64,5120]{1,0:T(8,128)(2,1)} %bitcast.11), channel_id=1, source_target_pairs={{4,0},{8,4},{12,8},{16,12},{20,16},{24,20},{28,24},{5,1},{9,5},{13... | collective-permute-start | bytes 1966088 | tf_op jit(solution)/shard_map/ppermute | solution.py:552
  3.7 5.5 %collective-permute-start.3 = (bf16[64,5120]{1,0:T(8,128)(2,1)}, bf16[64,5120]{1,0:T(8,128)(2,1)S(1)}, u32[]{:S(2)}, u32[]{:S(2)}) collective-permute-start(bf16[64,5120]{1,0:T(8,128)(2,1)} %bitcast.11), channel_id=1, source_target_pairs={{0,4},{4,8},{8,12},{12,16},{16,20},{20,24},{24,28},{1,5},{5,9},{9,... | collective-permute-start | bytes 1966088 | tf_op jit(solution)/shard_map/ppermute | solution.py:551
  9.2 0.0 copy-done.10
  9.2 2.2 %pack.1 = (bf16[10,16,1281]{2,1,0:T(8,128)(2,1)S(1)}, bf16[10,16,1281]{2,1,0:T(8,128)(2,1)}, bf16[10,16,1281]{2,1,0:T(8,128)(2,1)}, bf16[10,16,1281]{2,1,0:T(8,128)(2,1)}) custom-call(bf16[8,80,1281]{2,1,0:T(8,128)(2,1)S(1)} %bitcast.19), custom_call_target="tpu_custom_call" | custom-call | tf_op jit(solution)/shard_map/pack/pallas_call | solution.py:61
  11.4 0.0 collective-permute-start
  11.4 2.0 %collective-permute-start.1 = (bf16[10,16,1281]{2,1,0:T(8,128)(2,1)}, bf16[10,16,1281]{2,1,0:T(8,128)(2,1)S(1)}, u32[]{:S(2)}, u32[]{:S(2)}) collective-permute-start(bf16[10,16,1281]{2,1,0:T(8,128)(2,1)} %get-tuple-element.23), channel_id=1, source_target_pairs={{0,2},{1,3},{2,0},{3,1},{4,6},{5,7},{6,4},{7,5},{8,10},{9,11},{10,... | collective-permute-start | bytes 1229768 | tf_op jit(solution)/shard_map/ppermute | solution.py:550
  13.4 0.1 collective-permute-start.2
  13.5 0.0 copy-done.12
  13.6 0.1 dynamic_slice.3.pairs_ref
  13.7 0.1 broadcast_in_dim.36
  13.8 0.2 copy.14
  14.0 0.2 ne.26
  14.2 0.2 copy.15
  14.4 0.1 div.10
  14.6 0.2 copy.13
  14.7 0.1 rem.19
  14.9 0.1 reshape.56
  15.0 7.5 %copy.10.refs_2_ = bf16[20,1281,64]{2,1,0:T(8,128)(2,1)} copy(bf16[20,1281,64]{1,2,0:T(8,128)(2,1)} %param.7) | data formatting | bytes 6558720 | tf_op args[1]
  22.5 2.3 %collective-permute-done.1.refs_0_ = bf16[10,16,1281]{2,1,0:T(8,128)(2,1)S(1)} collective-permute-done((bf16[10,16,1281]{2,1,0:T(8,128)(2,1)}, bf16[10,16,1281]{2,1,0:T(8,128)(2,1)S(1)}, u32[]{:S(2)}, u32[]{:S(2)}) %collective-permute-start.1) | collective-permute-done | bytes 409952 | tf_op jit(solution)/shard_map/ppermute | solution.py:550
  24.8 9.2 %collective-permute-done.2.refs_1_ = bf16[10,16,1281]{2,1,0:T(8,128)(2,1)S(1)} collective-permute-done((bf16[10,16,1281]{2,1,0:T(8,128)(2,1)}, bf16[10,16,1281]{2,1,0:T(8,128)(2,1)S(1)}, u32[]{:S(2)}, u32[]{:S(2)}) %collective-permute-start.2) | collective-permute-done | bytes 409952 | tf_op jit(solution)/shard_map/ppermute | solution.py:550
  34.0 2.9 %copy-done = bf16[20,1281,64]{2,1,0:T(8,128)(2,1)S(1)} copy-done((bf16[20,1281,64]{2,1,0:T(8,128)(2,1)S(1)}, bf16[20,1281,64]{2,1,0:T(8,128)(2,1)}, u32[]{:S(2)}) %copy-start) | copy-done | bytes 3279384
  36.9 3.6 %legendre.3 = (bf16[8,64,128]{2,1,0:T(8,128)(2,1)S(1)}, bf16[8,64,128]{2,1,0:T(8,128)(2,1)S(1)}) custom-call(s32[20]{0:T(128)S(1)} %dynamic_slice.3.pairs_ref, bf16[10,16,1281]{2,1,0:T(8,128)(2,1)S(1)} %collective-permute-done.1.refs_0_, bf16[10,16,1281]{2,1,0:T(8,128)(2,1)S(1)} %collective-permute-done.2.refs_1_, bf16[20,1281,64]{2,1,0:T(8,128)(2,1)S(1)} %copy-done), custom_call_target="tpu_custom_call" | custom-call | tf_op jit(solution)/shard_map/legendre/pallas_call | solution.py:133
  40.5 0.0 collective-permute-done.refs_1_
  40.5 0.0 copy-done.1
  40.5 3.6 %legendre.2 = (bf16[8,64,128]{2,1,0:T(8,128)(2,1)S(1)}, bf16[8,64,128]{2,1,0:T(8,128)(2,1)S(1)}) custom-call(s32[20]{0:T(128)S(1)} %dynamic_slice.3.pairs_ref, bf16[10,16,1281]{2,1,0:T(8,128)(2,1)S(1)} %get-tuple-element.19.refs_0_, bf16[10,16,1281]{2,1,0:T(8,128)(2,1)S(1)} %collective-permute-done.refs_1_, bf16[20,1281,64]{2,1,0:T(8,128)(2,1)S(1)} %copy-done.1), custom_call_target="tpu_custom_call" | custom-call | tf_op jit(solution)/shard_map/legendre/pallas_call | solution.py:133
  44.1 0.1 pad_maximum_fusion.1
  44.2 1.4 %gather_fusion = bf16[4,8,64,128]{3,2,1,0:T(8,128)(2,1)} fusion(bf16[8,4,64,128]{3,2,0,1:T(8,128)(2,1)S(1)} %pad_maximum_fusion.1, s32[1024]{0:T(1024)S(1)} %pad_clamp_fusion), kind=kCustom, calls=%fused_computation | custom fusion | bytes 1048592 | tf_op jit(solution)/shard_map/jit(_take)/gather | solution.py:564
  45.6 1.2 %copy.12 = bf16[8,4,64,128]{3,2,1,0:T(8,128)(2,1)S(1)} copy(bf16[8,4,64,128]{3,2,0,1:T(8,128)(2,1)} %bitcast.24) | data formatting | bytes 1048576 | tf_op jit(solution)/shard_map/jit(_take)/gather | solution.py:564
  46.8 0.9 bitcast_select_fusion
  47.7 5.9 %all-to-all-start = ((bf16[32,64,128]{2,1,0:T(8,128)(2,1)}), bf16[32,64,128]{2,1,0:T(8,128)(2,1)S(1)}, u32[]{:S(2)}, u32[]{:S(2)}) async-start(bf16[32,64,128]{2,1,0:T(8,128)(2,1)} %bitcast_select_fusion), calls=%async_computation | async-start | bytes 1048576 | tf_op jit(solution)/shard_map/all_to_all | solution.py:565
  53.6 2.4 %fusion.order = bf16[1408,1280]{1,0:T(8,128)(2,1)} fusion(s32[1408]{0:T(1024)S(1)} %pad_bitcast_fusion, bf16[1408]{0:T(1024)(128)(2,1)S(1)} %select_convert_fusion), kind=kLoop, calls=%fused_computation.2 | loop fusion | flops 3604480 | bytes 3612928 | tf_op jit(solution)/shard_map/jit(_where)/select_n | solution.py:530
  56.0 0.0 collective-permute-done.4.above
  56.0 0.0 collective-permute-done.3.below
  56.0 0.0 copy-done.2
  56.0 0.0 copy-done.3
  56.0 4.3 %courant.1 = (f32[24,20,8,128]{3,2,1,0:T(8,128)S(1)}, f32[24,20,8,128]{3,2,1,0:T(8,128)S(1)}, f32[24,20,8,128]{3,2,1,0:T(8,128)S(1)}, f32[24,20,8,128]{3,2,1,0:T...) custom-call(f32[4,8,5120]{2,1,0:T(8,128)S(1)} %copy-done.2, f32[4,8,5120]{2,1,0:T(8,128)S(1)} %copy-done.3, ...), custom_call_target="tpu_custom_call" | custom-call | tf_op jit(solution)/shard_map/courant/pallas_call | solution.py:218
  60.3 0.0 copy-start.4
  60.3 1.3 %copy-done.4 = f32[24,20,8,128]{3,2,1,0:T(8,128)} copy-done((f32[24,20,8,128]{3,2,1,0:T(8,128)}, f32[24,20,8,128]{3,2,1,0:T(8,128)S(1)}, u32[]{:S(2)}) %copy-start.4) | copy-done | bytes 1966104
  61.6 1.3 %copy-done.5 = f32[24,20,8,128]{3,2,1,0:T(8,128)} copy-done((f32[24,20,8,128]{3,2,1,0:T(8,128)}, f32[24,20,8,128]{3,2,1,0:T(8,128)S(1)}, u32[]{:S(2)}) %copy-start.5) | copy-done | bytes 1966104
  62.9 1.4 %copy-done.6 = f32[24,20,8,128]{3,2,1,0:T(8,128)} copy-done((f32[24,20,8,128]{3,2,1,0:T(8,128)}, f32[24,20,8,128]{3,2,1,0:T(8,128)S(1)}, u32[]{:S(2)}) %copy-start.6) | copy-done | bytes 1966104
  64.2 1.3 %copy-done.7 = f32[24,20,8,128]{3,2,1,0:T(8,128)} copy-done((f32[24,20,8,128]{3,2,1,0:T(8,128)}, f32[24,20,8,128]{3,2,1,0:T(8,128)S(1)}, u32[]{:S(2)}) %copy-start.7) | copy-done | bytes 1966104
  65.5 1.4 %copy-done.8 = f32[24,20,8,128]{3,2,1,0:T(8,128)} copy-done((f32[24,20,8,128]{3,2,1,0:T(8,128)}, f32[24,20,8,128]{3,2,1,0:T(8,128)S(1)}, u32[]{:S(2)}) %copy-start.8) | copy-done | bytes 1966104
  66.9 1.3 %copy-done.9 = f32[24,20,8,128]{3,2,1,0:T(8,128)} copy-done((f32[24,20,8,128]{3,2,1,0:T(8,128)}, f32[24,20,8,128]{3,2,1,0:T(8,128)S(1)}, u32[]{:S(2)}) %copy-start.9) | copy-done | bytes 1966104
  68.2 1.0 all-to-all-done.arrived
  69.2 0.8 copy-done.11
  69.9 40.7 %advect.1 = f32[4,8,5120]{2,1,0:T(8,128)} custom-call(bf16[32,64,128]{2,1,0:T(8,128)(2,1)} %copy-done.11, bf16[1408,1280]{1,0:T(8,128)(2,1)} %fusion.order, bf16[20,256,512]{2,1,0:T(8,128)(2,1)} %constant.62.clone.table, f32[24,20,8,128]{3,2,1,0:T(8,128)} %copy-done.4, f32[24,20,8,128]{3,2,1,0:T(8,128)} %copy-done.5, f32[24,20,8,128]{3,2,1,0:T(8,128)} %copy-done.6, ...), custom_call_target="tpu_custom_call" | custom-call | tf_op jit(solution)/shard_map/advect/pallas_call | solution.py:490
  (25 shorter events, 0.1 us)
Async XLA Ops:
  0.0 9.2 %copy-start.10 = (bf16[2,4,80,1281]{3,2,1,0:T(8,128)(2,1)S(1)}, bf16[2,4,80,1281]{3,2,1,0:T(8,128)(2,1)}, u32[]{:S(2)}) copy-start(bf16[2,4,80,1281]{3,2,1,0:T(8,128)(2,1)} %param.6) | copy-start | bytes 4919044
  0.0 13.5 %copy-start.12 = (s32[640]{0:T(1024)S(1)}, s32[640]{0:T(1024)}, u32[]{:S(2)}) copy-start(s32[640]{0:T(1024)} %param.8) | copy-start | bytes 7684
  2.4 53.6 %collective-permute-start.4 = (bf16[64,5120]{1,0:T(8,128)(2,1)}, bf16[64,5120]{1,0:T(8,128)(2,1)S(1)}, u32[]{:S(2)}, u32[]{:S(2)}) collective-permute-start(bf16[64,5120]{1,0:T(8,128)(2,1)} %bitcast.11), channel_id=1, source_target_pairs={{4,0},{8,4},{12,8},{16,12},{20,16},{24,20},{28,24},{5,1},{9,5},{13... | collective-permute-start | bytes 1966088 | tf_op jit(solution)/shard_map/ppermute | solution.py:552
  3.7 52.3 %collective-permute-start.3 = (bf16[64,5120]{1,0:T(8,128)(2,1)}, bf16[64,5120]{1,0:T(8,128)(2,1)S(1)}, u32[]{:S(2)}, u32[]{:S(2)}) collective-permute-start(bf16[64,5120]{1,0:T(8,128)(2,1)} %bitcast.11), channel_id=1, source_target_pairs={{0,4},{4,8},{8,12},{12,16},{16,20},{20,24},{24,28},{1,5},{5,9},{9,... | collective-permute-start | bytes 1966088 | tf_op jit(solution)/shard_map/ppermute | solution.py:551
  11.4 29.1 %collective-permute-start = (bf16[10,16,1281]{2,1,0:T(8,128)(2,1)}, bf16[10,16,1281]{2,1,0:T(8,128)(2,1)S(1)}, u32[]{:S(2)}, u32[]{:S(2)}) collective-permute-start(bf16[10,16,1281]{2,1,0:T(8,128)(2,1)} %get-tuple-element.20), channel_id=1, source_target_pairs={{0,1},{1,0},{2,3},{3,2},{4,5},{5,4},{6,7},{7,6},{8,9},{9,8},{10,11... | collective-permute-start | bytes 1229768 | tf_op jit(solution)/shard_map/ppermute | solution.py:550
  11.4 13.4 %collective-permute-start.1 = (bf16[10,16,1281]{2,1,0:T(8,128)(2,1)}, bf16[10,16,1281]{2,1,0:T(8,128)(2,1)S(1)}, u32[]{:S(2)}, u32[]{:S(2)}) collective-permute-start(bf16[10,16,1281]{2,1,0:T(8,128)(2,1)} %get-tuple-element.23), channel_id=1, source_target_pairs={{0,2},{1,3},{2,0},{3,1},{4,6},{5,7},{6,4},{7,5},{8,10},{9,11},{10,... | collective-permute-start | bytes 1229768 | tf_op jit(solution)/shard_map/ppermute | solution.py:550
  13.4 20.7 %collective-permute-start.2 = (bf16[10,16,1281]{2,1,0:T(8,128)(2,1)}, bf16[10,16,1281]{2,1,0:T(8,128)(2,1)S(1)}, u32[]{:S(2)}, u32[]{:S(2)}) collective-permute-start(bf16[10,16,1281]{2,1,0:T(8,128)(2,1)} %get-tuple-element.24), channel_id=1, source_target_pairs={{0,3},{1,2},{2,1},{3,0},{4,7},{5,6},{6,5},{7,4},{8,11},{9,10},{10,... | collective-permute-start | bytes 1229768 | tf_op jit(solution)/shard_map/ppermute | solution.py:550
  34.0 2.9 %copy-start = (bf16[20,1281,64]{2,1,0:T(8,128)(2,1)S(1)}, bf16[20,1281,64]{2,1,0:T(8,128)(2,1)}, u32[]{:S(2)}) copy-start(bf16[20,1281,64]{2,1,0:T(8,128)(2,1)} %copy.10.refs_2_) | copy-start | bytes 9838084
  36.9 3.6 %copy-start.1 = (bf16[20,1281,64]{2,1,0:T(8,128)(2,1)S(1)}, bf16[20,1281,64]{2,1,0:T(8,128)(2,1)}, u32[]{:S(2)}) copy-start(bf16[20,1281,64]{2,1,0:T(8,128)(2,1)} %copy.10.refs_2_) | copy-start | bytes 9838084
  45.6 10.4 %copy-start.2 = (f32[4,8,5120]{2,1,0:T(8,128)S(1)}, f32[4,8,5120]{2,1,0:T(8,128)}, u32[]{:S(2)}) copy-start(f32[4,8,5120]{2,1,0:T(8,128)} %lon.1) | copy-start | bytes 1966084
  45.6 10.4 %copy-start.3 = (f32[4,8,5120]{2,1,0:T(8,128)S(1)}, f32[4,8,5120]{2,1,0:T(8,128)}, u32[]{:S(2)}) copy-start(f32[4,8,5120]{2,1,0:T(8,128)} %lat.1) | copy-start | bytes 1966084
  47.7 21.5 %all-to-all-start = ((bf16[32,64,128]{2,1,0:T(8,128)(2,1)}), bf16[32,64,128]{2,1,0:T(8,128)(2,1)S(1)}, u32[]{:S(2)}, u32[]{:S(2)}) async-start(bf16[32,64,128]{2,1,0:T(8,128)(2,1)} %bitcast_select_fusion), calls=%async_computation | async-start | bytes 1048576 | tf_op jit(solution)/shard_map/all_to_all | solution.py:565
  60.3 1.3 %copy-start.4 = (f32[24,20,8,128]{3,2,1,0:T(8,128)}, f32[24,20,8,128]{3,2,1,0:T(8,128)S(1)}, u32[]{:S(2)}) copy-start(f32[24,20,8,128]{3,2,1,0:T(8,128)S(1)} %get-tuple-element.27.cx) | copy-start | bytes 5898244
  61.6 1.3 %copy-start.5 = (f32[24,20,8,128]{3,2,1,0:T(8,128)}, f32[24,20,8,128]{3,2,1,0:T(8,128)S(1)}, u32[]{:S(2)}) copy-start(f32[24,20,8,128]{3,2,1,0:T(8,128)S(1)} %get-tuple-element.28.cy) | copy-start | bytes 5898244
  62.9 1.4 %copy-start.6 = (f32[24,20,8,128]{3,2,1,0:T(8,128)}, f32[24,20,8,128]{3,2,1,0:T(8,128)S(1)}, u32[]{:S(2)}) copy-start(f32[24,20,8,128]{3,2,1,0:T(8,128)S(1)} %get-tuple-element.29.ax) | copy-start | bytes 5898244
  64.2 1.3 %copy-start.7 = (f32[24,20,8,128]{3,2,1,0:T(8,128)}, f32[24,20,8,128]{3,2,1,0:T(8,128)S(1)}, u32[]{:S(2)}) copy-start(f32[24,20,8,128]{3,2,1,0:T(8,128)S(1)} %get-tuple-element.30.bx) | copy-start | bytes 5898244
  65.5 1.4 %copy-start.8 = (f32[24,20,8,128]{3,2,1,0:T(8,128)}, f32[24,20,8,128]{3,2,1,0:T(8,128)S(1)}, u32[]{:S(2)}) copy-start(f32[24,20,8,128]{3,2,1,0:T(8,128)S(1)} %get-tuple-element.31.ay) | copy-start | bytes 5898244
  66.9 1.3 %copy-start.9 = (f32[24,20,8,128]{3,2,1,0:T(8,128)}, f32[24,20,8,128]{3,2,1,0:T(8,128)S(1)}, u32[]{:S(2)}) copy-start(f32[24,20,8,128]{3,2,1,0:T(8,128)S(1)} %get-tuple-element.32.by) | copy-start | bytes 5898244
  69.2 0.8 copy-start.11
where the time goes:
time: 111 us
  Pallas kernels  54.2 us (49%)
  local copies, waits for them, and re-layouts  22.9 us (21%)
  starting transfers between devices  14.9 us (13%)
  waiting for transfers between devices  12.6 us (11%)
  other arithmetic  5.85 us (5%)
    pallas_call x1, Pallas kernels, advect(): pl.pallas_call(functools.partial(advect_kernel, pad), out_shape=jax.Shape...  40.7 us
    unnamed x27, local copies, waits for them, and re-layouts  19 us
    ppermute x3, waiting for transfers between devices, body(): blocks[step] = lax.ppermute(blocks[step], 'lev', pairs)  11.5 us
    pallas_call x2, Pallas kernels, legendre_sums(): pl.pallas_call(functools.partial(legendre_kernel, steps, bands, waves, pa...  7.15 us
    all_to_all x1, starting transfers between devices, body(): lax.all_to_all(stacked.reshape(-1, SUB * SUB, LANES), ('wave', 'lev'), 0,...  5.9 us
    ppermute x1, starting transfers between devices, body(): below = lax.ppermute(upper, 'wave', up)  5.54 us
    pallas_call x1, Pallas kernels, courant_fields(): pl.pallas_call(courant_kernel, out_shape=[out] * 6, compiler_params=param...  4.25 us
    gather x2, local copies, waits for them, and re-layouts, body(): stacked = jnp.take(stacked, level_rank ^ jnp.arange(level_count), axis=1)  2.6 us
  transfers between devices with their start and end apart: 6, of which 3 were waited for; matrix products, arithmetic and copies ran while one was open for 13% of the time, Pallas kernels for 12%

commit v1 on v0

v1 whole, which is shorter than its diff:
```python
import functools
import math

import jax
import jax.numpy as jnp
import ml_dtypes
import numpy as np
from jax import lax
from jax.experimental import pallas as pl
from jax.experimental.pallas import tpu as pltpu
from jax.sharding import PartitionSpec as P

PASSES = 4
HALO = 2 * PASSES
SUB = 8
LANES = 128
F32 = jnp.float32
BF16 = jnp.bfloat16


def params(mib):
    return pltpu.CompilerParams(vmem_limit_bytes=mib << 20)


def lane_index():
    return lax.broadcasted_iota(jnp.int32, (SUB, LANES), 1)


def pack_kernel(count, x_ref, *refs):
    outs, turned = refs[:count], refs[count]
    slots, degrees = x_ref.shape[1:]
    own = slots // count
    me = lax.axis_index("lev")

    def gather(first, rows):
        for lo in range(0, degrees, LANES):
            hi = min(lo + LANES, degrees)
            tile = jnp.stack(
                [x_ref[i, first : first + rows, lo:hi].astype(F32) for i in range(SUB)], 0
            )
            turned[first : first + rows, :, lo:hi] = jnp.swapaxes(tile, 0, 1)

    for first in range(0, slots, SUB):
        gather(first, SUB)
    for step, out in enumerate(outs):
        start = (me ^ step) * own

        def pair(i, carry, out=out, start=start):
            second = jnp.minimum(start + 2 * i + 1, slots - 1)
            both = [turned[start + 2 * i], turned[second]]
            out[i] = jnp.concatenate(both, 0).astype(BF16)
            return carry

        lax.fori_loop(0, out.shape[0], pair, 0)


def pack(spectral, count):
    parts, levels, slots, degrees = spectral.shape
    out = jax.ShapeDtypeStruct((-(-slots // count // 2), 2 * SUB, degrees), BF16)
    return pl.pallas_call(
        functools.partial(pack_kernel, count),
        out_shape=[out] * count,
        scratch_shapes=[pltpu.VMEM((slots, SUB, degrees), F32)],
        compiler_params=params(40),
        name="pack",
    )(spectral.reshape(parts * levels, slots, degrees))


def legendre_kernel(steps, bands, waves, pad, early, pairs_ref, *refs):
    count = len(steps)
    blocks, table, done = refs[:count], refs[count], refs[count + 1 : count + 1 + early]
    outs, sums = refs[count + 1 + early : -1], refs[-1]
    if early:
        me = lax.axis_index("lev")
        outs = [outs[0].at[:, me ^ step] for step in range(early + count)]
        for value, out in zip(done, outs):
            out[...] = value[...]
        outs = outs[early:]
    own, lats, degrees = table.shape
    wide = sums.shape[-1]
    band = lats // bands
    pieces = band // SUB + 2
    if wide > lats:
        sums[...] = jnp.zeros_like(sums)
    elif 2 * own < pad:
        sums[:, 2 * own :] = jnp.zeros((count, pad - 2 * own, SUB, wide), F32)

    def pair(i, carry):
        rows = jnp.concatenate([block[i] for block in blocks], 0).astype(F32)
        row = lax.broadcasted_iota(jnp.int32, rows.shape, 0) % (2 * SUB)
        degree = lax.broadcasted_iota(jnp.int32, rows.shape, 1)
        second = jnp.minimum(2 * i + 1, own - 1)
        bound = waves - jnp.where(row < SUB, pairs_ref[2 * i], pairs_ref[second])
        low = jnp.where(degree < bound, rows, 0.0)
        both = jnp.concatenate([low, rows - low], 0).astype(BF16)
        for j in range(2):
            got = lax.dot_general(
                both,
                table[second if j else 2 * i],
                (((1,), (1,)), ((), ())),
                preferred_element_type=F32,
            )
            for half in range(2):
                for d in range(count):
                    first = (half * count + d) * 2 * SUB + j * SUB
                    sums[d, 4 * i + 2 * j + half, :, :lats] = got[first : first + SUB]
        return carry

    lax.fori_loop(0, blocks[0].shape[0], pair, 0, unroll=5)
    lane = lane_index()
    nothing = jnp.zeros((SUB, LANES), F32)
    for d in range(count):
        tiles = [
            [jnp.swapaxes(sums[d, 8 * g : 8 * g + 8, :, k : k + LANES], 0, 1) for k in range(0, wide, LANES)]
            for g in range(pad // SUB)
        ]
        stood = []
        for i in range(SUB):
            once = [jnp.concatenate([tile[i] for tile in row], 1) for row in tiles]
            spare = (LANES - pieces * pad) // SUB
            tall = once * pieces + [jnp.zeros((SUB, wide), F32)] * spare
            stood.append(jnp.transpose(jnp.concatenate(tall, 0)))
        for w in range(bands):
            for i in range(0, SUB, 2):
                two = []
                for value in stood[i : i + 2]:
                    tile = nothing
                    for piece in reversed(range(pieces)):
                        first = w * band + (piece - 1) * SUB
                        there = value[first : first + SUB] if 0 <= first < lats else nothing
                        tile = there if piece == pieces - 1 else jnp.where(
                            lane < (piece + 1) * pad, there, tile
                        )
                    two.append(tile)
                outs[d][w, i * SUB : (i + 2) * SUB, :] = jnp.concatenate(two, 0).astype(BF16)


def legendre_sums(steps, blocks, table, own_pairs, bands, waves, pad, done=()):
    own, lats, degrees = table.shape
    wide = -(-lats // LANES) * LANES
    outs = [jax.ShapeDtypeStruct((bands, SUB * SUB, LANES), BF16)] * len(steps)
    if done:
        outs = jax.ShapeDtypeStruct((bands, len(done) + len(steps), SUB * SUB, LANES), BF16)
    vmem = pl.BlockSpec(memory_space=pltpu.VMEM)
    return pl.pallas_call(
        functools.partial(legendre_kernel, steps, bands, waves, pad, len(done)),
        out_shape=outs,
        in_specs=[pl.BlockSpec(memory_space=pltpu.SMEM)] + [vmem] * (len(steps) + 1 + len(done)),
        scratch_shapes=[pltpu.VMEM((len(steps), pad, SUB, wide), F32)],
        compiler_params=params(40),
        name="legendre",
    )(own_pairs, *blocks, table, *done)


def west_of_first(last_chunk, levels):
    turned = pltpu.roll(last_chunk, 1, 1)
    return jnp.where(lane_index() == 0, pltpu.roll(turned, levels, 0), turned)


def east_of_last(first_chunk, levels):
    turned = pltpu.roll(first_chunk, LANES - 1, 1)
    return jnp.where(lane_index() == LANES - 1, pltpu.roll(turned, SUB - levels, 0), turned)


def courant_kernel(lon, lat, below, above, far_fields, fields, turned, sems):
    cx, cy, ax, bx, ay, by = [fields.at[i] for i in range(6)]
    levels, band, nlon = lon.shape
    parts = SUB // levels
    rows, chunks = cx.shape[:2]
    span = nlon // parts
    for block in range(rows // SUB):

        def stand(n, carry, block=block):
            tiles = []
            for field, own in enumerate((lon, lat)):
                for part in range(parts):
                    lanes = pl.ds(pl.multiple_of(part * span + n * LANES, LANES), LANES)
                    if 0 < block < rows // SUB - 1:
                        for level in range(levels):
                            tiles.append(own[level, (block - 1) * SUB : block * SUB, lanes])
                    else:
                        far = below if block == 0 else above
                        first = field * levels * SUB
                        tiles.append(far[first : first + levels * SUB, lanes].astype(F32))
            start = pl.multiple_of(n * LANES, LANES)
            turned[pl.ds(start, LANES), :] = jnp.transpose(jnp.concatenate(tiles, 0))
            return carry

        def lie(v, carry, block=block):
            value = jnp.transpose(turned[pl.ds(v, LANES, stride=chunks), :])
            for field, out in enumerate((cx, cy)):
                both = value[field * SUB * SUB : (field + 1) * SUB * SUB]
                both = jnp.swapaxes(both.reshape(SUB, SUB, LANES), 0, 1)
                for t in range(SUB):
                    out[block * SUB + t, v] = both[t]
            return carry

        lax.fori_loop(0, span // LANES, stand, 0, unroll=2)
        lax.fori_loop(0, chunks, lie, 0, unroll=2)

    copies = [pltpu.make_async_copy(fields.at[i], far_fields.at[i], sems.at[i]) for i in range(6)]
    for copy in copies[:2]:
        copy.start()
    for ref in (ax, bx, ay, by):
        for t in (0, rows - 1):
            ref[t] = jnp.zeros(ref.shape[1:], F32)

    def factors(t, carry):
        u = [cx[t, v] for v in range(chunks)]
        w = [cy[t, v] for v in range(chunks)]
        near = [w[v] + cy[t + 1, v] for v in range(chunks)]
        west = [west_of_first(near[-1], levels)] + near[:-1]
        for v in range(chunks):
            ax[t, v] = 0.5 * (jnp.abs(u[v]) - u[v] * u[v])
            bx[t, v] = 0.0625 * u[v] * (near[v] + west[v])
        near = [u[v] + cx[t - 1, v] for v in range(chunks)]
        east = near[1:] + [east_of_last(near[0], levels)]
        for v in range(chunks):
            ay[t, v] = 0.5 * (jnp.abs(w[v]) - w[v] * w[v])
            by[t, v] = 0.0625 * w[v] * (near[v] + east[v])
        return carry

    lax.fori_loop(1, rows - 1, factors, 0)
    for copy in copies[2:]:
        copy.start()
    for copy in copies:
        copy.wait()


def courant_fields(lon, lat, below, above):
    levels, band, nlon = lon.shape
    parts = SUB // levels
    chunks = nlon // (parts * LANES)
    shape = (6, band + 2 * HALO, chunks, SUB, LANES)
    return pl.pallas_call(
        courant_kernel,
        out_shape=pltpu.HBM(shape, F32),
        out_specs=pl.BlockSpec(memory_space=pltpu.HBM),
        scratch_shapes=[
            pltpu.VMEM(shape, F32),
            pltpu.VMEM((nlon // parts, LANES), F32),
            pltpu.SemaphoreType.DMA((6,)),
        ],
        compiler_params=params(28),
        cost_estimate=pl.CostEstimate(
            flops=20_000_000_000, bytes_accessed=20_000_000, transcendentals=0
        ),
        name="courant",
    )(lon, lat, below, above)


def spread(real, imag, count):
    def weighted(function, v, values, parity):
        total = None
        for m in range(parity, len(values), 2):
            factor = function(2.0 * math.pi * (m * v % count) / count)
            if abs(factor) > 1e-9:
                term = values[m] if abs(factor - 1.0) < 1e-9 else factor * values[m]
                total = term if total is None else total + term
        return total

    def add(x, y):
        return y if x is None else x if y is None else x + y

    def subtract(x, y):
        return x if y is None else -y if x is None else x - y

    half = count // 2
    out = [None] * count
    for v in range(half // 2 + 1):
        sums = [
            [weighted(function, v, values, parity) for parity in range(2)]
            for function, values in (
                (math.cos, real),
                (math.sin, imag),
                (math.cos, imag),
                (math.sin, real),
            )
        ]
        (p0, p1), (q0, q1), (r0, r1), (u0, u1) = sums
        found = [(v, add(p0, p1), add(q0, q1), add(r0, r1), add(u0, u1))]
        if v < half - v:
            found.append(
                (half - v, subtract(p0, p1), subtract(q1, q0), subtract(r0, r1), subtract(u1, u0))
            )
        for w, p, q, r, u in found:
            out[w] = (subtract(p, q), add(r, u))
            if 0 < w < half:
                out[count - w] = (add(p, q), subtract(r, u))
    return out


def transform(
    arrived, order, order_copy, twist, table, lhs, mixed, terms, field, pad, levels
):
    sources = arrived.shape[0]
    rows, chunks = field.shape[:2]
    pieces = rows // SUB
    group = LANES // pad
    lane = lax.broadcasted_iota(jnp.int32, (SUB * SUB, LANES), 1)
    height = levels * SUB
    for g in range(-(-sources // group)):
        members = [arrived[q].astype(F32) for q in range(g * group, min(sources, (g + 1) * group))]
        for piece in range(pieces):
            value = None
            for i, member in enumerate(members):
                shift = pad * (i - piece) % LANES
                turned = pltpu.roll(member, shift, 1) if shift else member
                value = turned if value is None else jnp.where(lane >= i * pad, turned, value)
            value = value.astype(BF16)
            for c in range(2):
                first = (c * pieces + piece) * height
                lhs[first : first + height, g * LANES : (g + 1) * LANES] = value[
                    c * height : (c + 1) * height
                ]
    half = pieces * height
    near = table.shape[1]
    depth = mixed.shape[0]
    order_copy.wait()
    for m in range(depth):
        mixed[m] = jnp.dot(
            lhs[...], order[:, m * near : (m + 1) * near], preferred_element_type=F32
        )

    def vary(i, carry):
        span = pl.ds(pl.multiple_of(i * 2 * SUB, 2 * SUB), 2 * SUB)
        other = pl.ds(pl.multiple_of(half + i * 2 * SUB, 2 * SUB), 2 * SUB)
        for lo in range(0, near, LANES):
            lanes = slice(lo, lo + LANES)
            real = [mixed[m, span, lanes] for m in range(depth)]
            imag = [mixed[m, other, lanes] for m in range(depth)]
            for v, (x, y) in enumerate(spread(real, imag, chunks)):
                if v:
                    cos, sin = twist[2 * v : 2 * v + 1, lanes], twist[2 * v + 1 : 2 * v + 2, lanes]
                    x, y = x * cos - y * sin, x * sin + y * cos
                for c, value in enumerate((x, y)):
                    high = value.astype(BF16)
                    low = (value - high.astype(F32)).astype(BF16)
                    terms[v, span, c * near + lo : c * near + lo + LANES] = high
                    terms[v, span, (2 + c) * near + lo : (2 + c) * near + lo + LANES] = low
        return carry

    lax.fori_loop(0, half // (2 * SUB), vary, 0)
    parts = SUB // levels

    group = chunks // 2

    def finish(i, carry):
        both = terms[pl.ds(i * group, group)].reshape(group * half, 4 * near)
        high, low = both[:, : 2 * near], both[:, 2 * near :]
        value = jnp.dot(high, table[: 2 * near], preferred_element_type=F32)
        value += jnp.dot(low, table[: 2 * near], preferred_element_type=F32)
        value += jnp.dot(high, table[2 * near :], preferred_element_type=F32)
        for v in range(group):
            for piece in range(pieces):
                tiles = []
                for part in range(parts):
                    for level in range(levels):
                        first = v * half + (piece * levels + level) * SUB
                        lanes = slice(part * LANES, (part + 1) * LANES)
                        tiles.append(value[first : first + SUB, lanes])
                turned = jnp.swapaxes(jnp.stack(tiles, 0), 0, 1)
                for t in range(SUB):
                    field[piece * SUB + t, i * group + v] = turned[t]
        return carry

    lax.fori_loop(0, chunks // group, finish, 0)


def upwind_rows(t, count, old, new, cx, cy, levels):
    chunks = old.shape[1]
    west = [west_of_first(old[t + r, chunks - 1], levels) for r in range(count)]
    first, base = None, None
    for v in range(chunks + 1):
        if v < chunks:
            q = [old[t - 1 + r, v] for r in range(count + 2)]
            flux_lat, flux_lon = [], []
            for r in range(count + 1):
                speed = cy[t + r, v]
                flux_lat.append(jnp.maximum(speed, 0.0) * q[r] + jnp.minimum(speed, 0.0) * q[r + 1])
            for r in range(count):
                speed = cx[t + r, v]
                flux_lon.append(
                    jnp.maximum(speed, 0.0) * west[r] + jnp.minimum(speed, 0.0) * q[r + 1]
                )
            west = q[1 : count + 1]
            first = flux_lon if v == 0 else first
        else:
            flux_lon = [east_of_last(x, levels) for x in first]
        for r in range(count):
            if v > 0:
                new[t + r, v - 1] = base[r] - flux_lon[r]
        if v < chunks:
            base = [q[r + 1] + flux_lon[r] - (flux_lat[r + 1] - flux_lat[r]) for r in range(count)]


def corrective_rows(t, count, old, new, ax, bx, ay, by, levels):
    chunks = old.shape[1]
    span = range(count + 2)

    def inverse(x):
        return pl.reciprocal(jnp.maximum(x, 1.0), approx=True)

    def flux(a, b, gradient, cross, total, step):
        speed = a * gradient - b * cross
        return speed * total - jnp.abs(speed) * step

    here = [old[t - 1 + r, 0] for r in span]
    start = here
    west = [west_of_first(old[t - 1 + r, chunks - 1], levels) for r in span]
    size, size_west = [jnp.abs(x) for x in here], [jnp.abs(x) for x in west]
    first, base = None, None
    for v in range(chunks + 1):
        if v < chunks:
            if v + 1 < chunks:
                east = [old[t - 1 + r, v + 1] for r in span]
            else:
                east = [east_of_last(x, levels) for x in start]
            size_east = [jnp.abs(x) for x in east]
            flux_lat, flux_lon = [], []
            apart = [east[r] - west[r] for r in span]
            sizes_apart = [size_east[r] + size_west[r] for r in span]
            for r in range(count + 1):
                step = here[r + 1] - here[r]
                gradient = step * inverse(size[r + 1] + size[r])
                cross = (apart[r + 1] + apart[r]) * inverse(sizes_apart[r + 1] + sizes_apart[r])
                flux_lat.append(
                    flux(ay[t + r, v], by[t + r, v], gradient, cross, here[r + 1] + here[r], step)
                )
            total = [here[r] + west[r] for r in span]
            sizes = [size[r] + size_west[r] for r in span]
            for r in range(1, count + 1):
                step = here[r] - west[r]
                gradient = step * inverse(sizes[r])
                cross = (total[r + 1] - total[r - 1]) * inverse(sizes[r + 1] + sizes[r - 1])
                flux_lon.append(
                    flux(ax[t + r - 1, v], bx[t + r - 1, v], gradient, cross, total[r], step)
                )
            first = flux_lon if v == 0 else first
        else:
            flux_lon = [east_of_last(x, levels) for x in first]
        for r in range(count):
            if v > 0:
                new[t + r, v - 1] = base[r] - flux_lon[r]
        if v < chunks:
            base = [
                here[r + 1] + flux_lon[r] - (flux_lat[r + 1] - flux_lat[r]) for r in range(count)
            ]
            west, here, size_west, size = here, east, size, size_east


def advect_kernel(pad, arrived, far_order, twist, table, *refs):
    far_fields, out, fields, order, lhs, mixed, terms, field, upwind, turned, sems = refs
    cx, cy, ax, bx, ay, by = [fields.at[i] for i in range(6)]
    levels, band, nlon = out.shape
    rows, chunks = field.shape[:2]
    copies = [
        pltpu.make_async_copy(far_order, order, sems.at[0]),
        pltpu.make_async_copy(far_fields, fields, sems.at[1]),
    ]
    for copy in copies:
        copy.start()
    transform(
        arrived, order, copies[0], twist, table, lhs, mixed, terms, field, pad, levels
    )
    copies[1].wait()
    outermost = lax.axis_index("wave") == 0

    def clear(where):
        @pl.when(outermost)
        def _():
            where[HALO - 1] = jnp.zeros((chunks, SUB, LANES), F32)

    def one_pass(number, carry):
        start = 2 * number + 1

        def first(i, carry):
            upwind_rows(start + 2 * i, 2, field, upwind, cx, cy, levels)
            return carry

        lax.fori_loop(0, rows // 2 - 1 - 2 * number, first, 0)
        clear(upwind)

        def second(i, carry):
            corrective_rows(start + 1 + 4 * i, 4, upwind, field, ax, bx, ay, by, levels)
            return carry

        lax.fori_loop(0, rows // 4 - 1 - number, second, 0)
        clear(field)
        return carry

    lax.fori_loop(0, PASSES, one_pass, 0)
    span = nlon * levels // SUB
    for block in range(band // SUB):
        first = HALO + block * SUB

        def stand(v, carry, first=first):
            value = jnp.swapaxes(field[pl.ds(first, SUB), v], 0, 1).reshape(SUB * SUB, LANES)
            value = jnp.transpose(jnp.concatenate([value, value], 0))
            turned[pl.ds(v, LANES, stride=chunks), :] = value
            return carry

        lax.fori_loop(0, chunks, stand, 0, unroll=2)
        for n in range(span // LANES):
            value = jnp.transpose(turned[n * LANES : (n + 1) * LANES, :])
            for i in range(SUB):
                lanes = i // levels * span + n * LANES
                out[i % levels, block * SUB : (block + 1) * SUB, lanes : lanes + LANES] = value[
                    i * SUB : (i + 1) * SUB
                ]


def advect(arrived, order, twist, table, fields, shape, pad):
    levels, band, nlon = shape
    rows, chunks = fields.shape[1:3]
    half = rows * levels
    near = table.shape[1]
    order, fields = (pltpu.with_memory_space_constraint(x, pltpu.HBM) for x in (order, fields))
    vmem, far = pl.BlockSpec(memory_space=pltpu.VMEM), pl.BlockSpec(memory_space=pltpu.HBM)
    return pl.pallas_call(
        functools.partial(advect_kernel, pad),
        out_shape=jax.ShapeDtypeStruct(shape, F32),
        in_specs=[vmem, far, vmem, vmem, far],
        scratch_shapes=[
            pltpu.VMEM(fields.shape, F32),
            pltpu.VMEM(order.shape, BF16),
            pltpu.VMEM((2 * half, order.shape[0]), BF16),
            pltpu.VMEM((order.shape[1] // near, 2 * half, near), F32),
            pltpu.VMEM((chunks, half, 4 * near), BF16),
            pltpu.VMEM((rows, chunks, SUB, LANES), F32),
            pltpu.VMEM((rows, chunks, SUB, LANES), F32),
            pltpu.VMEM((nlon * levels // SUB, LANES), F32),
            pltpu.SemaphoreType.DMA((2,)),
        ],
        compiler_params=params(40),
        name="advect",
    )(arrived, order, twist, table, fields)


def fourier_tables(nlon, near):
    chunks = nlon // near
    f = np.arange(near)
    angle = 2.0 * np.pi / nlon * (np.arange(chunks)[:, None] * f[None, :] % nlon)
    twist = np.stack([np.cos(angle), np.sin(angle)], 1).reshape(2 * chunks, near)
    angle = 2.0 * np.pi / near * (f[:, None] * f[None, :] % near)
    whole = np.concatenate([np.cos(angle), -np.sin(angle)], 0).astype(np.float32)
    high = whole.astype(ml_dtypes.bfloat16)
    low = (whole - high.astype(np.float32)).astype(ml_dtypes.bfloat16)
    return twist.astype(np.float32), np.concatenate([high, low], 0)


def order_matrix(wave_table, sources, pad):
    waves = 2 * wave_table.shape[0]
    group = LANES // pad
    numbers = jnp.stack([wave_table, waves - 1 - wave_table], 1).reshape(sources, -1)
    extra = -sources % group
    column = jnp.pad(numbers, ((0, extra), (0, pad - numbers.shape[1])), constant_values=-1)
    column = column.reshape(-1, group * pad)
    column = jnp.pad(column, ((0, 0), (0, LANES - group * pad)), constant_values=-1).reshape(-1, 1)
    weight = jnp.where(column == 0, 1.0, 2.0).astype(BF16)
    return jnp.where(jnp.arange(waves)[None, :] == column, weight, jnp.zeros((), BF16))


def body(spectral, legendre, wave_table, courant_lon, courant_lat):
    wave_count, level_count = lax.axis_size("wave"), lax.axis_size("lev")
    wave_rank, level_rank = lax.axis_index("wave"), lax.axis_index("lev")
    levels, band, nlon = courant_lon.shape
    own = legendre.shape[0]
    waves = 2 * wave_table.shape[0]
    pad = -(-2 * own // SUB) * SUB

    up = [(i, i + 1) for i in range(wave_count - 1)]
    down = [(i + 1, i) for i in range(wave_count - 1)]
    blocks = list(pack(spectral, level_count))
    blocks, courant_lon, courant_lat = lax.optimization_barrier(
        (blocks, courant_lon, courant_lat)
    )
    for step in range(1, level_count):
        pairs = [(i, i ^ step) for i in range(level_count)]
        blocks[step] = lax.ppermute(blocks[step], "lev", pairs)
    winds = jnp.stack([courant_lon, courant_lat], 0).astype(BF16)
    upper = winds[:, :, band - HALO :].reshape(-1, nlon)
    lower = winds[:, :, :HALO].reshape(-1, nlon)
    below = lax.ppermute(upper, "wave", up)
    above = lax.ppermute(lower, "wave", down)

    own_pairs = lax.dynamic_slice_in_dim(
        wave_table, (wave_rank * level_count + level_rank) * own, own
    )
    turned = jnp.swapaxes(legendre, 1, 2)
    half = level_count // 2
    given = (turned, own_pairs, wave_count, waves, pad)
    early = legendre_sums(range(half), blocks[:half], *given)
    order = order_matrix(wave_table, wave_count * level_count, pad)
    early, order = lax.optimization_barrier((tuple(early), order))
    stacked = legendre_sums(range(half, level_count), blocks[half:], *given, done=early)
    arrived = lax.all_to_all(
        stacked.reshape(-1, SUB * SUB, LANES), ("wave", "lev"), 0, 0, tiled=True
    )

    fields = courant_fields(courant_lon, courant_lat, below, above)
    twist, table = fourier_tables(nlon, SUB // levels * LANES)
    return advect(
        arrived, order, jnp.asarray(twist), jnp.asarray(table), fields, courant_lon.shape, pad
    )


def solution(mesh):
    placed = (
        P(None, "lev", "wave", None),
        P(("wave", "lev"), None, None),
        P(),
        P("lev", "wave", None),
        P("lev", "wave", None),
    )
    return jax.shard_map(
        body, mesh=mesh, in_specs=placed, out_specs=P("lev", "wave", None), check_vma=False
    )
```

time: 111 us -> 83.1 us (0.75)
  local copies, waits for them, and re-layouts: 22.9 us -> 4.03 us
  Pallas kernels: 54.2 us -> 43.4 us
  waiting for transfers between devices: 12.6 us -> 14.7 us
  other arithmetic: 5.85 us -> 4.69 us
    pallas_call x1, Pallas kernels: 40.7 us -> 22.4 us  [advect(): pl.pallas_call(functools.partial(advect_kernel, pad), out_shape=jax.Shape...]
    unnamed x27 -> x16, local copies, waits for them, and re-layouts: 19 us -> 3.54 us
    pallas_call x1, Pallas kernels: 4.25 us -> 14 us  [courant_fields(): pl.pallas_call(courant_kernel, out_shape=pltpu.HBM(shape, F32), out_specs...]
    gather x2 -> x0, local copies, waits for them, and re-layouts: 2.6 us -> none  [body(): stacked = jnp.take(stacked, level_rank ^ jnp.arange(level_count), axis=1)]
    pallas_call x2, Pallas kernels: 7.15 us -> 5 us  [legendre_sums(): pl.pallas_call(functools.partial(legendre_kernel, steps, bands, waves, pa...]
    all_to_all x1, starting transfers between devices: 5.9 us -> 7.74 us  [body(): lax.all_to_all(stacked.reshape(-1, SUB * SUB, LANES), ('wave', 'lev'), 0,...]
    ppermute x3, waiting for transfers between devices: 11.5 us -> 13.2 us  [body(): blocks[step] = lax.ppermute(blocks[step], 'lev', pairs)]
  transfers between devices with their start and end apart: 6 -> 6, of which waited for: 3 -> 3; matrix products, arithmetic and copies ran while one was open for 13% -> 4% of each run, Pallas kernels for 12% -> 23%
where the time goes in v1:
time: 83.1 us; the launch traced here: 82.8 us
  Pallas kernels  43.4 us (52%)
  starting transfers between devices  15.9 us (19%)
  waiting for transfers between devices  14.7 us (18%)
  other arithmetic  4.69 us (6%)
  local copies, waits for them, and re-layouts  4.03 us (5%)
    pallas_call x1, Pallas kernels, advect(): pl.pallas_call(functools.partial(advect_kernel, pad), out_shape=jax.Shape...  22.4 us
    pallas_call x1, Pallas kernels, courant_fields(): pl.pallas_call(courant_kernel, out_shape=pltpu.HBM(shape, F32), out_specs...  14 us
    ppermute x3, waiting for transfers between devices, body(): blocks[step] = lax.ppermute(blocks[step], 'lev', pairs)  13.2 us
    all_to_all x1, starting transfers between devices, body(): lax.all_to_all(stacked.reshape(-1, SUB * SUB, LANES), ('wave', 'lev'), 0,...  7.74 us
    pallas_call x2, Pallas kernels, legendre_sums(): pl.pallas_call(functools.partial(legendre_kernel, steps, bands, waves, pa...  5 us
    ppermute x1, starting transfers between devices, body(): below = lax.ppermute(upper, 'wave', up)  4.9 us
    unnamed x16, local copies, waits for them, and re-layouts  3.54 us
    select_n x1, other arithmetic, order_matrix(): jnp.where(jnp.arange(waves)[None, :] == column, weight, jnp.zeros((), BF16))  2.42 us
  transfers between devices with their start and end apart: 6, of which 3 were waited for; matrix products, arithmetic and copies ran while one was open for 4% of the time, Pallas kernels for 23%

profile of v1, /device:TPU:0, one launch (start us, length us, event | category | flops | bytes accessed | tf_op | source)
XLA Modules:
  0.0 82.8 jit_solution(10872332337463657332)
XLA Ops:
  0.0 0.0 copy-start.2
  0.0 1.5 %copy-done.2 = bf16[2,4,80,1281]{3,2,1,0:T(8,128)(2,1)S(1)} copy-done((bf16[2,4,80,1281]{3,2,1,0:T(8,128)(2,1)S(1)}, bf16[2,4,80,1281]{3,2,1,0:T(8,128)(2,1)}, u32[]{:S(2)}) %copy-start.2) | copy-done | bytes 1639704
  1.5 0.0 copy-start.7
  1.5 2.0 %pack.1 = (bf16[10,16,1281]{2,1,0:T(8,128)(2,1)S(1)}, bf16[10,16,1281]{2,1,0:T(8,128)(2,1)S(1)}, bf16[10,16,1281]{2,1,0:T(8,128)(2,1)}, bf16[10,16,1281]{2,1,0:T(8,128)(2,1)}) custom-call(bf16[8,80,1281]{2,1,0:T(8,128)(2,1)S(1)} %bitcast.14), custom_call_target="tpu_custom_call" | custom-call | tf_op jit(solution)/shard_map/pack/pallas_call | solution.py:60
  3.5 1.4 %convert_bitcast_fusion = (bf16[1,4,8,5120]{3,2,1,0:T(8,128)(2,1)S(1)}, bf16[1,4,8,5120]{3,2,1,0:T(8,128)(2,1)S(1)}) fusion(f32[4,8,5120]{2,1,0:T(8,128)} %lat, f32[4,8,5120]{2,1,0:T(8,128)} %lon), kind=kLoop, calls=%fused_computation.3 | loop fusion | flops 327680 | bytes 1966080 | tf_op jit(solution)/shard_map/stack | solution.py:581
  4.8 0.9 %pad_maximum_fusion = bf16[2,4,8,5120]{3,2,1,0:T(8,128)(2,1)} fusion(bf16[1,4,8,5120]{3,2,1,0:T(8,128)(2,1)S(1)} %get-tuple-element.35, bf16[1,4,8,5120]{3,2,1,0:T(8,128)(2,1)S(1)} %get-tuple-element.36), kind=kLoop, calls=%fused_computation.2 | loop fusion | flops 327680 | bytes 1310720 | tf_op jit(solution)/shard_map/stack | solution.py:581
  5.7 4.9 %collective-permute-start.3 = (bf16[64,5120]{1,0:T(8,128)(2,1)}, bf16[64,5120]{1,0:T(8,128)(2,1)S(1)}, u32[]{:S(2)}, u32[]{:S(2)}) collective-permute-start(bf16[64,5120]{1,0:T(8,128)(2,1)} %bitcast.6), channel_id=1, source_target_pairs={{0,4},{4,8},{8,12},{12,16},{16,20},{20,24},{24,28},{1,5},{5,9},{9,... | collective-permute-start | bytes 1966088 | tf_op jit(solution)/shard_map/ppermute | solution.py:584
  10.6 1.3 %collective-permute-start.4 = (bf16[64,5120]{1,0:T(8,128)(2,1)}, bf16[64,5120]{1,0:T(8,128)(2,1)}, u32[]{:S(2)}, u32[]{:S(2)}) collective-permute-start(bf16[64,5120]{1,0:T(8,128)(2,1)} %bitcast.6), channel_id=1, source_target_pairs={{4,0},{8,4},{12,8},{16,12},{20,16},{24,20},{28,24},{5,1},{9,5},{13... | collective-permute-start | bytes 1966088 | tf_op jit(solution)/shard_map/ppermute | solution.py:585
  11.9 0.1 collective-permute-start.2
  12.0 1.6 %collective-permute-start = (bf16[10,16,1281]{2,1,0:T(8,128)(2,1)}, bf16[10,16,1281]{2,1,0:T(8,128)(2,1)S(1)}, u32[]{:S(2)}, u32[]{:S(2)}) collective-permute-start(bf16[10,16,1281]{2,1,0:T(8,128)(2,1)} %get-tuple-element.24), channel_id=1, source_target_pairs={{0,2},{1,3},{2,0},{3,1},{4,6},{5,7},{6,4},{7,5},{8,10},{9,11},{10,... | collective-permute-start | bytes 1229768 | tf_op jit(solution)/shard_map/ppermute | solution.py:580
  13.6 0.3 collective-permute-start.1
  13.9 0.0 copy-done.7
  13.9 0.2 copy.8
  14.1 0.1 reshape.30
  14.3 0.1 reshape.31
  14.4 2.4 %fusion.far_order = bf16[1408,1280]{1,0:T(8,128)(2,1)} fusion(s32[1408]{0:T(1024)S(1)} %pad_bitcast_fusion, bf16[1408]{0:T(1024)(128)(2,1)S(1)} %select_convert_fusion), kind=kLoop, calls=%fused_computation.1 | loop fusion | flops 3604480 | bytes 3612928 | tf_op jit(solution)/shard_map/jit(_where)/select_n | solution.py:561
  16.8 0.1 dynamic_slice.3.pairs_ref
  16.9 0.0 collective-permute-done.2.refs_1_
  16.9 0.0 copy-start
  16.9 2.0 %copy-done = bf16[20,1281,64]{1,2,0:T(8,128)(2,1)S(1)} copy-done((bf16[20,1281,64]{1,2,0:T(8,128)(2,1)S(1)}, bf16[20,1281,64]{1,2,0:T(8,128)(2,1)}, u32[]{:S(2)}) %copy-start) | copy-done | bytes 3279384
  18.9 0.0 copy-start.1
  18.9 2.1 %legendre.2 = (bf16[8,64,128]{2,1,0:T(8,128)(2,1)S(1)}, bf16[8,64,128]{2,1,0:T(8,128)(2,1)S(1)}) custom-call(s32[20]{0:T(128)S(1)} %dynamic_slice.3.pairs_ref, bf16[10,16,1281]{2,1,0:T(8,128)(2,1)S(1)} %get-tuple-element.26.refs_0_, bf16[10,16,1281]{2,1,0:T(8,128)(2,1)S(1)} %collective-permute-done.2.refs_1_, bf16[20,64,1281]{2,1,0:T(8,128)(2,1)S(1)} %bitcast.12), custom_call_target="tpu_custom_call" | custom-call | tf_op jit(solution)/shard_map/legendre/pallas_call | solution.py:145
  21.0 0.0 copy-start.3
  21.0 0.0 copy-start.4
  21.0 4.4 %collective-permute-done.refs_0_ = bf16[10,16,1281]{2,1,0:T(8,128)(2,1)S(1)} collective-permute-done((bf16[10,16,1281]{2,1,0:T(8,128)(2,1)}, bf16[10,16,1281]{2,1,0:T(8,128)(2,1)S(1)}, u32[]{:S(2)}, u32[]{:S(2)}) %collective-permute-start) | collective-permute-done | bytes 409952 | tf_op jit(solution)/shard_map/ppermute | solution.py:580
  25.4 8.7 %collective-permute-done.1.refs_1_ = bf16[10,16,1281]{2,1,0:T(8,128)(2,1)S(1)} collective-permute-done((bf16[10,16,1281]{2,1,0:T(8,128)(2,1)}, bf16[10,16,1281]{2,1,0:T(8,128)(2,1)S(1)}, u32[]{:S(2)}, u32[]{:S(2)}) %collective-permute-start.1) | collective-permute-done | bytes 409952 | tf_op jit(solution)/shard_map/ppermute | solution.py:580
  34.2 0.0 copy-done.1
  34.2 2.9 %legendre.3 = bf16[8,4,64,128]{3,2,1,0:T(8,128)(2,1)} custom-call(s32[20]{0:T(128)S(1)} %dynamic_slice.3.pairs_ref, bf16[10,16,1281]{2,1,0:T(8,128)(2,1)S(1)} %collective-permute-done.refs_0_, bf16[10,16,1281]{2,1,0:T(8,128)(2,1)S(1)} %collective-permute-done.1.refs_1_, bf16[20,64,1281]{2,1,0:T(8,128)(2,1)S(1)} %bitcast.13, ...), custom_call_target="tpu_custom_call" | custom-call | tf_op jit(solution)/shard_map/legendre/pallas_call | solution.py:145
  37.1 7.7 %all-to-all-start = ((bf16[32,64,128]{2,1,0:T(8,128)(2,1)}), bf16[32,64,128]{2,1,0:T(8,128)(2,1)S(1)}, u32[]{:S(2)}, u32[]{:S(2)}) async-start(bf16[32,64,128]{2,1,0:T(8,128)(2,1)} %bitcast.3), calls=%async_computation | async-start | bytes 1048576 | tf_op jit(solution)/shard_map/all_to_all | solution.py:597
  44.9 0.0 copy-start.5
  44.9 0.0 copy-start.6
  44.9 0.0 collective-permute-done.3.below
  44.9 0.0 collective-permute-done.4.above
  44.9 0.0 copy-done.3
  44.9 0.0 copy-done.4
  44.9 14.0 %courant.1.refs_0_ = f32[6,24,20,8,128]{4,3,2,1,0:T(8,128)} custom-call(f32[4,8,5120]{2,1,0:T(8,128)S(1)} %copy-done.3, f32[4,8,5120]{2,1,0:T(8,128)S(1)} %copy-done.4, bf16[64,5120]{1,0:T(8,128)(2,1)S(1)} %collective-permute-done.3.below, bf16[64,5120]{1,0:T(8,128)(2,1)} %collective-permute-done.4.above), custom_call_target="tpu_custom_call" | custom-call | flops 20000000000 | bytes 20000000 | tf_op jit(solution)/shard_map/courant/pallas_call | solution.py:235
  58.9 1.5 %all-to-all-done.arrived = bf16[32,64,128]{2,1,0:T(8,128)(2,1)S(1)} async-done(((bf16[32,64,128]{2,1,0:T(8,128)(2,1)}), bf16[32,64,128]{2,1,0:T(8,128)(2,1)S(1)}, u32[]{:S(2)}, u32[]{:S(2)}) %all-to-all-start) | async-done | bytes 524320 | tf_op jit(solution)/shard_map/all_to_all | solution.py:597
  60.4 0.0 copy-done.5
  60.4 0.0 copy-done.6
  60.4 22.4 %advect.1 = f32[4,8,5120]{2,1,0:T(8,128)} custom-call(bf16[32,64,128]{2,1,0:T(8,128)(2,1)S(1)} %all-to-all-done.arrived, bf16[1408,1280]{1,0:T(8,128)(2,1)} %fusion.far_order, f32[40,256]{1,0:T(8,128)S(1)} %copy-done.6, bf16[1024,256]{1,0:T(8,128)(2,1)S(1)} %copy-done.5, f32[6,24,20,8,128]{4,3,2,1,0:T(8,128)} %courant.1.refs_0_), custom_call_target="tpu_custom_call" | custom-call | tf_op jit(solution)/shard_map/advect/pallas_call | solution.py:520
  (7 shorter events, 0.0 us)
Async XLA Ops:
  0.0 1.5 %copy-start.2 = (bf16[2,4,80,1281]{3,2,1,0:T(8,128)(2,1)S(1)}, bf16[2,4,80,1281]{3,2,1,0:T(8,128)(2,1)}, u32[]{:S(2)}) copy-start(bf16[2,4,80,1281]{3,2,1,0:T(8,128)(2,1)} %param.7) | copy-start | bytes 4919044
  1.5 12.4 %copy-start.7 = (s32[640]{0:T(1024)S(1)}, s32[640]{0:T(1024)}, u32[]{:S(2)}) copy-start(s32[640]{0:T(1024)} %param.9) | copy-start | bytes 7684
  5.7 39.2 %collective-permute-start.3 = (bf16[64,5120]{1,0:T(8,128)(2,1)}, bf16[64,5120]{1,0:T(8,128)(2,1)S(1)}, u32[]{:S(2)}, u32[]{:S(2)}) collective-permute-start(bf16[64,5120]{1,0:T(8,128)(2,1)} %bitcast.6), channel_id=1, source_target_pairs={{0,4},{4,8},{8,12},{12,16},{16,20},{20,24},{24,28},{1,5},{5,9},{9,... | collective-permute-start | bytes 1966088 | tf_op jit(solution)/shard_map/ppermute | solution.py:584
  10.6 34.3 %collective-permute-start.4 = (bf16[64,5120]{1,0:T(8,128)(2,1)}, bf16[64,5120]{1,0:T(8,128)(2,1)}, u32[]{:S(2)}, u32[]{:S(2)}) collective-permute-start(bf16[64,5120]{1,0:T(8,128)(2,1)} %bitcast.6), channel_id=1, source_target_pairs={{4,0},{8,4},{12,8},{16,12},{20,16},{24,20},{28,24},{5,1},{9,5},{13... | collective-permute-start | bytes 1966088 | tf_op jit(solution)/shard_map/ppermute | solution.py:585
  11.9 4.9 %collective-permute-start.2 = (bf16[10,16,1281]{2,1,0:T(8,128)(2,1)S(1)}, bf16[10,16,1281]{2,1,0:T(8,128)(2,1)S(1)}, u32[]{:S(2)}, u32[]{:S(2)}) collective-permute-start(bf16[10,16,1281]{2,1,0:T(8,128)(2,1)S(1)} %get-tuple-element.27), channel_id=1, source_target_pairs={{0,1},{1,0},{2,3},{3,2},{4,5},{5,4},{6,7},{7,6},{8,9},{9,8},{10,11... | collective-permute-start | bytes 1229768 | tf_op jit(solution)/shard_map/ppermute | solution.py:580
  12.0 13.4 %collective-permute-start = (bf16[10,16,1281]{2,1,0:T(8,128)(2,1)}, bf16[10,16,1281]{2,1,0:T(8,128)(2,1)S(1)}, u32[]{:S(2)}, u32[]{:S(2)}) collective-permute-start(bf16[10,16,1281]{2,1,0:T(8,128)(2,1)} %get-tuple-element.24), channel_id=1, source_target_pairs={{0,2},{1,3},{2,0},{3,1},{4,6},{5,7},{6,4},{7,5},{8,10},{9,11},{10,... | collective-permute-start | bytes 1229768 | tf_op jit(solution)/shard_map/ppermute | solution.py:580
  13.6 20.6 %collective-permute-start.1 = (bf16[10,16,1281]{2,1,0:T(8,128)(2,1)}, bf16[10,16,1281]{2,1,0:T(8,128)(2,1)S(1)}, u32[]{:S(2)}, u32[]{:S(2)}) collective-permute-start(bf16[10,16,1281]{2,1,0:T(8,128)(2,1)} %get-tuple-element.25), channel_id=1, source_target_pairs={{0,3},{1,2},{2,1},{3,0},{4,7},{5,6},{6,5},{7,4},{8,11},{9,10},{10,... | collective-permute-start | bytes 1229768 | tf_op jit(solution)/shard_map/ppermute | solution.py:580
  16.9 2.0 %copy-start = (bf16[20,1281,64]{1,2,0:T(8,128)(2,1)S(1)}, bf16[20,1281,64]{1,2,0:T(8,128)(2,1)}, u32[]{:S(2)}) copy-start(bf16[20,1281,64]{1,2,0:T(8,128)(2,1)} %param.8) | copy-start | bytes 9838084
  18.9 15.3 %copy-start.1 = (bf16[20,1281,64]{1,2,0:T(8,128)(2,1)S(1)}, bf16[20,1281,64]{1,2,0:T(8,128)(2,1)}, u32[]{:S(2)}) copy-start(bf16[20,1281,64]{1,2,0:T(8,128)(2,1)} %param.8) | copy-start | bytes 9838084
  21.0 23.9 %copy-start.3 = (f32[4,8,5120]{2,1,0:T(8,128)S(1)}, f32[4,8,5120]{2,1,0:T(8,128)}, u32[]{:S(2)}) copy-start(f32[4,8,5120]{2,1,0:T(8,128)} %lon) | copy-start | bytes 1966084
  21.0 23.9 %copy-start.4 = (f32[4,8,5120]{2,1,0:T(8,128)S(1)}, f32[4,8,5120]{2,1,0:T(8,128)}, u32[]{:S(2)}) copy-start(f32[4,8,5120]{2,1,0:T(8,128)} %lat) | copy-start | bytes 1966084
  37.1 23.3 %all-to-all-start = ((bf16[32,64,128]{2,1,0:T(8,128)(2,1)}), bf16[32,64,128]{2,1,0:T(8,128)(2,1)S(1)}, u32[]{:S(2)}, u32[]{:S(2)}) async-start(bf16[32,64,128]{2,1,0:T(8,128)(2,1)} %bitcast.3), calls=%async_computation | async-start | bytes 1048576 | tf_op jit(solution)/shard_map/all_to_all | solution.py:597
  44.9 15.5 %copy-start.5 = (bf16[1024,256]{1,0:T(8,128)(2,1)S(1)}, bf16[1024,256]{1,0:T(8,128)(2,1)}, u32[]{:S(2)}) copy-start(bf16[1024,256]{1,0:T(8,128)(2,1)} %constant.33.clone.table) | copy-start | bytes 1572868
  44.9 15.5 %copy-start.6 = (f32[40,256]{1,0:T(8,128)S(1)}, f32[40,256]{1,0:T(8,128)}, u32[]{:S(2)}) copy-start(f32[40,256]{1,0:T(8,128)} %constant.32.clone.twist) | copy-start | bytes 122884

commit v2 on v1

--- a/solution.py
+++ b/solution.py
@@ -26,44 +26,64 @@
     return lax.broadcasted_iota(jnp.int32, (SUB, LANES), 1)
 
 
-def pack_kernel(count, x_ref, *refs):
-    outs, turned = refs[:count], refs[count]
-    slots, degrees = x_ref.shape[1:]
-    own = slots // count
+def pack_kernel(count, steps, x_ref, *refs):
+    turned = refs[-1]
+    degrees = x_ref.shape[2]
+    own = turned.shape[0] // (count // 2)
+    pairs = -(-own // 2)
+    whole = degrees // LANES
     me = lax.axis_index("lev")
-
-    def gather(first, rows):
-        for lo in range(0, degrees, LANES):
-            hi = min(lo + LANES, degrees)
-            tile = jnp.stack(
-                [x_ref[i, first : first + rows, lo:hi].astype(F32) for i in range(SUB)], 0
-            )
-            turned[first : first + rows, :, lo:hi] = jnp.swapaxes(tile, 0, 1)
-
-    for first in range(0, slots, SUB):
-        gather(first, SUB)
-    for step, out in enumerate(outs):
-        start = (me ^ step) * own
-
-        def pair(i, carry, out=out, start=start):
-            second = jnp.minimum(start + 2 * i + 1, slots - 1)
-            both = [turned[start + 2 * i], turned[second]]
-            out[i] = jnp.concatenate(both, 0).astype(BF16)
+    there = (me ^ steps[0]) // (count // 2)
+    for part in range(2):
+        start = part * turned.shape[0]
+        first = start // SUB * SUB
+
+        @pl.when(there == part)
+        def _(start=start, first=first):
+            for group in range(first, start + turned.shape[0], SUB):
+                for lo in range(0, degrees, LANES):
+                    hi = min(lo + LANES, degrees)
+                    tile = [x_ref[i, group : group + SUB, lo:hi].astype(F32) for i in range(SUB)]
+                    tile = jnp.swapaxes(jnp.stack(tile, 0), 0, 1)
+                    skip = max(start - group, 0)
+                    keep = min(start + turned.shape[0] - group, SUB)
+                    at = group + skip - start
+                    turned[at : at + keep - skip, :, lo:hi] = tile[skip:keep]
+
+    lane = lax.broadcasted_iota(jnp.int32, (2 * SUB, LANES), 1)
+    for step, out in zip(steps, refs):
+        start = (me ^ step) % (count // 2) * own
+
+        def two(i, start=start):
+            return start + 2 * i, start + jnp.minimum(2 * i + 1, own - 1)
+
+        def pair(i, carry, out=out, two=two):
+            for n in range(whole):
+                both = [turned[slot, :, n * LANES : (n + 1) * LANES] for slot in two(i)]
+                row = pl.multiple_of((i * whole + n) * 2 * SUB, 2 * SUB)
+                out[pl.ds(row, 2 * SUB), :] = jnp.concatenate(both, 0).astype(BF16)
             return carry
 
-        lax.fori_loop(0, out.shape[0], pair, 0)
-
-
-def pack(spectral, count):
-    parts, levels, slots, degrees = spectral.shape
-    out = jax.ShapeDtypeStruct((-(-slots // count // 2), 2 * SUB, degrees), BF16)
+        lax.fori_loop(0, pairs, pair, 0)
+        rest = jnp.zeros((2 * SUB, LANES), F32)
+        for i in range(pairs):
+            last = [turned[slot, :, whole * LANES :] for slot in two(i)]
+            rest = jnp.where(lane == i, jnp.concatenate(last, 0), rest)
+        out[pairs * whole * 2 * SUB :, :] = rest.astype(BF16)
+
+
+def pack(spectral, steps, count):
+    levels, slots, degrees = spectral.shape
+    pairs = -(-slots // count // 2)
+    out = jax.ShapeDtypeStruct(((pairs * (degrees // LANES) + 1) * 2 * SUB, LANES), BF16)
+    spectral = jnp.pad(spectral, ((0, 0), (0, -slots % (2 * SUB)), (0, 0)))
     return pl.pallas_call(
-        functools.partial(pack_kernel, count),
-        out_shape=[out] * count,
-        scratch_shapes=[pltpu.VMEM((slots, SUB, degrees), F32)],
+        functools.partial(pack_kernel, count, steps),
+        out_shape=[out] * len(steps),
+        scratch_shapes=[pltpu.VMEM((slots // 2, SUB, degrees), F32)],
         compiler_params=params(40),
         name="pack",
-    )(spectral.reshape(parts * levels, slots, degrees))
+    )(spectral)
 
 
 def legendre_kernel(steps, bands, waves, pad, early, pairs_ref, *refs):
@@ -77,6 +97,7 @@
             out[...] = value[...]
         outs = outs[early:]
     own, lats, degrees = table.shape
+    whole = degrees // LANES
     wide = sums.shape[-1]
     band = lats // bands
     pieces = band // SUB + 2
@@ -86,7 +107,16 @@
         sums[:, 2 * own :] = jnp.zeros((count, pad - 2 * own, SUB, wide), F32)
 
     def pair(i, carry):
-        rows = jnp.concatenate([block[i] for block in blocks], 0).astype(F32)
+        rows = []
+        for block in blocks:
+            parts = []
+            for n in range(whole):
+                first = pl.multiple_of((i * whole + n) * 2 * SUB, 2 * SUB)
+                parts.append(block[pl.ds(first, 2 * SUB), :].astype(F32))
+            rest = block[block.shape[0] - 2 * SUB :, :].astype(F32)
+            parts.append(pltpu.roll(rest, (LANES - i) % LANES, 1)[:, : degrees - whole * LANES])
+            rows.append(jnp.concatenate(parts, 1))
+        rows = jnp.concatenate(rows, 0)
         row = lax.broadcasted_iota(jnp.int32, rows.shape, 0) % (2 * SUB)
         degree = lax.broadcasted_iota(jnp.int32, rows.shape, 1)
         second = jnp.minimum(2 * i + 1, own - 1)
@@ -106,7 +136,7 @@
                     sums[d, 4 * i + 2 * j + half, :, :lats] = got[first : first + SUB]
         return carry
 
-    lax.fori_loop(0, blocks[0].shape[0], pair, 0, unroll=5)
+    lax.fori_loop(0, -(-own // 2), pair, 0, unroll=5)
     lane = lane_index()
     nothing = jnp.zeros((SUB, LANES), F32)
     for d in range(count):
@@ -162,48 +192,128 @@
     return jnp.where(lane_index() == LANES - 1, pltpu.roll(turned, SUB - levels, 0), turned)
 
 
-def courant_kernel(lon, lat, below, above, far_fields, fields, turned, sems):
-    cx, cy, ax, bx, ay, by = [fields.at[i] for i in range(6)]
+def halo_kernel(lon, lat, *refs):
+    levels, band = lon.shape[:2]
+    for halo, start in zip(refs, (0, band - HALO)):
+        for field, wind in enumerate((lon, lat)):
+            for level in range(0, levels, 2):
+                both = [wind[level + k, start : start + HALO, :] for k in range(2)]
+                row = (field * levels + level) * HALO
+                halo[row : row + 2 * HALO, :] = jnp.concatenate(both, 0).astype(BF16)
+
+
+def halos(lon, lat):
+    levels, band, nlon = lon.shape
+    halo = jax.ShapeDtypeStruct((2 * levels * HALO, nlon), BF16)
+    made = pl.pallas_call(
+        halo_kernel,
+        out_shape=[halo] * (1 if band == HALO else 2),
+        compiler_params=params(12),
+        name="halos",
+    )(lon, lat)
+    return made[0], made[-1]
+
+
+def turn(tiles_of, rows, start, turned):
+    chunks = rows.shape[2]
+
+    def stand(n, carry):
+        first = pl.multiple_of(n * LANES, LANES)
+        turned[pl.ds(first, LANES), :] = jnp.transpose(jnp.concatenate(tiles_of(n), 0))
+        return carry
+
+    def lie(v, carry):
+        value = jnp.transpose(turned[pl.ds(v, LANES, stride=chunks), :])
+        for field in range(2):
+            both = value[field * SUB * SUB : (field + 1) * SUB * SUB]
+            both = jnp.swapaxes(both.reshape(SUB, SUB, LANES), 0, 1)
+            for t in range(SUB):
+                rows[field, start + t, v] = both[t]
+        return carry
+
+    lax.fori_loop(0, turned.shape[0] // LANES, stand, 0, unroll=4)
+    lax.fori_loop(0, chunks, lie, 0, unroll=4)
+
+
+def lanes_of(part, n, span):
+    return pl.ds(pl.multiple_of(part * span + n * LANES, LANES), LANES)
+
+
+def own_courant_kernel(lon, lat, own, rows, turned, sem):
+    levels, band, _ = lon.shape
+    for start in range(0, band, SUB):
+
+        def tiles_of(n, start=start):
+            return [
+                wind[level, start : start + SUB, lanes_of(part, n, turned.shape[0])]
+                for wind in (lon, lat)
+                for part in range(SUB // levels)
+                for level in range(levels)
+            ]
+
+        turn(tiles_of, rows, start, turned)
+    copy = pltpu.make_async_copy(rows, own, sem)
+    copy.start()
+    copy.wait()
+
+
+def own_courant(lon, lat):
     levels, band, nlon = lon.shape
     parts = SUB // levels
-    rows, chunks = cx.shape[:2]
-    span = nlon // parts
-    for block in range(rows // SUB):
-
-        def stand(n, carry, block=block):
-            tiles = []
-            for field, own in enumerate((lon, lat)):
-                for part in range(parts):
-                    lanes = pl.ds(pl.multiple_of(part * span + n * LANES, LANES), LANES)
-                    if 0 < block < rows // SUB - 1:
-                        for level in range(levels):
-                            tiles.append(own[level, (block - 1) * SUB : block * SUB, lanes])
-                    else:
-                        far = below if block == 0 else above
-                        first = field * levels * SUB
-                        tiles.append(far[first : first + levels * SUB, lanes].astype(F32))
-            start = pl.multiple_of(n * LANES, LANES)
-            turned[pl.ds(start, LANES), :] = jnp.transpose(jnp.concatenate(tiles, 0))
-            return carry
-
-        def lie(v, carry, block=block):
-            value = jnp.transpose(turned[pl.ds(v, LANES, stride=chunks), :])
-            for field, out in enumerate((cx, cy)):
-                both = value[field * SUB * SUB : (field + 1) * SUB * SUB]
-                both = jnp.swapaxes(both.reshape(SUB, SUB, LANES), 0, 1)
-                for t in range(SUB):
-                    out[block * SUB + t, v] = both[t]
-            return carry
-
-        lax.fori_loop(0, span // LANES, stand, 0, unroll=2)
-        lax.fori_loop(0, chunks, lie, 0, unroll=2)
-
-    copies = [pltpu.make_async_copy(fields.at[i], far_fields.at[i], sems.at[i]) for i in range(6)]
-    for copy in copies[:2]:
-        copy.start()
-    for ref in (ax, bx, ay, by):
-        for t in (0, rows - 1):
-            ref[t] = jnp.zeros(ref.shape[1:], F32)
+    shape = (2, band, nlon // (parts * LANES), SUB, LANES)
+    return pl.pallas_call(
+        own_courant_kernel,
+        out_shape=pltpu.HBM(shape, F32),
+        out_specs=pl.BlockSpec(memory_space=pltpu.HBM),
+        scratch_shapes=[
+            pltpu.VMEM(shape, F32),
+            pltpu.VMEM((nlon // parts, LANES), F32),
+            pltpu.SemaphoreType.DMA,
+        ],
+        compiler_params=params(16),
+        name="own_courant",
+    )(lon, lat)
+
+
+def factor_kernel(levels, side, own, *refs):
+    far_out, fields, sems = refs[1:4] if side else refs
+    cx, cy, ax, bx, ay, by = [fields.at[i] for i in range(6)]
+    rows, chunks = fields.shape[1:3]
+    band = own.shape[1]
+    if side:
+        start, at = (0, HALO) if side < 0 else (band - 2, 0)
+        source, target = own.at[:, pl.ds(start, 2)], fields.at[pl.ds(0, 2), pl.ds(at, 2)]
+    else:
+        source, target = own, fields.at[pl.ds(0, 2)]
+    copy = pltpu.make_async_copy(source, target, sems.at[0])
+    copy.start()
+    if side:
+        received, turned = refs[0], refs[-1]
+
+        def tiles_of(n):
+            height = levels * SUB
+            return [
+                received[wind * height : (wind + 1) * height, lanes_of(part, n, turned.shape[0])].astype(F32)
+                for wind in range(2)
+                for part in range(SUB // levels)
+            ]
+
+        turn(tiles_of, fields, 0 if side < 0 else 2, turned)
+    copy.wait()
+    low = 0 if side < 0 else 1
+    height = far_out.shape[1]
+    copies = [
+        pltpu.make_async_copy(
+            fields.at[pl.ds(i, count), pl.ds(low, height)],
+            far_out.at[pl.ds(i, count)],
+            sems.at[1 + k],
+        )
+        for k, (i, count) in enumerate(((0, 2), (2, 4)))
+    ]
+    copies[0].start()
+    if side:
+        for i in range(2, 6):
+            fields[i, 0 if side < 0 else rows - 1] = jnp.zeros((chunks, SUB, LANES), F32)
 
     def factors(t, carry):
         u = [cx[t, v] for v in range(chunks)]
@@ -221,32 +331,35 @@
         return carry
 
     lax.fori_loop(1, rows - 1, factors, 0)
-    for copy in copies[2:]:
-        copy.start()
+    copies[1].start()
     for copy in copies:
         copy.wait()
 
 
-def courant_fields(lon, lat, below, above):
-    levels, band, nlon = lon.shape
-    parts = SUB // levels
-    chunks = nlon // (parts * LANES)
-    shape = (6, band + 2 * HALO, chunks, SUB, LANES)
+def factor_rows(own, received, side, levels):
+    _, band, chunks, _, _ = own.shape
+    rows = HALO + 2 if side else band
+    out = HALO + 1 if side else band - 2
+    vmem, far = pl.BlockSpec(memory_space=pltpu.VMEM), pl.BlockSpec(memory_space=pltpu.HBM)
+    extra = (received,) if side else ()
     return pl.pallas_call(
-        courant_kernel,
-        out_shape=pltpu.HBM(shape, F32),
-        out_specs=pl.BlockSpec(memory_space=pltpu.HBM),
+        functools.partial(factor_kernel, levels, side),
+        out_shape=pltpu.HBM((6, out, chunks, SUB, LANES), F32),
+        in_specs=[far] + [vmem] * len(extra),
+        out_specs=far,
         scratch_shapes=[
-            pltpu.VMEM(shape, F32),
-            pltpu.VMEM((nlon // parts, LANES), F32),
-            pltpu.SemaphoreType.DMA((6,)),
-        ],
-        compiler_params=params(28),
+            pltpu.VMEM((6, rows, chunks, SUB, LANES), F32),
+            pltpu.SemaphoreType.DMA((3,)),
+        ]
+        + [pltpu.VMEM((chunks * LANES, LANES), F32)] * len(extra),
+        compiler_params=params(16),
         cost_estimate=pl.CostEstimate(
-            flops=20_000_000_000, bytes_accessed=20_000_000, transcendentals=0
+            flops=30_000_000_000 if side > 0 else 1_000_000_000,
+            bytes_accessed=8_000_000,
+            transcendentals=0,
         ),
-        name="courant",
-    )(lon, lat, below, above)
+        name="factors",
+    )(pltpu.with_memory_space_constraint(own, pltpu.HBM), *extra)
 
 
 def spread(real, imag, count):
@@ -450,20 +563,24 @@
 
 
 def advect_kernel(pad, arrived, far_order, twist, table, *refs):
-    far_fields, out, fields, order, lhs, mixed, terms, field, upwind, turned, sems = refs
+    far_fields = refs[:3]
+    out, fields, order, lhs, mixed, terms, field, upwind, turned, sems = refs[3:]
     cx, cy, ax, bx, ay, by = [fields.at[i] for i in range(6)]
     levels, band, nlon = out.shape
     rows, chunks = field.shape[:2]
-    copies = [
-        pltpu.make_async_copy(far_order, order, sems.at[0]),
-        pltpu.make_async_copy(far_fields, fields, sems.at[1]),
-    ]
+    copies = [pltpu.make_async_copy(far_order, order, sems.at[0])]
+    start = 0
+    for i, far in enumerate(far_fields):
+        place = fields.at[:, pl.ds(start, far.shape[1])]
+        copies.append(pltpu.make_async_copy(far, place, sems.at[1 + i]))
+        start += far.shape[1]
     for copy in copies:
         copy.start()
     transform(
         arrived, order, copies[0], twist, table, lhs, mixed, terms, field, pad, levels
     )
-    copies[1].wait()
+    for copy in copies[1:]:
+        copy.wait()
     outermost = lax.axis_index("wave") == 0
 
     def clear(where):
@@ -512,17 +629,19 @@
 
 def advect(arrived, order, twist, table, fields, shape, pad):
     levels, band, nlon = shape
-    rows, chunks = fields.shape[1:3]
+    rows, chunks = sum(x.shape[1] for x in fields), fields[0].shape[2]
     half = rows * levels
     near = table.shape[1]
-    order, fields = (pltpu.with_memory_space_constraint(x, pltpu.HBM) for x in (order, fields))
+    order, *fields = [
+        pltpu.with_memory_space_constraint(x, pltpu.HBM) for x in (order, *fields)
+    ]
     vmem, far = pl.BlockSpec(memory_space=pltpu.VMEM), pl.BlockSpec(memory_space=pltpu.HBM)
     return pl.pallas_call(
         functools.partial(advect_kernel, pad),
         out_shape=jax.ShapeDtypeStruct(shape, F32),
-        in_specs=[vmem, far, vmem, vmem, far],
+        in_specs=[vmem, far, vmem, vmem] + [far] * 3,
         scratch_shapes=[
-            pltpu.VMEM(fields.shape, F32),
+            pltpu.VMEM((6, rows, chunks, SUB, LANES), F32),
             pltpu.VMEM(order.shape, BF16),
             pltpu.VMEM((2 * half, order.shape[0]), BF16),
             pltpu.VMEM((order.shape[1] // near, 2 * half, near), F32),
@@ -530,11 +649,11 @@
             pltpu.VMEM((rows, chunks, SUB, LANES), F32),
             pltpu.VMEM((rows, chunks, SUB, LANES), F32),
             pltpu.VMEM((nlon * levels // SUB, LANES), F32),
-            pltpu.SemaphoreType.DMA((2,)),
+            pltpu.SemaphoreType.DMA((4,)),
         ],
         compiler_params=params(40),
         name="advect",
-    )(arrived, order, twist, table, fields)
+    )(arrived, order, twist, table, *fields)
 
 
 def fourier_tables(nlon, near):
@@ -571,16 +690,17 @@
 
     up = [(i, i + 1) for i in range(wave_count - 1)]
     down = [(i + 1, i) for i in range(wave_count - 1)]
-    blocks = list(pack(spectral, level_count))
-    blocks, courant_lon, courant_lat = lax.optimization_barrier(
-        (blocks, courant_lon, courant_lat)
-    )
+    spectral = spectral.reshape((-1,) + spectral.shape[2:])
+    half = level_count // 2
+    far_blocks = pack(spectral, range(half, level_count), level_count)
+    far_blocks, spectral = lax.optimization_barrier((far_blocks, spectral))
+    blocks = list(pack(spectral, range(half), level_count)) + list(far_blocks)
     for step in range(1, level_count):
         pairs = [(i, i ^ step) for i in range(level_count)]
         blocks[step] = lax.ppermute(blocks[step], "lev", pairs)
-    winds = jnp.stack([courant_lon, courant_lat], 0).astype(BF16)
-    upper = winds[:, :, band - HALO :].reshape(-1, nlon)
-    lower = winds[:, :, :HALO].reshape(-1, nlon)
+    blocks[1], winds = lax.optimization_barrier((blocks[1], (courant_lon, courant_lat)))
+    lower, upper = halos(*winds)
+    own_winds = own_courant(*winds)
     below = lax.ppermute(upper, "wave", up)
     above = lax.ppermute(lower, "wave", down)
 
@@ -588,17 +708,21 @@
         wave_table, (wave_rank * level_count + level_rank) * own, own
     )
     turned = jnp.swapaxes(legendre, 1, 2)
-    half = level_count // 2
     given = (turned, own_pairs, wave_count, waves, pad)
-    early = legendre_sums(range(half), blocks[:half], *given)
+    sums = list(legendre_sums(range(half), blocks[:half], *given))
     order = order_matrix(wave_table, wave_count * level_count, pad)
-    early, order = lax.optimization_barrier((tuple(early), order))
-    stacked = legendre_sums(range(half, level_count), blocks[half:], *given, done=early)
+    sums, order, own_winds = lax.optimization_barrier((sums, order, own_winds))
+    for step in range(half, level_count - 1):
+        sums += legendre_sums([step], blocks[step : step + 1], *given)
+    stacked = legendre_sums([level_count - 1], blocks[-1:], *given, done=tuple(sums))
     arrived = lax.all_to_all(
         stacked.reshape(-1, SUB * SUB, LANES), ("wave", "lev"), 0, 0, tiled=True
     )
 
-    fields = courant_fields(courant_lon, courant_lat, below, above)
+    fields = [
+        factor_rows(own_winds, received, side, levels)
+        for side, received in ((-1, below), (0, None), (1, above))
+    ]
     twist, table = fourier_tables(nlon, SUB // levels * LANES)
     return advect(
         arrived, order, jnp.asarray(twist), jnp.asarray(table), fields, courant_lon.shape, pad

time: 83.1 us -> 77.9 us (0.937)
  the two profiles are of different devices: /device:TPU:0 before, /device:TPU:26 now
where the time goes in v2:
time: 77.9 us; the launch traced here: 77.5 us
  Pallas kernels  48.1 us (62%)
  starting transfers between devices  13.4 us (17%)
  waiting for transfers between devices  7.47 us (10%)
  local copies, waits for them, and re-layouts  5.81 us (7%)
  other arithmetic  2.45 us (3%)
    pallas_call x1, Pallas kernels, advect(): pl.pallas_call(functools.partial(advect_kernel, pad), out_shape=jax.Shape...  22.4 us
    pallas_call x3, Pallas kernels, factor_rows(): pl.pallas_call(functools.partial(factor_kernel, levels, side), out_shape=...  12.8 us
    ppermute x1, waiting for transfers between devices, body(): above = lax.ppermute(lower, 'wave', down)  7.46 us
    pallas_call x3, Pallas kernels, legendre_sums(): pl.pallas_call(functools.partial(legendre_kernel, steps, bands, waves, pa...  7.11 us
    unnamed x20, local copies, waits for them, and re-layouts  5.32 us
    all_to_all x1, starting transfers between devices, body(): lax.all_to_all(stacked.reshape(-1, SUB * SUB, LANES), ('wave', 'lev'), 0,...  4.93 us
    pallas_call x2, Pallas kernels, pack(): pl.pallas_call(functools.partial(pack_kernel, count, steps), out_shape=[o...  3.35 us
    ppermute x1, starting transfers between devices, body(): below = lax.ppermute(upper, 'wave', up)  3.34 us
  transfers between devices with their start and end apart: 6, of which 1 were waited for; matrix products, arithmetic and copies ran while one was open for 4% of the time, Pallas kernels for 29%

profile of v2, /device:TPU:26, one launch (start us, length us, event | category | flops | bytes accessed | tf_op | source)
XLA Modules:
  0.0 77.5 jit_solution(3580146528195408363)
XLA Ops:
  0.0 0.0 copy-start.2
  0.0 1.5 %copy-done.2 = bf16[2,4,80,1281]{3,2,1,0:T(8,128)(2,1)S(1)} copy-done((bf16[2,4,80,1281]{3,2,1,0:T(8,128)(2,1)S(1)}, bf16[2,4,80,1281]{3,2,1,0:T(8,128)(2,1)}, u32[]{:S(2)}) %copy-start.2) | copy-done | bytes 1639704
  1.5 0.0 copy-start.9
  1.5 0.0 copy-start.3
  1.5 0.0 copy-start.4
  1.5 1.7 %pack.2 = (bf16[1616,128]{1,0:T(8,128)(2,1)}, bf16[1616,128]{1,0:T(8,128)(2,1)}) custom-call(bf16[8,80,1281]{2,1,0:T(8,128)(2,1)S(1)} %bitcast.10), custom_call_target="tpu_custom_call" | custom-call | tf_op jit(solution)/shard_map/pack/pallas_call | solution.py:80
  3.2 1.6 %pack.3 = (bf16[1616,128]{1,0:T(8,128)(2,1)S(1)}, bf16[1616,128]{1,0:T(8,128)(2,1)}) custom-call(bf16[8,80,1281]{2,1,0:T(8,128)(2,1)S(1)} %bitcast.11), custom_call_target="tpu_custom_call" | custom-call | tf_op jit(solution)/shard_map/pack/pallas_call | solution.py:80
  4.8 0.0 collective-permute-start.1
  4.8 0.5 collective-permute-start.2
  5.4 1.3 %collective-permute-start = (bf16[1616,128]{1,0:T(8,128)(2,1)}, bf16[1616,128]{1,0:T(8,128)(2,1)S(1)}, u32[]{:S(2)}, u32[]{:S(2)}) collective-permute-start(bf16[1616,128]{1,0:T(8,128)(2,1)} %get-tuple-element.23), channel_id=1, source_target_pairs={{0,3},{1,2},{2,1},{3,0},{4,7},{5,6},{6,5},{7,4},{8,11},{9,10},{10,... | collective-permute-start | bytes 1241096 | tf_op jit(solution)/shard_map/ppermute | solution.py:700
  6.7 0.0 copy-done.9
  6.7 0.2 copy.8
  6.9 0.1 reshape.26
  7.1 0.1 reshape.27
  7.2 0.0 collective-permute-done.1.refs_1_
  7.2 0.0 copy-start.6
  7.2 0.8 %copy-done.6 = bf16[1616,128]{1,0:T(8,128)(2,1)} copy-done((bf16[1616,128]{1,0:T(8,128)(2,1)}, bf16[1616,128]{1,0:T(8,128)(2,1)S(1)}, u32[]{:S(2)}) %copy-start.6) | copy-done | bytes 413720
  8.0 0.0 copy-done.3
  8.0 0.0 copy-done.4
  8.0 0.1 halos.1
  8.1 3.3 %collective-permute-start.4 = (bf16[64,5120]{1,0:T(8,128)(2,1)S(1)}, bf16[64,5120]{1,0:T(8,128)(2,1)}, u32[]{:S(2)}, u32[]{:S(2)}) collective-permute-start(bf16[64,5120]{1,0:T(8,128)(2,1)S(1)} %halos.1), channel_id=1, source_target_pairs={{4,0},{8,4},{12,8},{16,12},{20,16},{24,20},{28,24},{5,1},{9,5},{13... | collective-permute-start | bytes 1966088 | tf_op jit(solution)/shard_map/ppermute | solution.py:705
  11.4 2.4 %fusion.far_order = bf16[1408,1280]{1,0:T(8,128)(2,1)} fusion(s32[1408]{0:T(1024)S(1)} %pad_bitcast_fusion, bf16[1408]{0:T(1024)(128)(2,1)S(1)} %select_convert_fusion), kind=kLoop, calls=%fused_computation.1 | loop fusion | flops 3604480 | bytes 3612928 | tf_op jit(solution)/shard_map/jit(_where)/select_n | solution.py:680
  13.8 0.1 dynamic_slice.3.pairs_ref
  13.9 2.5 %own_courant.1.own = f32[2,8,20,8,128]{4,3,2,1,0:T(8,128)} custom-call(f32[4,8,5120]{2,1,0:T(8,128)S(1)} %copy-done.3, f32[4,8,5120]{2,1,0:T(8,128)S(1)} %copy-done.4), custom_call_target="tpu_custom_call" | custom-call | tf_op jit(solution)/shard_map/own_courant/pallas_call | solution.py:264
  16.4 3.3 %collective-permute-start.3 = (bf16[64,5120]{1,0:T(8,128)(2,1)S(1)}, bf16[64,5120]{1,0:T(8,128)(2,1)S(1)}, u32[]{:S(2)}, u32[]{:S(2)}) collective-permute-start(bf16[64,5120]{1,0:T(8,128)(2,1)S(1)} %halos.1), channel_id=1, source_target_pairs={{0,4},{4,8},{8,12},{12,16},{16,20},{20,24},{24,28},{1,5},{5,9},{9,... | collective-permute-start | bytes 1966088 | tf_op jit(solution)/shard_map/ppermute | solution.py:704
  19.7 0.0 copy-start
  19.7 2.0 %copy-done = bf16[20,1281,64]{1,2,0:T(8,128)(2,1)S(1)} copy-done((bf16[20,1281,64]{1,2,0:T(8,128)(2,1)S(1)}, bf16[20,1281,64]{1,2,0:T(8,128)(2,1)}, u32[]{:S(2)}) %copy-start) | copy-done | bytes 3279384
  21.7 0.0 copy-start.7
  21.7 1.0 %copy-done.7 = bf16[1616,128]{1,0:T(8,128)(2,1)S(1)} copy-done((bf16[1616,128]{1,0:T(8,128)(2,1)S(1)}, bf16[1616,128]{1,0:T(8,128)(2,1)}, u32[]{:S(2)}) %copy-start.7) | copy-done | bytes 413720
  22.7 0.0 copy-start.1
  22.7 2.2 %legendre.3 = (bf16[8,64,128]{2,1,0:T(8,128)(2,1)S(1)}, bf16[8,64,128]{2,1,0:T(8,128)(2,1)S(1)}) custom-call(s32[20]{0:T(128)S(1)} %dynamic_slice.3.pairs_ref, bf16[1616,128]{1,0:T(8,128)(2,1)S(1)} %get-tuple-element.25.refs_0_, bf16[1616,128]{1,0:T(8,128)(2,1)S(1)} %copy-done.7, bf16[20,64,1281]{2,1,0:T(8,128)(2,1)S(1)} %bitcast.7), custom_call_target="tpu_custom_call" | custom-call | tf_op jit(solution)/shard_map/legendre/pallas_call | solution.py:175
  24.9 0.0 collective-permute-done.2.refs_0_
  24.9 0.0 copy-done.1
  24.9 2.1 %legendre.4.refs_4_ = bf16[8,64,128]{2,1,0:T(8,128)(2,1)S(1)} custom-call(s32[20]{0:T(128)S(1)} %dynamic_slice.3.pairs_ref, bf16[1616,128]{1,0:T(8,128)(2,1)S(1)} %collective-permute-done.2.refs_0_, bf16[20,64,1281]{2,1,0:T(8,128)(2,1)S(1)} %bitcast.8), custom_call_target="tpu_custom_call" | custom-call | tf_op jit(solution)/shard_map/legendre/pallas_call | solution.py:175
  27.0 0.0 collective-permute-done.refs_0_
  27.0 2.9 %legendre.5 = bf16[8,4,64,128]{3,2,1,0:T(8,128)(2,1)} custom-call(s32[20]{0:T(128)S(1)} %dynamic_slice.3.pairs_ref, bf16[1616,128]{1,0:T(8,128)(2,1)S(1)} %collective-permute-done.refs_0_, bf16[20,64,1281]{2,1,0:T(8,128)(2,1)S(1)} %bitcast.9, bf16[8,64,128]{2,1,0:T(8,128)(2,1)S(1)} %get-tuple-element.32.refs_2_, ...), custom_call_target="tpu_custom_call" | custom-call | tf_op jit(solution)/shard_map/legendre/pallas_call | solution.py:175
  29.9 4.9 %all-to-all-start = ((bf16[32,64,128]{2,1,0:T(8,128)(2,1)}), bf16[32,64,128]{2,1,0:T(8,128)(2,1)S(1)}, u32[]{:S(2)}, u32[]{:S(2)}) async-start(bf16[32,64,128]{2,1,0:T(8,128)(2,1)} %bitcast.3), calls=%async_computation | async-start | bytes 1048576 | tf_op jit(solution)/shard_map/all_to_all | solution.py:718
  34.8 3.5 %factors.4.refs_1_ = f32[6,6,20,8,128]{4,3,2,1,0:T(8,128)} custom-call(f32[2,8,20,8,128]{4,3,2,1,0:T(8,128)} %own_courant.1.own), custom_call_target="tpu_custom_call" | custom-call | flops 1000000000 | bytes 8000000 | tf_op jit(solution)/shard_map/factors/pallas_call | solution.py:345
  38.3 7.5 %collective-permute-done.4.refs_0_ = bf16[64,5120]{1,0:T(8,128)(2,1)} collective-permute-done((bf16[64,5120]{1,0:T(8,128)(2,1)S(1)}, bf16[64,5120]{1,0:T(8,128)(2,1)}, u32[]{:S(2)}, u32[]{:S(2)}) %collective-permute-start.4) | collective-permute-done | bytes 655392 | tf_op jit(solution)/shard_map/ppermute | solution.py:705
  45.8 5.1 %factors.5.refs_2_ = f32[6,9,20,8,128]{4,3,2,1,0:T(8,128)} custom-call(f32[2,8,20,8,128]{4,3,2,1,0:T(8,128)} %own_courant.1.own, bf16[64,5120]{1,0:T(8,128)(2,1)} %collective-permute-done.4.refs_0_), custom_call_target="tpu_custom_call" | custom-call | flops 30000001024 | bytes 8000000 | tf_op jit(solution)/shard_map/factors/pallas_call | solution.py:345
  50.9 0.0 copy-start.5
  50.9 0.0 copy-start.8
  51.0 0.0 collective-permute-done.3.refs_0_
  51.0 4.1 %factors.3.refs_0_ = f32[6,9,20,8,128]{4,3,2,1,0:T(8,128)} custom-call(f32[2,8,20,8,128]{4,3,2,1,0:T(8,128)} %own_courant.1.own, bf16[64,5120]{1,0:T(8,128)(2,1)S(1)} %collective-permute-done.3.refs_0_), custom_call_target="tpu_custom_call" | custom-call | flops 1000000000 | bytes 8000000 | tf_op jit(solution)/shard_map/factors/pallas_call | solution.py:345
  55.1 0.0 all-to-all-done.arrived
  55.1 0.0 copy-done.5
  55.1 0.0 copy-done.8
  55.1 22.4 %advect.1 = f32[4,8,5120]{2,1,0:T(8,128)} custom-call(bf16[32,64,128]{2,1,0:T(8,128)(2,1)S(1)} %all-to-all-done.arrived, bf16[1408,1280]{1,0:T(8,128)(2,1)} %fusion.far_order, f32[40,256]{1,0:T(8,128)S(1)} %copy-done.8, bf16[1024,256]{1,0:T(8,128)(2,1)S(1)} %copy-done.5, f32[6,9,20,8,128]{4,3,2,1,0:T(8,128)} %factors.3.refs_0_, ...), custom_call_target="tpu_custom_call" | custom-call | tf_op jit(solution)/shard_map/advect/pallas_call | solution.py:639
  (7 shorter events, 0.0 us)
Async XLA Ops:
  0.0 1.5 %copy-start.2 = (bf16[2,4,80,1281]{3,2,1,0:T(8,128)(2,1)S(1)}, bf16[2,4,80,1281]{3,2,1,0:T(8,128)(2,1)}, u32[]{:S(2)}) copy-start(bf16[2,4,80,1281]{3,2,1,0:T(8,128)(2,1)} %param.7) | copy-start | bytes 4919044
  1.5 5.2 %copy-start.9 = (s32[640]{0:T(1024)S(1)}, s32[640]{0:T(1024)}, u32[]{:S(2)}) copy-start(s32[640]{0:T(1024)} %param.9) | copy-start | bytes 7684
  1.5 6.5 %copy-start.3 = (f32[4,8,5120]{2,1,0:T(8,128)S(1)}, f32[4,8,5120]{2,1,0:T(8,128)}, u32[]{:S(2)}) copy-start(f32[4,8,5120]{2,1,0:T(8,128)} %lon.1) | copy-start | bytes 1966084
  1.5 6.5 %copy-start.4 = (f32[4,8,5120]{2,1,0:T(8,128)S(1)}, f32[4,8,5120]{2,1,0:T(8,128)}, u32[]{:S(2)}) copy-start(f32[4,8,5120]{2,1,0:T(8,128)} %lat.1) | copy-start | bytes 1966084
  4.8 2.4 %collective-permute-start.1 = (bf16[1616,128]{1,0:T(8,128)(2,1)}, bf16[1616,128]{1,0:T(8,128)(2,1)S(1)}, u32[]{:S(2)}, u32[]{:S(2)}) collective-permute-start(bf16[1616,128]{1,0:T(8,128)(2,1)} %get-tuple-element.26), channel_id=1, source_target_pairs={{0,1},{1,0},{2,3},{3,2},{4,5},{5,4},{6,7},{7,6},{8,9},{9,8},{10,11... | collective-permute-start | bytes 1241096 | tf_op jit(solution)/shard_map/ppermute | solution.py:700
  4.8 20.1 %collective-permute-start.2 = (bf16[1616,128]{1,0:T(8,128)(2,1)}, bf16[1616,128]{1,0:T(8,128)(2,1)S(1)}, u32[]{:S(2)}, u32[]{:S(2)}) collective-permute-start(bf16[1616,128]{1,0:T(8,128)(2,1)} %get-tuple-element.34), channel_id=1, source_target_pairs={{0,2},{1,3},{2,0},{3,1},{4,6},{5,7},{6,4},{7,5},{8,10},{9,11},{10,... | collective-permute-start | bytes 1241096 | tf_op jit(solution)/shard_map/ppermute | solution.py:700
  5.4 21.6 %collective-permute-start = (bf16[1616,128]{1,0:T(8,128)(2,1)}, bf16[1616,128]{1,0:T(8,128)(2,1)S(1)}, u32[]{:S(2)}, u32[]{:S(2)}) collective-permute-start(bf16[1616,128]{1,0:T(8,128)(2,1)} %get-tuple-element.23), channel_id=1, source_target_pairs={{0,3},{1,2},{2,1},{3,0},{4,7},{5,6},{6,5},{7,4},{8,11},{9,10},{10,... | collective-permute-start | bytes 1241096 | tf_op jit(solution)/shard_map/ppermute | solution.py:700
  7.2 0.8 %copy-start.6 = (bf16[1616,128]{1,0:T(8,128)(2,1)}, bf16[1616,128]{1,0:T(8,128)(2,1)S(1)}, u32[]{:S(2)}) copy-start(bf16[1616,128]{1,0:T(8,128)(2,1)S(1)} %collective-permute-done.1.refs_1_) | copy-start | bytes 1241092
  8.1 37.7 %collective-permute-start.4 = (bf16[64,5120]{1,0:T(8,128)(2,1)S(1)}, bf16[64,5120]{1,0:T(8,128)(2,1)}, u32[]{:S(2)}, u32[]{:S(2)}) collective-permute-start(bf16[64,5120]{1,0:T(8,128)(2,1)S(1)} %halos.1), channel_id=1, source_target_pairs={{4,0},{8,4},{12,8},{16,12},{20,16},{24,20},{28,24},{5,1},{9,5},{13... | collective-permute-start | bytes 1966088 | tf_op jit(solution)/shard_map/ppermute | solution.py:705
  16.4 34.6 %collective-permute-start.3 = (bf16[64,5120]{1,0:T(8,128)(2,1)S(1)}, bf16[64,5120]{1,0:T(8,128)(2,1)S(1)}, u32[]{:S(2)}, u32[]{:S(2)}) collective-permute-start(bf16[64,5120]{1,0:T(8,128)(2,1)S(1)} %halos.1), channel_id=1, source_target_pairs={{0,4},{4,8},{8,12},{12,16},{16,20},{20,24},{24,28},{1,5},{5,9},{9,... | collective-permute-start | bytes 1966088 | tf_op jit(solution)/shard_map/ppermute | solution.py:704
  19.7 2.0 %copy-start = (bf16[20,1281,64]{1,2,0:T(8,128)(2,1)S(1)}, bf16[20,1281,64]{1,2,0:T(8,128)(2,1)}, u32[]{:S(2)}) copy-start(bf16[20,1281,64]{1,2,0:T(8,128)(2,1)} %param.8) | copy-start | bytes 9838084
  21.7 1.0 %copy-start.7 = (bf16[1616,128]{1,0:T(8,128)(2,1)S(1)}, bf16[1616,128]{1,0:T(8,128)(2,1)}, u32[]{:S(2)}) copy-start(bf16[1616,128]{1,0:T(8,128)(2,1)} %copy-done.6) | copy-start | bytes 1241092
  22.7 2.2 %copy-start.1 = (bf16[20,1281,64]{1,2,0:T(8,128)(2,1)S(1)}, bf16[20,1281,64]{1,2,0:T(8,128)(2,1)}, u32[]{:S(2)}) copy-start(bf16[20,1281,64]{1,2,0:T(8,128)(2,1)} %param.8) | copy-start | bytes 9838084
  29.9 25.2 %all-to-all-start = ((bf16[32,64,128]{2,1,0:T(8,128)(2,1)}), bf16[32,64,128]{2,1,0:T(8,128)(2,1)S(1)}, u32[]{:S(2)}, u32[]{:S(2)}) async-start(bf16[32,64,128]{2,1,0:T(8,128)(2,1)} %bitcast.3), calls=%async_computation | async-start | bytes 1048576 | tf_op jit(solution)/shard_map/all_to_all | solution.py:718
  50.9 4.2 %copy-start.5 = (bf16[1024,256]{1,0:T(8,128)(2,1)S(1)}, bf16[1024,256]{1,0:T(8,128)(2,1)}, u32[]{:S(2)}) copy-start(bf16[1024,256]{1,0:T(8,128)(2,1)} %constant.33.clone.table) | copy-start | bytes 1572868
  50.9 4.2 %copy-start.8 = (f32[40,256]{1,0:T(8,128)S(1)}, f32[40,256]{1,0:T(8,128)}, u32[]{:S(2)}) copy-start(f32[40,256]{1,0:T(8,128)} %constant.32.clone.twist) | copy-start | bytes 122884

commit v3 on v2

--- a/solution.py
+++ b/solution.py
@@ -321,13 +321,13 @@
         near = [w[v] + cy[t + 1, v] for v in range(chunks)]
         west = [west_of_first(near[-1], levels)] + near[:-1]
         for v in range(chunks):
-            ax[t, v] = 0.5 * (jnp.abs(u[v]) - u[v] * u[v])
-            bx[t, v] = 0.0625 * u[v] * (near[v] + west[v])
+            ax[t, v] = jnp.abs(u[v]) - u[v] * u[v]
+            bx[t, v] = 0.125 * u[v] * (near[v] + west[v])
         near = [u[v] + cx[t - 1, v] for v in range(chunks)]
         east = near[1:] + [east_of_last(near[0], levels)]
         for v in range(chunks):
-            ay[t, v] = 0.5 * (jnp.abs(w[v]) - w[v] * w[v])
-            by[t, v] = 0.0625 * w[v] * (near[v] + east[v])
+            ay[t, v] = jnp.abs(w[v]) - w[v] * w[v]
+            by[t, v] = 0.125 * w[v] * (near[v] + east[v])
         return carry
 
     lax.fori_loop(1, rows - 1, factors, 0)
@@ -480,6 +480,10 @@
     lax.fori_loop(0, chunks // group, finish, 0)
 
 
+def donor(a, b, speed):
+    return speed * jnp.where(speed > 0.0, a, b)
+
+
 def upwind_rows(t, count, old, new, cx, cy, levels):
     chunks = old.shape[1]
     west = [west_of_first(old[t + r, chunks - 1], levels) for r in range(count)]
@@ -490,12 +494,10 @@
             flux_lat, flux_lon = [], []
             for r in range(count + 1):
                 speed = cy[t + r, v]
-                flux_lat.append(jnp.maximum(speed, 0.0) * q[r] + jnp.minimum(speed, 0.0) * q[r + 1])
+                flux_lat.append(donor(q[r], q[r + 1], speed))
             for r in range(count):
                 speed = cx[t + r, v]
-                flux_lon.append(
-                    jnp.maximum(speed, 0.0) * west[r] + jnp.minimum(speed, 0.0) * q[r + 1]
-                )
+                flux_lon.append(donor(west[r], q[r + 1], speed))
             west = q[1 : count + 1]
             first = flux_lon if v == 0 else first
         else:
@@ -513,10 +515,6 @@
 
     def inverse(x):
         return pl.reciprocal(jnp.maximum(x, 1.0), approx=True)
-
-    def flux(a, b, gradient, cross, total, step):
-        speed = a * gradient - b * cross
-        return speed * total - jnp.abs(speed) * step
 
     here = [old[t - 1 + r, 0] for r in span]
     start = here
@@ -537,18 +535,16 @@
                 step = here[r + 1] - here[r]
                 gradient = step * inverse(size[r + 1] + size[r])
                 cross = (apart[r + 1] + apart[r]) * inverse(sizes_apart[r + 1] + sizes_apart[r])
-                flux_lat.append(
-                    flux(ay[t + r, v], by[t + r, v], gradient, cross, here[r + 1] + here[r], step)
-                )
+                speed = ay[t + r, v] * gradient - by[t + r, v] * cross
+                flux_lat.append(donor(here[r], here[r + 1], speed))
             total = [here[r] + west[r] for r in span]
             sizes = [size[r] + size_west[r] for r in span]
             for r in range(1, count + 1):
                 step = here[r] - west[r]
                 gradient = step * inverse(sizes[r])
                 cross = (total[r + 1] - total[r - 1]) * inverse(sizes[r + 1] + sizes[r - 1])
-                flux_lon.append(
-                    flux(ax[t + r - 1, v], bx[t + r - 1, v], gradient, cross, total[r], step)
-                )
+                speed = ax[t + r - 1, v] * gradient - bx[t + r - 1, v] * cross
+                flux_lon.append(donor(west[r], here[r], speed))
             first = flux_lon if v == 0 else first
         else:
             flux_lon = [east_of_last(x, levels) for x in first]
@@ -588,25 +584,26 @@
         def _():
             where[HALO - 1] = jnp.zeros((chunks, SUB, LANES), F32)
 
-    def one_pass(number, carry):
-        start = 2 * number + 1
+    def one_pass(number):
+        start, height = 2 * number + 1, rows // 2 - 1 - 2 * number
 
         def first(i, carry):
-            upwind_rows(start + 2 * i, 2, field, upwind, cx, cy, levels)
+            upwind_rows(start + height * i, height, field, upwind, cx, cy, levels)
             return carry
 
-        lax.fori_loop(0, rows // 2 - 1 - 2 * number, first, 0)
+        lax.fori_loop(0, 2, first, 0)
         clear(upwind)
 
         def second(i, carry):
-            corrective_rows(start + 1 + 4 * i, 4, upwind, field, ax, bx, ay, by, levels)
+            at = start + 1 + (height - 1) * i
+            corrective_rows(at, height - 1, upwind, field, ax, bx, ay, by, levels)
             return carry
 
-        lax.fori_loop(0, rows // 4 - 1 - number, second, 0)
+        lax.fori_loop(0, 2, second, 0)
         clear(field)
-        return carry
-
-    lax.fori_loop(0, PASSES, one_pass, 0)
+
+    for number in range(PASSES):
+        one_pass(number)
     span = nlon * levels // SUB
     for block in range(band // SUB):
         first = HALO + block * SUB
@@ -709,11 +706,9 @@
     )
     turned = jnp.swapaxes(legendre, 1, 2)
     given = (turned, own_pairs, wave_count, waves, pad)
-    sums = list(legendre_sums(range(half), blocks[:half], *given))
+    sums = list(legendre_sums(range(level_count - 1), blocks[:-1], *given))
     order = order_matrix(wave_table, wave_count * level_count, pad)
     sums, order, own_winds = lax.optimization_barrier((sums, order, own_winds))
-    for step in range(half, level_count - 1):
-        sums += legendre_sums([step], blocks[step : step + 1], *given)
     stacked = legendre_sums([level_count - 1], blocks[-1:], *given, done=tuple(sums))
     arrived = lax.all_to_all(
         stacked.reshape(-1, SUB * SUB, LANES), ("wave", "lev"), 0, 0, tiled=True

time: 77.9 us -> 72.9 us (0.936)
  Pallas kernels: 48.1 us -> 42.9 us
  local copies, waits for them, and re-layouts: 5.81 us -> 4.01 us
  starting transfers between devices: 13.4 us -> 14.6 us
  waiting for transfers between devices: 7.47 us -> 8.31 us
    pallas_call x1, Pallas kernels: 22.4 us -> 18.9 us  [advect(): pl.pallas_call(functools.partial(advect_kernel, pad), out_shape=jax.Shape...]
    unnamed x20 -> x16, local copies, waits for them, and re-layouts: 5.32 us -> 3.53 us
    ppermute x3, waiting for transfers between devices: 0.01 us -> 1.2 us  [body(): blocks[step] = lax.ppermute(blocks[step], 'lev', pairs)]
    all_to_all x1, starting transfers between devices: 4.93 us -> 6.03 us  [body(): lax.all_to_all(stacked.reshape(-1, SUB * SUB, LANES), ('wave', 'lev'), 0,...]
    pallas_call x3 -> x2, Pallas kernels: 7.11 us -> 6.16 us  [legendre_sums(): pl.pallas_call(functools.partial(legendre_kernel, steps, bands, waves, pa...]
    pallas_call x2, Pallas kernels: 3.35 us -> 2.56 us  [pack(): pl.pallas_call(functools.partial(pack_kernel, count, steps), out_shape=[o...]
  transfers between devices with their start and end apart: 6 -> 6, of which waited for: 1 -> 2; matrix products, arithmetic and copies ran while one was open for 4% -> 4% of each run, Pallas kernels for 29% -> 30%
where the time goes in v3:
time: 72.9 us; the launch traced here: 72.5 us
  Pallas kernels  42.9 us (59%)
  starting transfers between devices  14.6 us (20%)
  waiting for transfers between devices  8.31 us (11%)
  local copies, waits for them, and re-layouts  4.01 us (6%)
  other arithmetic  2.46 us (3%)
    pallas_call x1, Pallas kernels, advect(): pl.pallas_call(functools.partial(advect_kernel, pad), out_shape=jax.Shape...  18.9 us
    pallas_call x3, Pallas kernels, factor_rows(): pl.pallas_call(functools.partial(factor_kernel, levels, side), out_shape=...  12.7 us
    ppermute x1, waiting for transfers between devices, body(): above = lax.ppermute(lower, 'wave', down)  7.11 us
    pallas_call x2, Pallas kernels, legendre_sums(): pl.pallas_call(functools.partial(legendre_kernel, steps, bands, waves, pa...  6.16 us
    all_to_all x1, starting transfers between devices, body(): lax.all_to_all(stacked.reshape(-1, SUB * SUB, LANES), ('wave', 'lev'), 0,...  6.03 us
    unnamed x16, local copies, waits for them, and re-layouts  3.53 us
    ppermute x1, starting transfers between devices, body(): below = lax.ppermute(upper, 'wave', up)  3.33 us
    ppermute x1, starting transfers between devices, body(): above = lax.ppermute(lower, 'wave', down)  3.31 us
  transfers between devices with their start and end apart: 6, of which 2 were waited for; matrix products, arithmetic and copies ran while one was open for 4% of the time, Pallas kernels for 30%

profile of v3, /device:TPU:26, one launch (start us, length us, event | category | flops | bytes accessed | tf_op | source)
XLA Modules:
  0.0 72.5 jit_solution(8515944630549190059)
XLA Ops:
  0.0 0.0 copy-start.2
  0.0 1.5 %copy-done.2 = bf16[2,4,80,1281]{3,2,1,0:T(8,128)(2,1)S(1)} copy-done((bf16[2,4,80,1281]{3,2,1,0:T(8,128)(2,1)S(1)}, bf16[2,4,80,1281]{3,2,1,0:T(8,128)(2,1)}, u32[]{:S(2)}) %copy-start.2) | copy-done | bytes 1639704
  1.5 0.0 copy-start.7
  1.5 0.0 copy-start.3
  1.5 0.0 copy-start.4
  1.5 1.7 %pack.2 = (bf16[1616,128]{1,0:T(8,128)(2,1)}, bf16[1616,128]{1,0:T(8,128)(2,1)}) custom-call(bf16[8,80,1281]{2,1,0:T(8,128)(2,1)S(1)} %bitcast.9), custom_call_target="tpu_custom_call" | custom-call | tf_op jit(solution)/shard_map/pack/pallas_call | solution.py:80
  3.2 0.9 %pack.3 = (bf16[1616,128]{1,0:T(8,128)(2,1)S(1)}, bf16[1616,128]{1,0:T(8,128)(2,1)S(1)}) custom-call(bf16[8,80,1281]{2,1,0:T(8,128)(2,1)S(1)} %bitcast.10), custom_call_target="tpu_custom_call" | custom-call | tf_op jit(solution)/shard_map/pack/pallas_call | solution.py:80
  4.1 0.1 collective-permute-start.1
  4.1 0.6 collective-permute-start.2
  4.7 1.3 %collective-permute-start = (bf16[1616,128]{1,0:T(8,128)(2,1)}, bf16[1616,128]{1,0:T(8,128)(2,1)S(1)}, u32[]{:S(2)}, u32[]{:S(2)}) collective-permute-start(bf16[1616,128]{1,0:T(8,128)(2,1)} %get-tuple-element.25), channel_id=1, source_target_pairs={{0,3},{1,2},{2,1},{3,0},{4,7},{5,6},{6,5},{7,4},{8,11},{9,10},{10,... | collective-permute-start | bytes 1241096 | tf_op jit(solution)/shard_map/ppermute | solution.py:697
  6.0 0.0 copy-done.7
  6.0 0.2 copy.8
  6.2 0.1 reshape.26
  6.4 0.1 reshape.27
  6.5 0.0 collective-permute-done.1.refs_1_
  6.5 0.0 copy-done.3
  6.5 0.0 copy-done.4
  6.5 0.1 halos.1
  6.6 3.3 %collective-permute-start.4 = (bf16[64,5120]{1,0:T(8,128)(2,1)S(1)}, bf16[64,5120]{1,0:T(8,128)(2,1)}, u32[]{:S(2)}, u32[]{:S(2)}) collective-permute-start(bf16[64,5120]{1,0:T(8,128)(2,1)S(1)} %halos.1), channel_id=1, source_target_pairs={{4,0},{8,4},{12,8},{16,12},{20,16},{24,20},{28,24},{5,1},{9,5},{13... | collective-permute-start | bytes 1966088 | tf_op jit(solution)/shard_map/ppermute | solution.py:702
  9.9 2.4 %fusion.far_order = bf16[1408,1280]{1,0:T(8,128)(2,1)} fusion(s32[1408]{0:T(1024)S(1)} %pad_bitcast_fusion, bf16[1408]{0:T(1024)(128)(2,1)S(1)} %select_convert_fusion), kind=kLoop, calls=%fused_computation.1 | loop fusion | flops 3604480 | bytes 3612928 | tf_op jit(solution)/shard_map/jit(_where)/select_n | solution.py:677
  12.4 0.1 dynamic_slice.3.pairs_ref
  12.4 2.4 %own_courant.1.own = f32[2,8,20,8,128]{4,3,2,1,0:T(8,128)} custom-call(f32[4,8,5120]{2,1,0:T(8,128)S(1)} %copy-done.3, f32[4,8,5120]{2,1,0:T(8,128)S(1)} %copy-done.4), custom_call_target="tpu_custom_call" | custom-call | tf_op jit(solution)/shard_map/own_courant/pallas_call | solution.py:264
  14.9 3.3 %collective-permute-start.3 = (bf16[64,5120]{1,0:T(8,128)(2,1)S(1)}, bf16[64,5120]{1,0:T(8,128)(2,1)S(1)}, u32[]{:S(2)}, u32[]{:S(2)}) collective-permute-start(bf16[64,5120]{1,0:T(8,128)(2,1)S(1)} %halos.1), channel_id=1, source_target_pairs={{0,4},{4,8},{8,12},{12,16},{16,20},{20,24},{24,28},{1,5},{5,9},{9,... | collective-permute-start | bytes 1966088 | tf_op jit(solution)/shard_map/ppermute | solution.py:701
  18.2 0.0 collective-permute-done.2.refs_2_
  18.2 0.0 copy-start
  18.2 2.0 %copy-done = bf16[20,1281,64]{1,2,0:T(8,128)(2,1)S(1)} copy-done((bf16[20,1281,64]{1,2,0:T(8,128)(2,1)S(1)}, bf16[20,1281,64]{1,2,0:T(8,128)(2,1)}, u32[]{:S(2)}) %copy-start) | copy-done | bytes 3279384
  20.3 0.0 copy-start.1
  20.3 3.3 %legendre.2 = (bf16[8,64,128]{2,1,0:T(8,128)(2,1)S(1)}, bf16[8,64,128]{2,1,0:T(8,128)(2,1)S(1)}, bf16[8,64,128]{2,1,0:T(8,128)(2,1)S(1)}) custom-call(s32[20]{0:T(128)S(1)} %dynamic_slice.3.pairs_ref, bf16[1616,128]{1,0:T(8,128)(2,1)S(1)} %get-tuple-element.27.refs_0_, bf16[1616,128]{1,0:T(8,128)(2,1)S(1)} %collective-permute-done.1.refs_1_, ...), custom_call_target="tpu_custom_call" | custom-call | tf_op jit(solution)/shard_map/legendre/pallas_call | solution.py:175
  23.5 1.2 %collective-permute-done.refs_0_ = bf16[1616,128]{1,0:T(8,128)(2,1)S(1)} collective-permute-done((bf16[1616,128]{1,0:T(8,128)(2,1)}, bf16[1616,128]{1,0:T(8,128)(2,1)S(1)}, u32[]{:S(2)}, u32[]{:S(2)}) %collective-permute-start) | collective-permute-done | bytes 413728 | tf_op jit(solution)/shard_map/ppermute | solution.py:697
  24.7 0.0 copy-done.1
  24.7 2.9 %legendre.3 = bf16[8,4,64,128]{3,2,1,0:T(8,128)(2,1)} custom-call(s32[20]{0:T(128)S(1)} %dynamic_slice.3.pairs_ref, bf16[1616,128]{1,0:T(8,128)(2,1)S(1)} %collective-permute-done.refs_0_, bf16[20,64,1281]{2,1,0:T(8,128)(2,1)S(1)} %bitcast.8, bf16[8,64,128]{2,1,0:T(8,128)(2,1)S(1)} %get-tuple-element.36.refs_2_, ...), custom_call_target="tpu_custom_call" | custom-call | tf_op jit(solution)/shard_map/legendre/pallas_call | solution.py:175
  27.6 6.0 %all-to-all-start = ((bf16[32,64,128]{2,1,0:T(8,128)(2,1)}), bf16[32,64,128]{2,1,0:T(8,128)(2,1)S(1)}, u32[]{:S(2)}, u32[]{:S(2)}) async-start(bf16[32,64,128]{2,1,0:T(8,128)(2,1)} %bitcast.3), calls=%async_computation | async-start | bytes 1048576 | tf_op jit(solution)/shard_map/all_to_all | solution.py:713
  33.7 3.5 %factors.4.refs_1_ = f32[6,6,20,8,128]{4,3,2,1,0:T(8,128)} custom-call(f32[2,8,20,8,128]{4,3,2,1,0:T(8,128)} %own_courant.1.own), custom_call_target="tpu_custom_call" | custom-call | flops 1000000000 | bytes 8000000 | tf_op jit(solution)/shard_map/factors/pallas_call | solution.py:345
  37.1 7.1 %collective-permute-done.4.refs_0_ = bf16[64,5120]{1,0:T(8,128)(2,1)} collective-permute-done((bf16[64,5120]{1,0:T(8,128)(2,1)S(1)}, bf16[64,5120]{1,0:T(8,128)(2,1)}, u32[]{:S(2)}, u32[]{:S(2)}) %collective-permute-start.4) | collective-permute-done | bytes 655392 | tf_op jit(solution)/shard_map/ppermute | solution.py:702
  44.2 5.1 %factors.5.refs_2_ = f32[6,9,20,8,128]{4,3,2,1,0:T(8,128)} custom-call(f32[2,8,20,8,128]{4,3,2,1,0:T(8,128)} %own_courant.1.own, bf16[64,5120]{1,0:T(8,128)(2,1)} %collective-permute-done.4.refs_0_), custom_call_target="tpu_custom_call" | custom-call | flops 30000001024 | bytes 8000000 | tf_op jit(solution)/shard_map/factors/pallas_call | solution.py:345
  49.4 0.0 copy-start.5
  49.4 0.0 copy-start.6
  49.4 0.0 collective-permute-done.3.refs_0_
  49.4 4.1 %factors.3.refs_0_ = f32[6,9,20,8,128]{4,3,2,1,0:T(8,128)} custom-call(f32[2,8,20,8,128]{4,3,2,1,0:T(8,128)} %own_courant.1.own, bf16[64,5120]{1,0:T(8,128)(2,1)S(1)} %collective-permute-done.3.refs_0_), custom_call_target="tpu_custom_call" | custom-call | flops 1000000000 | bytes 8000000 | tf_op jit(solution)/shard_map/factors/pallas_call | solution.py:345
  53.6 0.0 all-to-all-done.arrived
  53.6 0.0 copy-done.5
  53.6 0.0 copy-done.6
  53.6 18.9 %advect.1 = f32[4,8,5120]{2,1,0:T(8,128)} custom-call(bf16[32,64,128]{2,1,0:T(8,128)(2,1)S(1)} %all-to-all-done.arrived, bf16[1408,1280]{1,0:T(8,128)(2,1)} %fusion.far_order, f32[40,256]{1,0:T(8,128)S(1)} %copy-done.6, bf16[1024,256]{1,0:T(8,128)(2,1)S(1)} %copy-done.5, f32[6,9,20,8,128]{4,3,2,1,0:T(8,128)} %factors.3.refs_0_, ...), custom_call_target="tpu_custom_call" | custom-call | tf_op jit(solution)/shard_map/advect/pallas_call | solution.py:636
  (7 shorter events, 0.0 us)
Async XLA Ops:
  0.0 1.5 %copy-start.2 = (bf16[2,4,80,1281]{3,2,1,0:T(8,128)(2,1)S(1)}, bf16[2,4,80,1281]{3,2,1,0:T(8,128)(2,1)}, u32[]{:S(2)}) copy-start(bf16[2,4,80,1281]{3,2,1,0:T(8,128)(2,1)} %param.7) | copy-start | bytes 4919044
  1.5 4.5 %copy-start.7 = (s32[640]{0:T(1024)S(1)}, s32[640]{0:T(1024)}, u32[]{:S(2)}) copy-start(s32[640]{0:T(1024)} %param.9) | copy-start | bytes 7684
  1.5 5.0 %copy-start.3 = (f32[4,8,5120]{2,1,0:T(8,128)S(1)}, f32[4,8,5120]{2,1,0:T(8,128)}, u32[]{:S(2)}) copy-start(f32[4,8,5120]{2,1,0:T(8,128)} %lon.1) | copy-start | bytes 1966084
  1.5 5.0 %copy-start.4 = (f32[4,8,5120]{2,1,0:T(8,128)S(1)}, f32[4,8,5120]{2,1,0:T(8,128)}, u32[]{:S(2)}) copy-start(f32[4,8,5120]{2,1,0:T(8,128)} %lat.1) | copy-start | bytes 1966084
  4.1 2.4 %collective-permute-start.1 = (bf16[1616,128]{1,0:T(8,128)(2,1)S(1)}, bf16[1616,128]{1,0:T(8,128)(2,1)S(1)}, u32[]{:S(2)}, u32[]{:S(2)}) collective-permute-start(bf16[1616,128]{1,0:T(8,128)(2,1)S(1)} %get-tuple-element.28), channel_id=1, source_target_pairs={{0,1},{1,0},{2,3},{3,2},{4,5},{5,4},{6,7},{7,6},{8,9},{9,8},{10,11... | collective-permute-start | bytes 1241096 | tf_op jit(solution)/shard_map/ppermute | solution.py:697
  4.1 14.1 %collective-permute-start.2 = (bf16[1616,128]{1,0:T(8,128)(2,1)}, bf16[1616,128]{1,0:T(8,128)(2,1)}, u32[]{:S(2)}, u32[]{:S(2)}) collective-permute-start(bf16[1616,128]{1,0:T(8,128)(2,1)} %get-tuple-element.30), channel_id=1, source_target_pairs={{0,2},{1,3},{2,0},{3,1},{4,6},{5,7},{6,4},{7,5},{8,10},{9,11},{10,... | collective-permute-start | bytes 1241096 | tf_op jit(solution)/shard_map/ppermute | solution.py:697
  4.7 20.0 %collective-permute-start = (bf16[1616,128]{1,0:T(8,128)(2,1)}, bf16[1616,128]{1,0:T(8,128)(2,1)S(1)}, u32[]{:S(2)}, u32[]{:S(2)}) collective-permute-start(bf16[1616,128]{1,0:T(8,128)(2,1)} %get-tuple-element.25), channel_id=1, source_target_pairs={{0,3},{1,2},{2,1},{3,0},{4,7},{5,6},{6,5},{7,4},{8,11},{9,10},{10,... | collective-permute-start | bytes 1241096 | tf_op jit(solution)/shard_map/ppermute | solution.py:697
  6.6 37.7 %collective-permute-start.4 = (bf16[64,5120]{1,0:T(8,128)(2,1)S(1)}, bf16[64,5120]{1,0:T(8,128)(2,1)}, u32[]{:S(2)}, u32[]{:S(2)}) collective-permute-start(bf16[64,5120]{1,0:T(8,128)(2,1)S(1)} %halos.1), channel_id=1, source_target_pairs={{4,0},{8,4},{12,8},{16,12},{20,16},{24,20},{28,24},{5,1},{9,5},{13... | collective-permute-start | bytes 1966088 | tf_op jit(solution)/shard_map/ppermute | solution.py:702
  14.9 34.5 %collective-permute-start.3 = (bf16[64,5120]{1,0:T(8,128)(2,1)S(1)}, bf16[64,5120]{1,0:T(8,128)(2,1)S(1)}, u32[]{:S(2)}, u32[]{:S(2)}) collective-permute-start(bf16[64,5120]{1,0:T(8,128)(2,1)S(1)} %halos.1), channel_id=1, source_target_pairs={{0,4},{4,8},{8,12},{12,16},{16,20},{20,24},{24,28},{1,5},{5,9},{9,... | collective-permute-start | bytes 1966088 | tf_op jit(solution)/shard_map/ppermute | solution.py:701
  18.2 2.0 %copy-start = (bf16[20,1281,64]{1,2,0:T(8,128)(2,1)S(1)}, bf16[20,1281,64]{1,2,0:T(8,128)(2,1)}, u32[]{:S(2)}) copy-start(bf16[20,1281,64]{1,2,0:T(8,128)(2,1)} %param.8) | copy-start | bytes 9838084
  20.3 4.5 %copy-start.1 = (bf16[20,1281,64]{1,2,0:T(8,128)(2,1)S(1)}, bf16[20,1281,64]{1,2,0:T(8,128)(2,1)}, u32[]{:S(2)}) copy-start(bf16[20,1281,64]{1,2,0:T(8,128)(2,1)} %param.8) | copy-start | bytes 9838084
  27.6 25.9 %all-to-all-start = ((bf16[32,64,128]{2,1,0:T(8,128)(2,1)}), bf16[32,64,128]{2,1,0:T(8,128)(2,1)S(1)}, u32[]{:S(2)}, u32[]{:S(2)}) async-start(bf16[32,64,128]{2,1,0:T(8,128)(2,1)} %bitcast.3), calls=%async_computation | async-start | bytes 1048576 | tf_op jit(solution)/shard_map/all_to_all | solution.py:713
  49.4 4.2 %copy-start.5 = (bf16[1024,256]{1,0:T(8,128)(2,1)S(1)}, bf16[1024,256]{1,0:T(8,128)(2,1)}, u32[]{:S(2)}) copy-start(bf16[1024,256]{1,0:T(8,128)(2,1)} %constant.33.clone.table) | copy-start | bytes 1572868
  49.4 4.2 %copy-start.6 = (f32[40,256]{1,0:T(8,128)S(1)}, f32[40,256]{1,0:T(8,128)}, u32[]{:S(2)}) copy-start(f32[40,256]{1,0:T(8,128)} %constant.32.clone.twist) | copy-start | bytes 122884

commit v4 on v3

--- a/solution.py
+++ b/solution.py
@@ -192,28 +192,6 @@
     return jnp.where(lane_index() == LANES - 1, pltpu.roll(turned, SUB - levels, 0), turned)
 
 
-def halo_kernel(lon, lat, *refs):
-    levels, band = lon.shape[:2]
-    for halo, start in zip(refs, (0, band - HALO)):
-        for field, wind in enumerate((lon, lat)):
-            for level in range(0, levels, 2):
-                both = [wind[level + k, start : start + HALO, :] for k in range(2)]
-                row = (field * levels + level) * HALO
-                halo[row : row + 2 * HALO, :] = jnp.concatenate(both, 0).astype(BF16)
-
-
-def halos(lon, lat):
-    levels, band, nlon = lon.shape
-    halo = jax.ShapeDtypeStruct((2 * levels * HALO, nlon), BF16)
-    made = pl.pallas_call(
-        halo_kernel,
-        out_shape=[halo] * (1 if band == HALO else 2),
-        compiler_params=params(12),
-        name="halos",
-    )(lon, lat)
-    return made[0], made[-1]
-
-
 def turn(tiles_of, rows, start, turned):
     chunks = rows.shape[2]
 
@@ -239,81 +217,9 @@
     return pl.ds(pl.multiple_of(part * span + n * LANES, LANES), LANES)
 
 
-def own_courant_kernel(lon, lat, own, rows, turned, sem):
-    levels, band, _ = lon.shape
-    for start in range(0, band, SUB):
-
-        def tiles_of(n, start=start):
-            return [
-                wind[level, start : start + SUB, lanes_of(part, n, turned.shape[0])]
-                for wind in (lon, lat)
-                for part in range(SUB // levels)
-                for level in range(levels)
-            ]
-
-        turn(tiles_of, rows, start, turned)
-    copy = pltpu.make_async_copy(rows, own, sem)
-    copy.start()
-    copy.wait()
-
-
-def own_courant(lon, lat):
-    levels, band, nlon = lon.shape
-    parts = SUB // levels
-    shape = (2, band, nlon // (parts * LANES), SUB, LANES)
-    return pl.pallas_call(
-        own_courant_kernel,
-        out_shape=pltpu.HBM(shape, F32),
-        out_specs=pl.BlockSpec(memory_space=pltpu.HBM),
-        scratch_shapes=[
-            pltpu.VMEM(shape, F32),
-            pltpu.VMEM((nlon // parts, LANES), F32),
-            pltpu.SemaphoreType.DMA,
-        ],
-        compiler_params=params(16),
-        name="own_courant",
-    )(lon, lat)
-
-
-def factor_kernel(levels, side, own, *refs):
-    far_out, fields, sems = refs[1:4] if side else refs
+def add_factors(fields, levels, start, stop):
     cx, cy, ax, bx, ay, by = [fields.at[i] for i in range(6)]
-    rows, chunks = fields.shape[1:3]
-    band = own.shape[1]
-    if side:
-        start, at = (0, HALO) if side < 0 else (band - 2, 0)
-        source, target = own.at[:, pl.ds(start, 2)], fields.at[pl.ds(0, 2), pl.ds(at, 2)]
-    else:
-        source, target = own, fields.at[pl.ds(0, 2)]
-    copy = pltpu.make_async_copy(source, target, sems.at[0])
-    copy.start()
-    if side:
-        received, turned = refs[0], refs[-1]
-
-        def tiles_of(n):
-            height = levels * SUB
-            return [
-                received[wind * height : (wind + 1) * height, lanes_of(part, n, turned.shape[0])].astype(F32)
-                for wind in range(2)
-                for part in range(SUB // levels)
-            ]
-
-        turn(tiles_of, fields, 0 if side < 0 else 2, turned)
-    copy.wait()
-    low = 0 if side < 0 else 1
-    height = far_out.shape[1]
-    copies = [
-        pltpu.make_async_copy(
-            fields.at[pl.ds(i, count), pl.ds(low, height)],
-            far_out.at[pl.ds(i, count)],
-            sems.at[1 + k],
-        )
-        for k, (i, count) in enumerate(((0, 2), (2, 4)))
-    ]
-    copies[0].start()
-    if side:
-        for i in range(2, 6):
-            fields[i, 0 if side < 0 else rows - 1] = jnp.zeros((chunks, SUB, LANES), F32)
+    chunks = fields.shape[2]
 
     def factors(t, carry):
         u = [cx[t, v] for v in range(chunks)]
@@ -330,36 +236,153 @@
             by[t, v] = 0.125 * w[v] * (near[v] + east[v])
         return carry
 
-    lax.fori_loop(1, rows - 1, factors, 0)
+    lax.fori_loop(start, stop, factors, 0)
+
+
+def own_courant_kernel(lon, lat, own, upper, lower, rows, turned, sem):
+    levels, band, _ = lon.shape
+    chunks = rows.shape[2]
+    for start in range(0, band, SUB):
+
+        def tiles_of(n, start=start):
+            return [
+                wind[level, start : start + SUB, lanes_of(part, n, turned.shape[0])]
+                for wind in (lon, lat)
+                for part in range(SUB // levels)
+                for level in range(levels)
+            ]
+
+        turn(tiles_of, rows, start, turned)
+    copy = pltpu.make_async_copy(rows, own, sem)
+    copy.start()
+    for out, start in ((upper, band - HALO + 1), (lower, 0)):
+        for i in range(out.shape[0]):
+            wind, t = halo_row(i)
+            for v in range(0, chunks, 2):
+                both = jnp.concatenate([rows[wind, start + t, v], rows[wind, start + t, v + 1]], 0)
+                out[i, v * SUB : (v + 2) * SUB, :] = both.astype(BF16)
+    copy.wait()
+
+
+def halo_row(i):
+    return divmod(i, HALO - 1) if i < 2 * HALO - 2 else (1, HALO - 1)
+
+
+def own_courant(lon, lat):
+    levels, band, nlon = lon.shape
+    parts = SUB // levels
+    chunks = nlon // (parts * LANES)
+    shape = (2, band, chunks, SUB, LANES)
+    far, vmem = pl.BlockSpec(memory_space=pltpu.HBM), pl.BlockSpec(memory_space=pltpu.VMEM)
+    return pl.pallas_call(
+        own_courant_kernel,
+        out_shape=[
+            pltpu.HBM(shape, F32),
+            jax.ShapeDtypeStruct((2 * HALO - 2, chunks * SUB, LANES), BF16),
+            jax.ShapeDtypeStruct((2 * HALO - 1, chunks * SUB, LANES), BF16),
+        ],
+        out_specs=[far, vmem, vmem],
+        scratch_shapes=[
+            pltpu.VMEM(shape, F32),
+            pltpu.VMEM((chunks * LANES, LANES), F32),
+            pltpu.SemaphoreType.DMA,
+        ],
+        compiler_params=params(16),
+        name="own_courant",
+    )(lon, lat)
+
+
+def inner_kernel(levels, own, far_out, fields, sems):
+    rows = fields.shape[1]
+    copy = pltpu.make_async_copy(own, fields.at[pl.ds(0, 2)], sems.at[0])
+    copy.start()
+    copy.wait()
+    add_factors(fields, levels, 1, rows - 1)
+    copy = pltpu.make_async_copy(fields.at[:, pl.ds(1, rows - 2)], far_out, sems.at[1])
+    copy.start()
+    copy.wait()
+
+
+def inner_fields(own, levels):
+    _, band, chunks, _, _ = own.shape
+    far = pl.BlockSpec(memory_space=pltpu.HBM)
+    return pl.pallas_call(
+        functools.partial(inner_kernel, levels),
+        out_shape=pltpu.HBM((6, band - 2, chunks, SUB, LANES), F32),
+        in_specs=[far],
+        out_specs=far,
+        scratch_shapes=[
+            pltpu.VMEM((6, band, chunks, SUB, LANES), F32),
+            pltpu.SemaphoreType.DMA((2,)),
+        ],
+        compiler_params=params(16),
+        name="inner",
+    )(pltpu.with_memory_space_constraint(own, pltpu.HBM))
+
+
+def edge_kernel(levels, side, own, received, far_out, fields, sems):
+    rows, chunks = fields.shape[1:3]
+    band = own.shape[1]
+    copy = pltpu.make_async_copy(
+        own.at[:, pl.ds((band - 2) * side, 2)],
+        fields.at[pl.ds(0, 2), pl.ds(0 if side else HALO, 2)],
+        sems.at[0],
+    )
+    copy.start()
+    for i in range(side, 6):
+        fields[i, rows - 1 if side else 0] = jnp.zeros(fields.shape[2:], F32)
+    if side:
+        fields[0, rows - 1] = jnp.zeros(fields.shape[2:], F32)
+    for i in range(received.shape[0]):
+        wind, t = halo_row(i)
+        for v in range(0, chunks, 2):
+            both = received[i, v * SUB : (v + 2) * SUB, :].astype(F32)
+            fields[wind, 1 + side + t, v] = both[:SUB]
+            fields[wind, 1 + side + t, v + 1] = both[SUB:]
+    copy.wait()
+    middle = rows // 2
+    spans = [
+        (0, 2, side, HALO + 1),
+        (2, 4, side, middle - side),
+        (2, 4, middle, HALO + 1 + side - middle),
+    ]
+    copies = [
+        pltpu.make_async_copy(
+            fields.at[pl.ds(first, count), pl.ds(t, height)],
+            far_out.at[pl.ds(first, count), pl.ds(t - side, height)],
+            sems.at[1 + i],
+        )
+        for i, (first, count, t, height) in enumerate(spans)
+    ]
+    copies[0].start()
+    add_factors(fields, levels, 1, middle)
     copies[1].start()
+    add_factors(fields, levels, middle, rows - 1)
+    copies[2].start()
     for copy in copies:
         copy.wait()
 
 
-def factor_rows(own, received, side, levels):
-    _, band, chunks, _, _ = own.shape
-    rows = HALO + 2 if side else band
-    out = HALO + 1 if side else band - 2
+def edge_fields(own, received, side, levels):
+    chunks = own.shape[2]
     vmem, far = pl.BlockSpec(memory_space=pltpu.VMEM), pl.BlockSpec(memory_space=pltpu.HBM)
-    extra = (received,) if side else ()
     return pl.pallas_call(
-        functools.partial(factor_kernel, levels, side),
-        out_shape=pltpu.HBM((6, out, chunks, SUB, LANES), F32),
-        in_specs=[far] + [vmem] * len(extra),
+        functools.partial(edge_kernel, levels, side),
+        out_shape=pltpu.HBM((6, HALO + 1, chunks, SUB, LANES), F32),
+        in_specs=[far, vmem],
         out_specs=far,
         scratch_shapes=[
-            pltpu.VMEM((6, rows, chunks, SUB, LANES), F32),
-            pltpu.SemaphoreType.DMA((3,)),
-        ]
-        + [pltpu.VMEM((chunks * LANES, LANES), F32)] * len(extra),
+            pltpu.VMEM((6, HALO + 2, chunks, SUB, LANES), F32),
+            pltpu.SemaphoreType.DMA((4,)),
+        ],
         compiler_params=params(16),
         cost_estimate=pl.CostEstimate(
-            flops=30_000_000_000 if side > 0 else 1_000_000_000,
+            flops=6_000_000_000 if side else 1_000_000_000,
             bytes_accessed=8_000_000,
             transcendentals=0,
         ),
-        name="factors",
-    )(pltpu.with_memory_space_constraint(own, pltpu.HBM), *extra)
+        name="edge",
+    )(pltpu.with_memory_space_constraint(own, pltpu.HBM), received)
 
 
 def spread(real, imag, count):
@@ -404,7 +427,7 @@
 
 
 def transform(
-    arrived, order, order_copy, twist, table, lhs, mixed, terms, field, pad, levels
+    arrived, numbers, order, twist, table, lhs, mixed, terms, field, pad, levels
 ):
     sources = arrived.shape[0]
     rows, chunks = field.shape[:2]
@@ -429,7 +452,17 @@
     half = pieces * height
     near = table.shape[1]
     depth = mixed.shape[0]
-    order_copy.wait()
+    column = lax.broadcasted_iota(jnp.int32, (2 * SUB, LANES), 1)
+
+    def one_hot(i, carry):
+        span = pl.ds(pl.multiple_of(i * 2 * SUB, 2 * SUB), 2 * SUB)
+        number = jnp.broadcast_to(numbers[span, :], (2 * SUB, LANES))
+        weight = jnp.where(number == 0, 1.0, 2.0)
+        for lo in range(0, order.shape[1], LANES):
+            order[span, lo : lo + LANES] = jnp.where(column + lo == number, weight, 0.0).astype(BF16)
+        return carry
+
+    lax.fori_loop(0, order.shape[0] // (2 * SUB), one_hot, 0, unroll=4)
     for m in range(depth):
         mixed[m] = jnp.dot(
             lhs[...], order[:, m * near : (m + 1) * near], preferred_element_type=F32
@@ -558,24 +591,22 @@
             west, here, size_west, size = here, east, size, size_east
 
 
-def advect_kernel(pad, arrived, far_order, twist, table, *refs):
+def advect_kernel(pad, arrived, numbers, twist, table, *refs):
     far_fields = refs[:3]
     out, fields, order, lhs, mixed, terms, field, upwind, turned, sems = refs[3:]
     cx, cy, ax, bx, ay, by = [fields.at[i] for i in range(6)]
     levels, band, nlon = out.shape
     rows, chunks = field.shape[:2]
-    copies = [pltpu.make_async_copy(far_order, order, sems.at[0])]
+    copies = []
     start = 0
     for i, far in enumerate(far_fields):
         place = fields.at[:, pl.ds(start, far.shape[1])]
-        copies.append(pltpu.make_async_copy(far, place, sems.at[1 + i]))
+        copies.append(pltpu.make_async_copy(far, place, sems.at[i]))
         start += far.shape[1]
     for copy in copies:
         copy.start()
-    transform(
-        arrived, order, copies[0], twist, table, lhs, mixed, terms, field, pad, levels
-    )
-    for copy in copies[1:]:
+    transform(arrived, numbers, order, twist, table, lhs, mixed, terms, field, pad, levels)
+    for copy in copies:
         copy.wait()
     outermost = lax.axis_index("wave") == 0
 
@@ -624,33 +655,32 @@
                 ]
 
 
-def advect(arrived, order, twist, table, fields, shape, pad):
+def advect(arrived, numbers, twist, table, fields, waves, shape, pad):
     levels, band, nlon = shape
     rows, chunks = sum(x.shape[1] for x in fields), fields[0].shape[2]
     half = rows * levels
     near = table.shape[1]
-    order, *fields = [
-        pltpu.with_memory_space_constraint(x, pltpu.HBM) for x in (order, *fields)
-    ]
+    fields = [pltpu.with_memory_space_constraint(x, pltpu.HBM) for x in fields]
+    order = (numbers.shape[0], waves)
     vmem, far = pl.BlockSpec(memory_space=pltpu.VMEM), pl.BlockSpec(memory_space=pltpu.HBM)
     return pl.pallas_call(
         functools.partial(advect_kernel, pad),
         out_shape=jax.ShapeDtypeStruct(shape, F32),
-        in_specs=[vmem, far, vmem, vmem] + [far] * 3,
+        in_specs=[vmem] * 4 + [far] * 3,
         scratch_shapes=[
             pltpu.VMEM((6, rows, chunks, SUB, LANES), F32),
-            pltpu.VMEM(order.shape, BF16),
-            pltpu.VMEM((2 * half, order.shape[0]), BF16),
-            pltpu.VMEM((order.shape[1] // near, 2 * half, near), F32),
+            pltpu.VMEM(order, BF16),
+            pltpu.VMEM((2 * half, order[0]), BF16),
+            pltpu.VMEM((waves // near, 2 * half, near), F32),
             pltpu.VMEM((chunks, half, 4 * near), BF16),
             pltpu.VMEM((rows, chunks, SUB, LANES), F32),
             pltpu.VMEM((rows, chunks, SUB, LANES), F32),
             pltpu.VMEM((nlon * levels // SUB, LANES), F32),
-            pltpu.SemaphoreType.DMA((4,)),
+            pltpu.SemaphoreType.DMA((3,)),
         ],
         compiler_params=params(40),
         name="advect",
-    )(arrived, order, twist, table, *fields)
+    )(arrived, numbers, twist, table, *fields)
 
 
 def fourier_tables(nlon, near):
@@ -665,16 +695,16 @@
     return twist.astype(np.float32), np.concatenate([high, low], 0)
 
 
-def order_matrix(wave_table, sources, pad):
+def arrival(wave_table, sources, pad):
     waves = 2 * wave_table.shape[0]
     group = LANES // pad
     numbers = jnp.stack([wave_table, waves - 1 - wave_table], 1).reshape(sources, -1)
     extra = -sources % group
     column = jnp.pad(numbers, ((0, extra), (0, pad - numbers.shape[1])), constant_values=-1)
     column = column.reshape(-1, group * pad)
-    column = jnp.pad(column, ((0, 0), (0, LANES - group * pad)), constant_values=-1).reshape(-1, 1)
-    weight = jnp.where(column == 0, 1.0, 2.0).astype(BF16)
-    return jnp.where(jnp.arange(waves)[None, :] == column, weight, jnp.zeros((), BF16))
+    column = jnp.pad(column, ((0, 0), (0, LANES - group * pad)), constant_values=-1)
+    column = column.reshape(-1, 1)
+    return column
 
 
 def body(spectral, legendre, wave_table, courant_lon, courant_lat):
@@ -696,8 +726,7 @@
         pairs = [(i, i ^ step) for i in range(level_count)]
         blocks[step] = lax.ppermute(blocks[step], "lev", pairs)
     blocks[1], winds = lax.optimization_barrier((blocks[1], (courant_lon, courant_lat)))
-    lower, upper = halos(*winds)
-    own_winds = own_courant(*winds)
+    own_winds, upper, lower = own_courant(*winds)
     below = lax.ppermute(upper, "wave", up)
     above = lax.ppermute(lower, "wave", down)
 
@@ -707,20 +736,20 @@
     turned = jnp.swapaxes(legendre, 1, 2)
     given = (turned, own_pairs, wave_count, waves, pad)
     sums = list(legendre_sums(range(level_count - 1), blocks[:-1], *given))
-    order = order_matrix(wave_table, wave_count * level_count, pad)
-    sums, order, own_winds = lax.optimization_barrier((sums, order, own_winds))
+    numbers = arrival(wave_table, wave_count * level_count, pad)
     stacked = legendre_sums([level_count - 1], blocks[-1:], *given, done=tuple(sums))
     arrived = lax.all_to_all(
         stacked.reshape(-1, SUB * SUB, LANES), ("wave", "lev"), 0, 0, tiled=True
     )
 
     fields = [
-        factor_rows(own_winds, received, side, levels)
-        for side, received in ((-1, below), (0, None), (1, above))
+        edge_fields(own_winds, below, 0, levels),
+        inner_fields(own_winds, levels),
+        edge_fields(own_winds, above, 1, levels),
     ]
     twist, table = fourier_tables(nlon, SUB // levels * LANES)
     return advect(
-        arrived, order, jnp.asarray(twist), jnp.asarray(table), fields, courant_lon.shape, pad
+        arrived, numbers, jnp.asarray(twist), jnp.asarray(table), fields, waves, courant_lon.shape, pad
     )
 
 

time: 72.9 us -> 71.2 us (0.977)
  the two profiles are of different devices: /device:TPU:26 before, /device:TPU:0 now
where the time goes in v4:
time: 71.2 us; the launch traced here: 70.6 us
  Pallas kernels  41.2 us (58%)
  starting transfers between devices  14.2 us (20%)
  waiting for transfers between devices  10.5 us (15%)
  local copies, waits for them, and re-layouts  4.32 us (6%)
    pallas_call x1, Pallas kernels, advect(): pl.pallas_call(functools.partial(advect_kernel, pad), out_shape=jax.Shape...  19.3 us
    pallas_call x2, Pallas kernels, edge_fields(): pl.pallas_call(functools.partial(edge_kernel, levels, side), out_shape=pl...  6.67 us
    all_to_all x1, starting transfers between devices, body(): lax.all_to_all(stacked.reshape(-1, SUB * SUB, LANES), ('wave', 'lev'), 0,...  6.1 us
    ppermute x3, waiting for transfers between devices, body(): blocks[step] = lax.ppermute(blocks[step], 'lev', pairs)  5.73 us
    pallas_call x2, Pallas kernels, legendre_sums(): pl.pallas_call(functools.partial(legendre_kernel, steps, bands, waves, pa...  5.56 us
    ppermute x1, waiting for transfers between devices, body(): below = lax.ppermute(upper, 'wave', up)  4.81 us
    unnamed x19, local copies, waits for them, and re-layouts  3.84 us
    pallas_call x1, Pallas kernels, inner_fields(): pl.pallas_call(functools.partial(inner_kernel, levels), out_shape=pltpu.H...  3.79 us
  transfers between devices with their start and end apart: 6, of which 3 were waited for; matrix products, arithmetic and copies ran while one was open for 1% of the time, Pallas kernels for 27%

profile of v4, /device:TPU:0, one launch (start us, length us, event | category | flops | bytes accessed | tf_op | source)
XLA Modules:
  0.0 70.6 jit_solution(3999690440839008535)
XLA Ops:
  0.0 0.0 copy-start.2
  0.0 1.5 %copy-done.2 = bf16[2,4,80,1281]{3,2,1,0:T(8,128)(2,1)S(1)} copy-done((bf16[2,4,80,1281]{3,2,1,0:T(8,128)(2,1)S(1)}, bf16[2,4,80,1281]{3,2,1,0:T(8,128)(2,1)}, u32[]{:S(2)}) %copy-start.2) | copy-done | bytes 1639704
  1.5 0.0 copy-start.3
  1.5 0.0 copy-start.4
  1.5 0.0 copy-start.7
  1.5 1.7 %pack.2 = (bf16[1616,128]{1,0:T(8,128)(2,1)}, bf16[1616,128]{1,0:T(8,128)(2,1)}) custom-call(bf16[8,80,1281]{2,1,0:T(8,128)(2,1)S(1)} %bitcast.12), custom_call_target="tpu_custom_call" | custom-call | tf_op jit(solution)/shard_map/pack/pallas_call | solution.py:80
  3.2 0.9 %pack.3 = (bf16[1616,128]{1,0:T(8,128)(2,1)S(1)}, bf16[1616,128]{1,0:T(8,128)(2,1)S(1)}) custom-call(bf16[8,80,1281]{2,1,0:T(8,128)(2,1)S(1)} %bitcast.13), custom_call_target="tpu_custom_call" | custom-call | tf_op jit(solution)/shard_map/pack/pallas_call | solution.py:80
  4.1 0.5 collective-permute-start.1
  4.6 2.6 %collective-permute-start.2 = (bf16[1616,128]{1,0:T(8,128)(2,1)}, bf16[1616,128]{1,0:T(8,128)(2,1)S(1)}, u32[]{:S(2)}, u32[]{:S(2)}) collective-permute-start(bf16[1616,128]{1,0:T(8,128)(2,1)} %get-tuple-element.28), channel_id=1, source_target_pairs={{0,2},{1,3},{2,0},{3,1},{4,6},{5,7},{6,4},{7,5},{8,10},{9,11},{10,... | collective-permute-start | bytes 1241096 | tf_op jit(solution)/shard_map/ppermute | solution.py:727
  7.1 0.1 collective-permute-start
  7.2 0.0 collective-permute-done.1.refs_1_
  7.2 0.0 copy-done.3
  7.2 0.0 copy-done.4
  7.2 3.3 %own_courant.1 = (f32[2,8,20,8,128]{4,3,2,1,0:T(8,128)}, bf16[14,160,128]{2,1,0:T(8,128)(2,1)}, bf16[15,160,128]{2,1,0:T(8,128)(2,1)S(1)}) custom-call(f32[4,8,5120]{2,1,0:T(8,128)S(1)} %copy-done.3, f32[4,8,5120]{2,1,0:T(8,128)S(1)} %copy-done.4), custom_call_target="tpu_custom_call" | custom-call | tf_op jit(solution)/shard_map/own_courant/pallas_call | solution.py:277
  10.6 3.7 %collective-permute-start.3 = (bf16[14,160,128]{2,1,0:T(8,128)(2,1)}, bf16[14,160,128]{2,1,0:T(8,128)(2,1)S(1)}, u32[]{:S(2)}, u32[]{:S(2)}) collective-permute-start(bf16[14,160,128]{2,1,0:T(8,128)(2,1)} %get-tuple-element.35), channel_id=1, source_target_pairs={{0,4},{4,8},{8,12},{12,16},{16,20},{20,24},{24,28},{1,5},{5,9},{9,... | collective-permute-start | bytes 1720328 | tf_op jit(solution)/shard_map/ppermute | solution.py:730
  14.3 1.3 %collective-permute-start.4 = (bf16[15,160,128]{2,1,0:T(8,128)(2,1)S(1)}, bf16[15,160,128]{2,1,0:T(8,128)(2,1)S(1)}, u32[]{:S(2)}, u32[]{:S(2)}) collective-permute-start(bf16[15,160,128]{2,1,0:T(8,128)(2,1)S(1)} %get-tuple-element.36), channel_id=1, source_target_pairs={{4,0},{8,4},{12,8},{16,12},{20,16},{24,20},{28,24},{5,1},{9,5},{13... | collective-permute-start | bytes 1843208 | tf_op jit(solution)/shard_map/ppermute | solution.py:731
  15.6 0.0 copy-done.7
  15.6 0.1 dynamic_slice.3.pairs_ref
  15.7 2.1 %collective-permute-done.2.refs_2_ = bf16[1616,128]{1,0:T(8,128)(2,1)S(1)} collective-permute-done((bf16[1616,128]{1,0:T(8,128)(2,1)}, bf16[1616,128]{1,0:T(8,128)(2,1)S(1)}, u32[]{:S(2)}, u32[]{:S(2)}) %collective-permute-start.2) | collective-permute-done | bytes 413728 | tf_op jit(solution)/shard_map/ppermute | solution.py:727
  17.8 0.0 copy-start
  17.8 2.0 %copy-done = bf16[20,1281,64]{1,2,0:T(8,128)(2,1)S(1)} copy-done((bf16[20,1281,64]{1,2,0:T(8,128)(2,1)S(1)}, bf16[20,1281,64]{1,2,0:T(8,128)(2,1)}, u32[]{:S(2)}) %copy-start) | copy-done | bytes 3279384
  19.8 0.0 copy-start.1
  19.8 2.7 %legendre.2 = (bf16[8,64,128]{2,1,0:T(8,128)(2,1)S(1)}, bf16[8,64,128]{2,1,0:T(8,128)(2,1)S(1)}, bf16[8,64,128]{2,1,0:T(8,128)(2,1)S(1)}) custom-call(s32[20]{0:T(128)S(1)} %dynamic_slice.3.pairs_ref, bf16[1616,128]{1,0:T(8,128)(2,1)S(1)} %get-tuple-element.25.refs_0_, bf16[1616,128]{1,0:T(8,128)(2,1)S(1)} %collective-permute-done.1.refs_1_, ...), custom_call_target="tpu_custom_call" | custom-call | tf_op jit(solution)/shard_map/legendre/pallas_call | solution.py:175
  22.5 3.6 %collective-permute-done.refs_0_ = bf16[1616,128]{1,0:T(8,128)(2,1)S(1)} collective-permute-done((bf16[1616,128]{1,0:T(8,128)(2,1)}, bf16[1616,128]{1,0:T(8,128)(2,1)S(1)}, u32[]{:S(2)}, u32[]{:S(2)}) %collective-permute-start) | collective-permute-done | bytes 413728 | tf_op jit(solution)/shard_map/ppermute | solution.py:727
  26.1 0.0 copy-done.1
  26.1 2.9 %legendre.3 = bf16[8,4,64,128]{3,2,1,0:T(8,128)(2,1)} custom-call(s32[20]{0:T(128)S(1)} %dynamic_slice.3.pairs_ref, bf16[1616,128]{1,0:T(8,128)(2,1)S(1)} %collective-permute-done.refs_0_, bf16[20,64,1281]{2,1,0:T(8,128)(2,1)S(1)} %bitcast.11, bf16[8,64,128]{2,1,0:T(8,128)(2,1)S(1)} %get-tuple-element.29.refs_2_, ...), custom_call_target="tpu_custom_call" | custom-call | tf_op jit(solution)/shard_map/legendre/pallas_call | solution.py:175
  29.0 6.1 %all-to-all-start = ((bf16[32,64,128]{2,1,0:T(8,128)(2,1)}), bf16[32,64,128]{2,1,0:T(8,128)(2,1)S(1)}, u32[]{:S(2)}, u32[]{:S(2)}) async-start(bf16[32,64,128]{2,1,0:T(8,128)(2,1)} %bitcast.2), calls=%async_computation | async-start | bytes 1048576 | tf_op jit(solution)/shard_map/all_to_all | solution.py:741
  35.2 0.2 copy.8
  35.3 0.1 reshape.17
  35.5 0.1 reshape.18
  35.6 0.3 copy.11
  35.9 3.8 %inner.1.refs_1_ = f32[6,6,20,8,128]{4,3,2,1,0:T(8,128)} custom-call(f32[2,8,20,8,128]{4,3,2,1,0:T(8,128)} %get-tuple-element.34.own), custom_call_target="tpu_custom_call" | custom-call | tf_op jit(solution)/shard_map/inner/pallas_call | solution.py:309
  39.7 4.8 %collective-permute-done.3.received = bf16[14,160,128]{2,1,0:T(8,128)(2,1)S(1)} collective-permute-done((bf16[14,160,128]{2,1,0:T(8,128)(2,1)}, bf16[14,160,128]{2,1,0:T(8,128)(2,1)S(1)}, u32[]{:S(2)}, u32[]{:S(2)}) %collective-permute-start.3) | collective-permute-done | bytes 573472 | tf_op jit(solution)/shard_map/ppermute | solution.py:730
  44.5 3.3 %edge.2.refs_0_ = f32[6,9,20,8,128]{4,3,2,1,0:T(8,128)} custom-call(f32[2,8,20,8,128]{4,3,2,1,0:T(8,128)} %get-tuple-element.34.own, bf16[14,160,128]{2,1,0:T(8,128)(2,1)S(1)} %collective-permute-done.3.received), custom_call_target="tpu_custom_call" | custom-call | flops 1000000000 | bytes 8000000 | tf_op jit(solution)/shard_map/edge/pallas_call | solution.py:369
  47.7 0.0 copy-start.5
  47.8 0.0 copy-start.6
  47.8 0.0 collective-permute-done.4.received
  47.8 3.4 %edge.3.refs_2_ = f32[6,9,20,8,128]{4,3,2,1,0:T(8,128)} custom-call(f32[2,8,20,8,128]{4,3,2,1,0:T(8,128)} %get-tuple-element.34.own, bf16[15,160,128]{2,1,0:T(8,128)(2,1)S(1)} %collective-permute-done.4.received), custom_call_target="tpu_custom_call" | custom-call | flops 6000000000 | bytes 8000000 | tf_op jit(solution)/shard_map/edge/pallas_call | solution.py:369
  51.2 0.0 all-to-all-done.arrived
  51.2 0.0 copy-done.5
  51.2 0.0 copy-done.6
  51.2 19.3 %advect.1 = f32[4,8,5120]{2,1,0:T(8,128)} custom-call(bf16[32,64,128]{2,1,0:T(8,128)(2,1)S(1)} %all-to-all-done.arrived, s32[1408,1]{1,0:T(8,128)S(1)} %bitcast.14, f32[40,256]{1,0:T(8,128)S(1)} %copy-done.6, bf16[1024,256]{1,0:T(8,128)(2,1)S(1)} %copy-done.5, f32[6,9,20,8,128]{4,3,2,1,0:T(8,128)} %edge.2.refs_0_, f32[6,6,20,8,128]{4,3,2,1,0:T(8,128)} %inner.1.refs_1_, ...), custom_call_target="tpu_custom_call" | custom-call | tf_op jit(solution)/shard_map/advect/pallas_call | solution.py:666
  (7 shorter events, 0.0 us)
Async XLA Ops:
  0.0 1.5 %copy-start.2 = (bf16[2,4,80,1281]{3,2,1,0:T(8,128)(2,1)S(1)}, bf16[2,4,80,1281]{3,2,1,0:T(8,128)(2,1)}, u32[]{:S(2)}) copy-start(bf16[2,4,80,1281]{3,2,1,0:T(8,128)(2,1)} %param.7) | copy-start | bytes 4919044
  1.5 5.7 %copy-start.3 = (f32[4,8,5120]{2,1,0:T(8,128)S(1)}, f32[4,8,5120]{2,1,0:T(8,128)}, u32[]{:S(2)}) copy-start(f32[4,8,5120]{2,1,0:T(8,128)} %lon) | copy-start | bytes 1966084
  1.5 5.7 %copy-start.4 = (f32[4,8,5120]{2,1,0:T(8,128)S(1)}, f32[4,8,5120]{2,1,0:T(8,128)}, u32[]{:S(2)}) copy-start(f32[4,8,5120]{2,1,0:T(8,128)} %lat) | copy-start | bytes 1966084
  1.5 14.1 %copy-start.7 = (s32[640]{0:T(1024)S(1)}, s32[640]{0:T(1024)}, u32[]{:S(2)}) copy-start(s32[640]{0:T(1024)} %param.9) | copy-start | bytes 7684
  4.1 3.2 %collective-permute-start.1 = (bf16[1616,128]{1,0:T(8,128)(2,1)S(1)}, bf16[1616,128]{1,0:T(8,128)(2,1)S(1)}, u32[]{:S(2)}, u32[]{:S(2)}) collective-permute-start(bf16[1616,128]{1,0:T(8,128)(2,1)S(1)} %get-tuple-element.26), channel_id=1, source_target_pairs={{0,1},{1,0},{2,3},{3,2},{4,5},{5,4},{6,7},{7,6},{8,9},{9,8},{10,11... | collective-permute-start | bytes 1241096 | tf_op jit(solution)/shard_map/ppermute | solution.py:727
  4.6 13.2 %collective-permute-start.2 = (bf16[1616,128]{1,0:T(8,128)(2,1)}, bf16[1616,128]{1,0:T(8,128)(2,1)S(1)}, u32[]{:S(2)}, u32[]{:S(2)}) collective-permute-start(bf16[1616,128]{1,0:T(8,128)(2,1)} %get-tuple-element.28), channel_id=1, source_target_pairs={{0,2},{1,3},{2,0},{3,1},{4,6},{5,7},{6,4},{7,5},{8,10},{9,11},{10,... | collective-permute-start | bytes 1241096 | tf_op jit(solution)/shard_map/ppermute | solution.py:727
  7.1 19.0 %collective-permute-start = (bf16[1616,128]{1,0:T(8,128)(2,1)}, bf16[1616,128]{1,0:T(8,128)(2,1)S(1)}, u32[]{:S(2)}, u32[]{:S(2)}) collective-permute-start(bf16[1616,128]{1,0:T(8,128)(2,1)} %get-tuple-element.23), channel_id=1, source_target_pairs={{0,3},{1,2},{2,1},{3,0},{4,7},{5,6},{6,5},{7,4},{8,11},{9,10},{10,... | collective-permute-start | bytes 1241096 | tf_op jit(solution)/shard_map/ppermute | solution.py:727
  10.6 33.9 %collective-permute-start.3 = (bf16[14,160,128]{2,1,0:T(8,128)(2,1)}, bf16[14,160,128]{2,1,0:T(8,128)(2,1)S(1)}, u32[]{:S(2)}, u32[]{:S(2)}) collective-permute-start(bf16[14,160,128]{2,1,0:T(8,128)(2,1)} %get-tuple-element.35), channel_id=1, source_target_pairs={{0,4},{4,8},{8,12},{12,16},{16,20},{20,24},{24,28},{1,5},{5,9},{9,... | collective-permute-start | bytes 1720328 | tf_op jit(solution)/shard_map/ppermute | solution.py:730
  14.3 33.5 %collective-permute-start.4 = (bf16[15,160,128]{2,1,0:T(8,128)(2,1)S(1)}, bf16[15,160,128]{2,1,0:T(8,128)(2,1)S(1)}, u32[]{:S(2)}, u32[]{:S(2)}) collective-permute-start(bf16[15,160,128]{2,1,0:T(8,128)(2,1)S(1)} %get-tuple-element.36), channel_id=1, source_target_pairs={{4,0},{8,4},{12,8},{16,12},{20,16},{24,20},{28,24},{5,1},{9,5},{13... | collective-permute-start | bytes 1843208 | tf_op jit(solution)/shard_map/ppermute | solution.py:731
  17.8 2.0 %copy-start = (bf16[20,1281,64]{1,2,0:T(8,128)(2,1)S(1)}, bf16[20,1281,64]{1,2,0:T(8,128)(2,1)}, u32[]{:S(2)}) copy-start(bf16[20,1281,64]{1,2,0:T(8,128)(2,1)} %param.8) | copy-start | bytes 9838084
  19.8 6.3 %copy-start.1 = (bf16[20,1281,64]{1,2,0:T(8,128)(2,1)S(1)}, bf16[20,1281,64]{1,2,0:T(8,128)(2,1)}, u32[]{:S(2)}) copy-start(bf16[20,1281,64]{1,2,0:T(8,128)(2,1)} %param.8) | copy-start | bytes 9838084
  29.0 22.2 %all-to-all-start = ((bf16[32,64,128]{2,1,0:T(8,128)(2,1)}), bf16[32,64,128]{2,1,0:T(8,128)(2,1)S(1)}, u32[]{:S(2)}, u32[]{:S(2)}) async-start(bf16[32,64,128]{2,1,0:T(8,128)(2,1)} %bitcast.2), calls=%async_computation | async-start | bytes 1048576 | tf_op jit(solution)/shard_map/all_to_all | solution.py:741
  47.7 3.5 %copy-start.5 = (bf16[1024,256]{1,0:T(8,128)(2,1)S(1)}, bf16[1024,256]{1,0:T(8,128)(2,1)}, u32[]{:S(2)}) copy-start(bf16[1024,256]{1,0:T(8,128)(2,1)} %constant.26.clone.table) | copy-start | bytes 1572868
  47.8 3.5 %copy-start.6 = (f32[40,256]{1,0:T(8,128)S(1)}, f32[40,256]{1,0:T(8,128)}, u32[]{:S(2)}) copy-start(f32[40,256]{1,0:T(8,128)} %constant.25.clone.twist) | copy-start | bytes 122884

commit v5 on v4

--- a/solution.py
+++ b/solution.py
@@ -136,7 +136,7 @@
                     sums[d, 4 * i + 2 * j + half, :, :lats] = got[first : first + SUB]
         return carry
 
-    lax.fori_loop(0, -(-own // 2), pair, 0, unroll=5)
+    lax.fori_loop(0, -(-own // 2), pair, 0, unroll=10)
     lane = lane_index()
     nothing = jnp.zeros((SUB, LANES), F32)
     for d in range(count):
@@ -236,7 +236,7 @@
             by[t, v] = 0.125 * w[v] * (near[v] + east[v])
         return carry
 
-    lax.fori_loop(start, stop, factors, 0)
+    lax.fori_loop(start, stop, factors, 0, unroll=4)
 
 
 def own_courant_kernel(lon, lat, own, upper, lower, rows, turned, sem):
@@ -462,7 +462,7 @@
             order[span, lo : lo + LANES] = jnp.where(column + lo == number, weight, 0.0).astype(BF16)
         return carry
 
-    lax.fori_loop(0, order.shape[0] // (2 * SUB), one_hot, 0, unroll=4)
+    lax.fori_loop(0, order.shape[0] // (2 * SUB), one_hot, 0, unroll=44)
     for m in range(depth):
         mixed[m] = jnp.dot(
             lhs[...], order[:, m * near : (m + 1) * near], preferred_element_type=F32
@@ -480,10 +480,7 @@
                     cos, sin = twist[2 * v : 2 * v + 1, lanes], twist[2 * v + 1 : 2 * v + 2, lanes]
                     x, y = x * cos - y * sin, x * sin + y * cos
                 for c, value in enumerate((x, y)):
-                    high = value.astype(BF16)
-                    low = (value - high.astype(F32)).astype(BF16)
-                    terms[v, span, c * near + lo : c * near + lo + LANES] = high
-                    terms[v, span, (2 + c) * near + lo : (2 + c) * near + lo + LANES] = low
+                    terms[v, span, c * near + lo : c * near + lo + LANES] = value.astype(BF16)
         return carry
 
     lax.fori_loop(0, half // (2 * SUB), vary, 0)
@@ -492,11 +489,9 @@
     group = chunks // 2
 
     def finish(i, carry):
-        both = terms[pl.ds(i * group, group)].reshape(group * half, 4 * near)
-        high, low = both[:, : 2 * near], both[:, 2 * near :]
-        value = jnp.dot(high, table[: 2 * near], preferred_element_type=F32)
-        value += jnp.dot(low, table[: 2 * near], preferred_element_type=F32)
-        value += jnp.dot(high, table[2 * near :], preferred_element_type=F32)
+        both = terms[pl.ds(i * group, group)].reshape(group * half, 2 * near)
+        value = jnp.dot(both, table[: 2 * near], preferred_element_type=F32)
+        value += jnp.dot(both, table[2 * near :], preferred_element_type=F32)
         for v in range(group):
             for piece in range(pieces):
                 tiles = []
@@ -645,7 +640,7 @@
             turned[pl.ds(v, LANES, stride=chunks), :] = value
             return carry
 
-        lax.fori_loop(0, chunks, stand, 0, unroll=2)
+        lax.fori_loop(0, chunks, stand, 0, unroll=20)
         for n in range(span // LANES):
             value = jnp.transpose(turned[n * LANES : (n + 1) * LANES, :])
             for i in range(SUB):
@@ -672,7 +667,7 @@
             pltpu.VMEM(order, BF16),
             pltpu.VMEM((2 * half, order[0]), BF16),
             pltpu.VMEM((waves // near, 2 * half, near), F32),
-            pltpu.VMEM((chunks, half, 4 * near), BF16),
+            pltpu.VMEM((chunks, half, 2 * near), BF16),
             pltpu.VMEM((rows, chunks, SUB, LANES), F32),
             pltpu.VMEM((rows, chunks, SUB, LANES), F32),
             pltpu.VMEM((nlon * levels // SUB, LANES), F32),

time: 71.2 us -> 68.1 us (0.956)
  Pallas kernels: 41.2 us -> 37 us
  waiting for transfers between devices: 10.5 us -> 11.5 us
    pallas_call x1, Pallas kernels: 19.3 us -> 16.4 us  [advect(): pl.pallas_call(functools.partial(advect_kernel, pad), out_shape=jax.Shape...]
    ppermute x1, waiting for transfers between devices: 4.81 us -> 5.59 us  [body(): below = lax.ppermute(upper, 'wave', up)]
where the time goes in v5:
time: 68.1 us; the launch traced here: 67.4 us
  Pallas kernels  37 us (54%)
  starting transfers between devices  14.2 us (21%)
  waiting for transfers between devices  11.5 us (17%)
  local copies, waits for them, and re-layouts  4.32 us (6%)
    pallas_call x1, Pallas kernels, advect(): pl.pallas_call(functools.partial(advect_kernel, pad), out_shape=jax.Shape...  16.4 us
    pallas_call x2, Pallas kernels, edge_fields(): pl.pallas_call(functools.partial(edge_kernel, levels, side), out_shape=pl...  6.19 us
    all_to_all x1, starting transfers between devices, body(): lax.all_to_all(stacked.reshape(-1, SUB * SUB, LANES), ('wave', 'lev'), 0,...  6.1 us
    ppermute x3, waiting for transfers between devices, body(): blocks[step] = lax.ppermute(blocks[step], 'lev', pairs)  5.96 us
    ppermute x1, waiting for transfers between devices, body(): below = lax.ppermute(upper, 'wave', up)  5.59 us
    pallas_call x2, Pallas kernels, legendre_sums(): pl.pallas_call(functools.partial(legendre_kernel, steps, bands, waves, pa...  5.07 us
    unnamed x19, local copies, waits for them, and re-layouts  3.84 us
    ppermute x1, starting transfers between devices, body(): below = lax.ppermute(upper, 'wave', up)  3.69 us
  transfers between devices with their start and end apart: 6, of which 3 were waited for; matrix products, arithmetic and copies ran while one was open for 1% of the time, Pallas kernels for 27%

profile of v5, /device:TPU:0, one launch (start us, length us, event | category | flops | bytes accessed | tf_op | source)
XLA Modules:
  0.0 67.4 jit_solution(10849678652852493678)
XLA Ops:
  0.0 0.0 copy-start.2
  0.0 1.5 %copy-done.2 = bf16[2,4,80,1281]{3,2,1,0:T(8,128)(2,1)S(1)} copy-done((bf16[2,4,80,1281]{3,2,1,0:T(8,128)(2,1)S(1)}, bf16[2,4,80,1281]{3,2,1,0:T(8,128)(2,1)}, u32[]{:S(2)}) %copy-start.2) | copy-done | bytes 1639704
  1.5 0.0 copy-start.3
  1.5 0.0 copy-start.4
  1.5 0.0 copy-start.7
  1.5 1.7 %pack.2 = (bf16[1616,128]{1,0:T(8,128)(2,1)}, bf16[1616,128]{1,0:T(8,128)(2,1)}) custom-call(bf16[8,80,1281]{2,1,0:T(8,128)(2,1)S(1)} %bitcast.12), custom_call_target="tpu_custom_call" | custom-call | tf_op jit(solution)/shard_map/pack/pallas_call | solution.py:80
  3.2 0.9 %pack.3 = (bf16[1616,128]{1,0:T(8,128)(2,1)S(1)}, bf16[1616,128]{1,0:T(8,128)(2,1)S(1)}) custom-call(bf16[8,80,1281]{2,1,0:T(8,128)(2,1)S(1)} %bitcast.13), custom_call_target="tpu_custom_call" | custom-call | tf_op jit(solution)/shard_map/pack/pallas_call | solution.py:80
  4.1 0.5 collective-permute-start.1
  4.6 2.6 %collective-permute-start.2 = (bf16[1616,128]{1,0:T(8,128)(2,1)}, bf16[1616,128]{1,0:T(8,128)(2,1)S(1)}, u32[]{:S(2)}, u32[]{:S(2)}) collective-permute-start(bf16[1616,128]{1,0:T(8,128)(2,1)} %get-tuple-element.28), channel_id=1, source_target_pairs={{0,2},{1,3},{2,0},{3,1},{4,6},{5,7},{6,4},{7,5},{8,10},{9,11},{10,... | collective-permute-start | bytes 1241096 | tf_op jit(solution)/shard_map/ppermute | solution.py:722
  7.1 0.1 collective-permute-start
  7.2 0.0 collective-permute-done.1.refs_1_
  7.2 0.0 copy-done.3
  7.2 0.0 copy-done.4
  7.2 3.3 %own_courant.1 = (f32[2,8,20,8,128]{4,3,2,1,0:T(8,128)}, bf16[14,160,128]{2,1,0:T(8,128)(2,1)}, bf16[15,160,128]{2,1,0:T(8,128)(2,1)S(1)}) custom-call(f32[4,8,5120]{2,1,0:T(8,128)S(1)} %copy-done.3, f32[4,8,5120]{2,1,0:T(8,128)S(1)} %copy-done.4), custom_call_target="tpu_custom_call" | custom-call | tf_op jit(solution)/shard_map/own_courant/pallas_call | solution.py:277
  10.6 3.7 %collective-permute-start.3 = (bf16[14,160,128]{2,1,0:T(8,128)(2,1)}, bf16[14,160,128]{2,1,0:T(8,128)(2,1)S(1)}, u32[]{:S(2)}, u32[]{:S(2)}) collective-permute-start(bf16[14,160,128]{2,1,0:T(8,128)(2,1)} %get-tuple-element.35), channel_id=1, source_target_pairs={{0,4},{4,8},{8,12},{12,16},{16,20},{20,24},{24,28},{1,5},{5,9},{9,... | collective-permute-start | bytes 1720328 | tf_op jit(solution)/shard_map/ppermute | solution.py:725
  14.3 1.3 %collective-permute-start.4 = (bf16[15,160,128]{2,1,0:T(8,128)(2,1)S(1)}, bf16[15,160,128]{2,1,0:T(8,128)(2,1)S(1)}, u32[]{:S(2)}, u32[]{:S(2)}) collective-permute-start(bf16[15,160,128]{2,1,0:T(8,128)(2,1)S(1)} %get-tuple-element.36), channel_id=1, source_target_pairs={{4,0},{8,4},{12,8},{16,12},{20,16},{24,20},{28,24},{5,1},{9,5},{13... | collective-permute-start | bytes 1843208 | tf_op jit(solution)/shard_map/ppermute | solution.py:726
  15.6 0.0 copy-done.7
  15.6 0.1 dynamic_slice.3.pairs_ref
  15.7 2.1 %collective-permute-done.2.refs_2_ = bf16[1616,128]{1,0:T(8,128)(2,1)S(1)} collective-permute-done((bf16[1616,128]{1,0:T(8,128)(2,1)}, bf16[1616,128]{1,0:T(8,128)(2,1)S(1)}, u32[]{:S(2)}, u32[]{:S(2)}) %collective-permute-start.2) | collective-permute-done | bytes 413728 | tf_op jit(solution)/shard_map/ppermute | solution.py:722
  17.8 0.0 copy-start
  17.8 2.0 %copy-done = bf16[20,1281,64]{1,2,0:T(8,128)(2,1)S(1)} copy-done((bf16[20,1281,64]{1,2,0:T(8,128)(2,1)S(1)}, bf16[20,1281,64]{1,2,0:T(8,128)(2,1)}, u32[]{:S(2)}) %copy-start) | copy-done | bytes 3279384
  19.8 0.0 copy-start.1
  19.8 2.4 %legendre.2 = (bf16[8,64,128]{2,1,0:T(8,128)(2,1)S(1)}, bf16[8,64,128]{2,1,0:T(8,128)(2,1)S(1)}, bf16[8,64,128]{2,1,0:T(8,128)(2,1)S(1)}) custom-call(s32[20]{0:T(128)S(1)} %dynamic_slice.3.pairs_ref, bf16[1616,128]{1,0:T(8,128)(2,1)S(1)} %get-tuple-element.25.refs_0_, bf16[1616,128]{1,0:T(8,128)(2,1)S(1)} %collective-permute-done.1.refs_1_, ...), custom_call_target="tpu_custom_call" | custom-call | tf_op jit(solution)/shard_map/legendre/pallas_call | solution.py:175
  22.2 3.9 %collective-permute-done.refs_0_ = bf16[1616,128]{1,0:T(8,128)(2,1)S(1)} collective-permute-done((bf16[1616,128]{1,0:T(8,128)(2,1)}, bf16[1616,128]{1,0:T(8,128)(2,1)S(1)}, u32[]{:S(2)}, u32[]{:S(2)}) %collective-permute-start) | collective-permute-done | bytes 413728 | tf_op jit(solution)/shard_map/ppermute | solution.py:722
  26.1 0.0 copy-done.1
  26.1 2.6 %legendre.3 = bf16[8,4,64,128]{3,2,1,0:T(8,128)(2,1)} custom-call(s32[20]{0:T(128)S(1)} %dynamic_slice.3.pairs_ref, bf16[1616,128]{1,0:T(8,128)(2,1)S(1)} %collective-permute-done.refs_0_, bf16[20,64,1281]{2,1,0:T(8,128)(2,1)S(1)} %bitcast.11, bf16[8,64,128]{2,1,0:T(8,128)(2,1)S(1)} %get-tuple-element.29.refs_2_, ...), custom_call_target="tpu_custom_call" | custom-call | tf_op jit(solution)/shard_map/legendre/pallas_call | solution.py:175
  28.7 6.1 %all-to-all-start = ((bf16[32,64,128]{2,1,0:T(8,128)(2,1)}), bf16[32,64,128]{2,1,0:T(8,128)(2,1)S(1)}, u32[]{:S(2)}, u32[]{:S(2)}) async-start(bf16[32,64,128]{2,1,0:T(8,128)(2,1)} %bitcast.2), calls=%async_computation | async-start | bytes 1048576 | tf_op jit(solution)/shard_map/all_to_all | solution.py:736
  34.9 0.2 copy.8
  35.1 0.1 reshape.17
  35.2 0.1 reshape.18
  35.3 0.3 copy.11
  35.6 3.4 %inner.1.refs_1_ = f32[6,6,20,8,128]{4,3,2,1,0:T(8,128)} custom-call(f32[2,8,20,8,128]{4,3,2,1,0:T(8,128)} %get-tuple-element.34.own), custom_call_target="tpu_custom_call" | custom-call | tf_op jit(solution)/shard_map/inner/pallas_call | solution.py:309
  39.0 5.6 %collective-permute-done.3.received = bf16[14,160,128]{2,1,0:T(8,128)(2,1)S(1)} collective-permute-done((bf16[14,160,128]{2,1,0:T(8,128)(2,1)}, bf16[14,160,128]{2,1,0:T(8,128)(2,1)S(1)}, u32[]{:S(2)}, u32[]{:S(2)}) %collective-permute-start.3) | collective-permute-done | bytes 573472 | tf_op jit(solution)/shard_map/ppermute | solution.py:725
  44.6 3.0 %edge.2.refs_0_ = f32[6,9,20,8,128]{4,3,2,1,0:T(8,128)} custom-call(f32[2,8,20,8,128]{4,3,2,1,0:T(8,128)} %get-tuple-element.34.own, bf16[14,160,128]{2,1,0:T(8,128)(2,1)S(1)} %collective-permute-done.3.received), custom_call_target="tpu_custom_call" | custom-call | flops 1000000000 | bytes 8000000 | tf_op jit(solution)/shard_map/edge/pallas_call | solution.py:369
  47.6 0.0 copy-start.5
  47.6 0.0 copy-start.6
  47.6 0.0 collective-permute-done.4.received
  47.7 3.1 %edge.3.refs_2_ = f32[6,9,20,8,128]{4,3,2,1,0:T(8,128)} custom-call(f32[2,8,20,8,128]{4,3,2,1,0:T(8,128)} %get-tuple-element.34.own, bf16[15,160,128]{2,1,0:T(8,128)(2,1)S(1)} %collective-permute-done.4.received), custom_call_target="tpu_custom_call" | custom-call | flops 6000000000 | bytes 8000000 | tf_op jit(solution)/shard_map/edge/pallas_call | solution.py:369
  50.8 0.0 all-to-all-done.arrived
  50.8 0.0 copy-done.5
  50.8 0.0 copy-done.6
  50.8 16.4 %advect.1 = f32[4,8,5120]{2,1,0:T(8,128)} custom-call(bf16[32,64,128]{2,1,0:T(8,128)(2,1)S(1)} %all-to-all-done.arrived, s32[1408,1]{1,0:T(8,128)S(1)} %bitcast.14, f32[40,256]{1,0:T(8,128)S(1)} %copy-done.6, bf16[1024,256]{1,0:T(8,128)(2,1)S(1)} %copy-done.5, f32[6,9,20,8,128]{4,3,2,1,0:T(8,128)} %edge.2.refs_0_, f32[6,6,20,8,128]{4,3,2,1,0:T(8,128)} %inner.1.refs_1_, ...), custom_call_target="tpu_custom_call" | custom-call | tf_op jit(solution)/shard_map/advect/pallas_call | solution.py:661
  (7 shorter events, 0.0 us)
Async XLA Ops:
  0.0 1.5 %copy-start.2 = (bf16[2,4,80,1281]{3,2,1,0:T(8,128)(2,1)S(1)}, bf16[2,4,80,1281]{3,2,1,0:T(8,128)(2,1)}, u32[]{:S(2)}) copy-start(bf16[2,4,80,1281]{3,2,1,0:T(8,128)(2,1)} %param.7) | copy-start | bytes 4919044
  1.5 5.7 %copy-start.3 = (f32[4,8,5120]{2,1,0:T(8,128)S(1)}, f32[4,8,5120]{2,1,0:T(8,128)}, u32[]{:S(2)}) copy-start(f32[4,8,5120]{2,1,0:T(8,128)} %lon) | copy-start | bytes 1966084
  1.5 5.7 %copy-start.4 = (f32[4,8,5120]{2,1,0:T(8,128)S(1)}, f32[4,8,5120]{2,1,0:T(8,128)}, u32[]{:S(2)}) copy-start(f32[4,8,5120]{2,1,0:T(8,128)} %lat) | copy-start | bytes 1966084
  1.5 14.1 %copy-start.7 = (s32[640]{0:T(1024)S(1)}, s32[640]{0:T(1024)}, u32[]{:S(2)}) copy-start(s32[640]{0:T(1024)} %param.9) | copy-start | bytes 7684
  4.1 3.2 %collective-permute-start.1 = (bf16[1616,128]{1,0:T(8,128)(2,1)S(1)}, bf16[1616,128]{1,0:T(8,128)(2,1)S(1)}, u32[]{:S(2)}, u32[]{:S(2)}) collective-permute-start(bf16[1616,128]{1,0:T(8,128)(2,1)S(1)} %get-tuple-element.26), channel_id=1, source_target_pairs={{0,1},{1,0},{2,3},{3,2},{4,5},{5,4},{6,7},{7,6},{8,9},{9,8},{10,11... | collective-permute-start | bytes 1241096 | tf_op jit(solution)/shard_map/ppermute | solution.py:722
  4.6 13.2 %collective-permute-start.2 = (bf16[1616,128]{1,0:T(8,128)(2,1)}, bf16[1616,128]{1,0:T(8,128)(2,1)S(1)}, u32[]{:S(2)}, u32[]{:S(2)}) collective-permute-start(bf16[1616,128]{1,0:T(8,128)(2,1)} %get-tuple-element.28), channel_id=1, source_target_pairs={{0,2},{1,3},{2,0},{3,1},{4,6},{5,7},{6,4},{7,5},{8,10},{9,11},{10,... | collective-permute-start | bytes 1241096 | tf_op jit(solution)/shard_map/ppermute | solution.py:722
  7.1 19.0 %collective-permute-start = (bf16[1616,128]{1,0:T(8,128)(2,1)}, bf16[1616,128]{1,0:T(8,128)(2,1)S(1)}, u32[]{:S(2)}, u32[]{:S(2)}) collective-permute-start(bf16[1616,128]{1,0:T(8,128)(2,1)} %get-tuple-element.23), channel_id=1, source_target_pairs={{0,3},{1,2},{2,1},{3,0},{4,7},{5,6},{6,5},{7,4},{8,11},{9,10},{10,... | collective-permute-start | bytes 1241096 | tf_op jit(solution)/shard_map/ppermute | solution.py:722
  10.6 34.0 %collective-permute-start.3 = (bf16[14,160,128]{2,1,0:T(8,128)(2,1)}, bf16[14,160,128]{2,1,0:T(8,128)(2,1)S(1)}, u32[]{:S(2)}, u32[]{:S(2)}) collective-permute-start(bf16[14,160,128]{2,1,0:T(8,128)(2,1)} %get-tuple-element.35), channel_id=1, source_target_pairs={{0,4},{4,8},{8,12},{12,16},{16,20},{20,24},{24,28},{1,5},{5,9},{9,... | collective-permute-start | bytes 1720328 | tf_op jit(solution)/shard_map/ppermute | solution.py:725
  14.3 33.4 %collective-permute-start.4 = (bf16[15,160,128]{2,1,0:T(8,128)(2,1)S(1)}, bf16[15,160,128]{2,1,0:T(8,128)(2,1)S(1)}, u32[]{:S(2)}, u32[]{:S(2)}) collective-permute-start(bf16[15,160,128]{2,1,0:T(8,128)(2,1)S(1)} %get-tuple-element.36), channel_id=1, source_target_pairs={{4,0},{8,4},{12,8},{16,12},{20,16},{24,20},{28,24},{5,1},{9,5},{13... | collective-permute-start | bytes 1843208 | tf_op jit(solution)/shard_map/ppermute | solution.py:726
  17.8 2.0 %copy-start = (bf16[20,1281,64]{1,2,0:T(8,128)(2,1)S(1)}, bf16[20,1281,64]{1,2,0:T(8,128)(2,1)}, u32[]{:S(2)}) copy-start(bf16[20,1281,64]{1,2,0:T(8,128)(2,1)} %param.8) | copy-start | bytes 9838084
  19.8 6.3 %copy-start.1 = (bf16[20,1281,64]{1,2,0:T(8,128)(2,1)S(1)}, bf16[20,1281,64]{1,2,0:T(8,128)(2,1)}, u32[]{:S(2)}) copy-start(bf16[20,1281,64]{1,2,0:T(8,128)(2,1)} %param.8) | copy-start | bytes 9838084
  28.7 22.1 %all-to-all-start = ((bf16[32,64,128]{2,1,0:T(8,128)(2,1)}), bf16[32,64,128]{2,1,0:T(8,128)(2,1)S(1)}, u32[]{:S(2)}, u32[]{:S(2)}) async-start(bf16[32,64,128]{2,1,0:T(8,128)(2,1)} %bitcast.2), calls=%async_computation | async-start | bytes 1048576 | tf_op jit(solution)/shard_map/all_to_all | solution.py:736
  47.6 3.2 %copy-start.5 = (bf16[1024,256]{1,0:T(8,128)(2,1)S(1)}, bf16[1024,256]{1,0:T(8,128)(2,1)}, u32[]{:S(2)}) copy-start(bf16[1024,256]{1,0:T(8,128)(2,1)} %constant.26.clone.table) | copy-start | bytes 1572868
  47.6 3.2 %copy-start.6 = (f32[40,256]{1,0:T(8,128)S(1)}, f32[40,256]{1,0:T(8,128)}, u32[]{:S(2)}) copy-start(f32[40,256]{1,0:T(8,128)} %constant.25.clone.twist) | copy-start | bytes 122884
